TPU v7x, 32 devices: a whole 2x2x4 slice. The times are simulated.
32 devices in a mesh: slab: 8 (over z, core), brick: 4 (over y, x).
Axes of the slice: x: 2, y: 2, z: 4, core: 2. Of those that a mesh axis runs over, the one named last changes fastest.
Arguments:
- features: bfloat16 [64, 65536], P(None, ('slab', 'brick')), may hold values from -6 to 6
- tangents: bfloat16 [4, 64, 65536], P(None, None, ('slab', 'brick')), may hold values from -6 to 6
- route: int32 [65536, 1], P(('slab', 'brick')), may hold values from 0 to 3; in each aligned block of 2048 rows (0 to 2047, 2048 to 4095, ...) at most 1024 rows name the same one
- cell_local: int32 [65536], P(('slab', 'brick')), may hold values from 0 to 8191
- stencil: int32 [65536], P(('slab', 'brick')), may hold values from 0 to 7
- stencil_table: float32 [8, 64], replicated, may hold values from -6 to 6
- taps1: float32 [3, 3, 64], replicated, may hold values from -3.5 to 3.5
- taps2: float32 [3, 3, 64], replicated, may hold values from -3.5 to 3.5
- point1: bfloat16 [64, 64], replicated, may hold values from -0.75 to 0.75
- point2: bfloat16 [64, 64], replicated, may hold values from -0.75 to 0.75
- bias1: float32 [64], replicated, may hold values from -3 to 3
- bias2: float32 [64], replicated, may hold values from -3 to 3
- readout: float32 [64], replicated, may hold values from -12 to 12
Outputs:
- hvp: float32 [4, 64, 65536], P(None, None, ('slab', 'brick'))
Inputs may be any that keep to these rules, and one draw needn't show every extreme that they name: `route`: at most 1024 of the atoms of one device name one brick, and some device names some brick exactly 1024 times.
All inputs are finite; a program needn't handle non-finite values.
Results may differ from a plain program's by a relative error of at most 0.008.
The roundings to bfloat16 on the way count: a program that leaves them out, or rounds other values in their place, can miss the bound.
Values may be sent and summed in bfloat16 or wider, within the bound.
No kernel may reach another device: no remote copies, remote signals or barrier semaphores. Data moves between devices by JAX's collectives and lax.ppermute only.
A program may use at most 192 MiB of HBM per device.

v0:
```python
import jax
import jax.numpy as jnp
from jax import lax
from jax.sharding import PartitionSpec as P

NG = 64
CH = 64
NT = 4
KSETS = 8


def extended(shard, sides, width):
    for axis, dim in sides:
        peers, length = (lax.axis_size(axis), shard.shape[dim])
        up = [(i, (i + 1) % peers) for i in range(peers)]
        down = [(j, i) for i, j in up]
        last = lax.slice_in_dim(shard, length - width, length, axis=dim)
        leading = lax.slice_in_dim(shard, 0, width, axis=dim)
        before = lax.ppermute(last, axis, up)
        after = lax.ppermute(leading, axis, down)
        shard = jnp.concatenate([before, shard, after], axis=dim)
    return shard


def dsilu(v):
    sg = jax.nn.sigmoid(v)
    return sg * (1.0 + v * (1.0 - sg))


def ddsilu(v):
    sg = jax.nn.sigmoid(v)
    return sg * (1.0 - sg) * (2.0 + v * (1.0 - 2.0 * sg))


def sweep(padded, taps, flip):
    kernel = taps[:, ::-1, :] if flip else taps

    def weight(axis, tap):
        return kernel[axis, tap][:, None, None, None]

    along_z = (
        weight(0, 0) * padded[:, :, :-2]
        + weight(0, 1) * padded[:, :, 1:-1]
        + weight(0, 2) * padded[:, :, 2:]
    )
    across = (
        weight(1, 0) * along_z[:, :, :, :-2]
        + weight(1, 1) * along_z[:, :, :, 1:-1]
        + weight(1, 2) * along_z[:, :, :, 2:]
    )
    return (
        weight(2, 0) * jnp.roll(across, 1, 4)
        + weight(2, 1) * across
        + weight(2, 2) * jnp.roll(across, -1, 4)
    )


def depth(field, taps, flip):
    side = extended(field, (("brick", 3),), 1)
    padded = extended(side, (("slab", 2),), 1)
    return sweep(padded.astype(jnp.float32), taps, flip)


def mixing(point, field):
    return jnp.einsum("oc,vczyx->vozyx", point, field, preferred_element_type=jnp.float32)


def mixing_back(point, field):
    return jnp.einsum("co,vczyx->vozyx", point, field, preferred_element_type=jnp.float32)


def shards(
    features,
    tangents,
    route,
    cell_local,
    stencil,
    stencil_table,
    taps1,
    taps2,
    point1,
    point2,
    bias1,
    bias2,
    readout,
):
    bricks = lax.axis_size("brick")
    count = features.shape[1]
    capacity = 2 * count // bricks
    depth_z = NG // lax.axis_size("slab")
    depth_y = NG // bricks
    cells = depth_z * depth_y * NG
    vectors = NT + 1
    onehot_set = (stencil[None, :] == jnp.arange(KSETS, dtype=jnp.int32)[:, None]).astype(
        jnp.float32
    )
    tab = jnp.dot(stencil_table.T, onehot_set, precision=lax.Precision.HIGHEST)
    stacked = jnp.concatenate([features[None], tangents], 0)
    deposits = (stacked.astype(jnp.float32) * tab).astype(jnp.bfloat16).reshape(vectors * CH, count)
    target = route[:, 0]
    onehot_dest = (target[:, None] == jnp.arange(bricks, dtype=jnp.int32)[None, :]).astype(
        jnp.int32
    )
    position = jnp.sum(jnp.cumsum(onehot_dest, 0) * onehot_dest, 1) - 1
    slot = target * capacity + position
    outgoing = jnp.zeros((vectors * CH, bricks * capacity), jnp.bfloat16).at[:, slot].set(deposits)
    outgoing = outgoing.reshape(vectors * CH, bricks, capacity)
    labels = jnp.full((bricks * capacity,), cells, jnp.int32).at[slot].set(cell_local)
    labels = labels.reshape(1, bricks, capacity)
    arrived, arrived_labels = (
        lax.all_to_all(outgoing, "brick", split_axis=1, concat_axis=1, tiled=True),
        lax.all_to_all(labels, "brick", split_axis=1, concat_axis=1, tiled=True),
    )
    flat_labels = arrived_labels.reshape(-1)
    grid = jnp.zeros((vectors * CH, cells + 1), jnp.float32)
    grid = grid.at[:, flat_labels].add(arrived.reshape(vectors * CH, -1).astype(jnp.float32))
    charge = grid[:, :cells].astype(jnp.bfloat16).reshape(vectors, CH, depth_z, depth_y, NG)
    bias_one = bias1[:, None, None, None]
    bias_two = bias2[:, None, None, None]
    scale = readout[:, None, None, None]
    pre1 = mixing(point1, depth(charge[:1], taps1, False).astype(jnp.bfloat16)) + bias_one
    hidden = jax.nn.silu(pre1).astype(jnp.bfloat16)
    pre2 = mixing(point2, depth(hidden, taps2, False).astype(jnp.bfloat16)) + bias_two
    g_two = (dsilu(pre2) * scale).astype(jnp.bfloat16)
    g_one = depth(mixing_back(point2, g_two).astype(jnp.bfloat16), taps2, True)
    t_one = mixing(point1, depth(charge[1:], taps1, False).astype(jnp.bfloat16))
    moved = (dsilu(pre1) * t_one).astype(jnp.bfloat16)
    dz_two = mixing(point2, depth(moved, taps2, False).astype(jnp.bfloat16))
    dg_two = (ddsilu(pre2) * scale * dz_two).astype(jnp.bfloat16)
    dg_one = depth(mixing_back(point2, dg_two).astype(jnp.bfloat16), taps2, True)
    energy_term = (ddsilu(pre1) * t_one * g_one + dsilu(pre1) * dg_one).astype(jnp.bfloat16)
    back_one = mixing_back(point1, energy_term).astype(jnp.bfloat16)
    final = depth(back_one, taps1, True).astype(jnp.bfloat16).reshape(NT * CH, cells)
    picked = jnp.take(final, jnp.minimum(flat_labels, cells - 1), axis=1).reshape(
        NT * CH, bricks, capacity
    )
    returned = lax.all_to_all(picked, "brick", split_axis=1, concat_axis=1, tiled=True).reshape(
        NT * CH, bricks * capacity
    )
    mine = jnp.take(returned, slot, axis=1).reshape(NT, CH, count)
    return mine.astype(jnp.float32) * tab


def solution(mesh):
    placed = (
        P(None, ("slab", "brick")),
        P(None, None, ("slab", "brick")),
        P(("slab", "brick"), None),
        P(("slab", "brick")),
        P(("slab", "brick")),
        P(),
        P(),
        P(),
        P(),
        P(),
        P(),
        P(),
        P(),
    )
    return jax.shard_map(
        shards,
        mesh=mesh,
        in_specs=placed,
        out_specs=P(None, None, ("slab", "brick")),
        check_vma=False,
    )
```

profile of v0, /device:TPU:0, one launch (start us, length us, event | category | flops | bytes accessed | tf_op | source)
XLA Modules:
  0.0 784.5 jit_solution(12797079127721020908)
XLA Ops:
  23.4 10.9 %scatter_custom_fusion.1 = bf16[320,4096]{0,1:T(8,128)(2,1)S(1)} fusion(s32[2048]{0:T(1024)S(1)} %bitcast.251, bf16[320,2048]{0,1:T(8,128)(2,1)} %copy.33, bf16[]{:T(256)} %constant.54.clone.1), kind=kCustom, calls=%fused_computation.181 | custom fusion | bytes 3932162 | tf_op jit(solution)/shard_map/scatter | solution.py:106
  42.2 29.2 %all-to-all-done.1 = bf16[320,4,1024]{2,0,1:T(8,128)(2,1)S(1)} async-done(((bf16[320,4,1024]{2,0,1:T(8,128)(2,1)}), bf16[320,4,1024]{2,0,1:T(8,128)(2,1)S(1)}, u32[]{:S(2)}, u32[]{:S(2)}) %all-to-all-start.1) | async-done | bytes 2621472 | tf_op jit(solution)/shard_map/all_to_all | solution.py:111
  81.5 33.1 %scatter_custom_fusion.2 = f32[320,8193]{0,1:T(8,128)} fusion(s32[4096]{0:T(1024)S(1)} %bitcast.254, f32[4096,320]{1,0:T(8,128)} %copy.36, f32[]{:T(128)} %constant.33.clone.1), kind=kCustom, calls=%fused_computation.81 | custom fusion | flops 1310720 | bytes 10487552 | tf_op jit(solution)/shard_map/scatter-add | solution.py:116
  127.1 12.9 %reshape.610 = bf16[4,64,8,16,64]{1,0,4,3,2:T(4,128)(2,1)} reshape(bf16[256,8192]{0,1:T(8,128)(2,1)} %slice.581) | data formatting | bytes 8388608 | tf_op jit(solution)/shard_map/slice | solution.py:126
  164.7 8.9 %constant_dynamic-update-slice_fusion.1 = bf16[4,64,8,18,64]{1,4,3,2,0:T(8,128)(2,1)} fusion(bf16[4,64,8,18,64]{1,4,3,2,0:T(8,128)(2,1)} %constant_dynamic-update-slice_fusion.2, bf16[4,64,8,16,64]{1,0,4,3,2:T(4,128)(2,1)} %reshape.610), kind=kLoop, calls=%fused_computation.229 | loop fusion | bytes 16777216
  220.1 9.9 %fusion.6 = f32[4,64,8,18,64]{1,4,3,2,0:T(8,128)} fusion(f32[4,64,10,18,64]{1,4,3,2,0:T(8,128)S(1)} %maximum_convert_fusion, f32[64]{0:T(128)S(1)} %get-tuple-element.78, f32[64]{0:T(128)S(1)} %get-tuple-element.79, f32[64]{0:T(128)S(1)} %get-tuple-element.81), kind=kLoop, calls=%fused_computation.21 | loop fusion | flops 11796480 | bytes 37749504 | tf_op jit(solution)/shard_map/add | solution.py:42
  230.1 17.2 %fusion.14 = f32[4,64,8,16,64]{1,4,3,2,0:T(8,128)S(1)} fusion(f32[4,64,8,18,64]{1,4,3,2,0:T(8,128)} %fusion.6, f32[64]{0:T(128)S(1)} %get-tuple-element.85, f32[64]{0:T(128)S(1)} %get-tuple-element.80, f32[64]{0:T(128)S(1)} %get-tuple-element.82), kind=kLoop, calls=%fused_computation.41 | loop fusion | flops 10485760 | bytes 33555200 | tf_op jit(solution)/shard_map/add | solution.py:47
  247.7 12.7 %fusion.132 = (f32[4,64,8,16,63]{1,4,3,2,0:T(8,128)}, f32[4,64,8,16,63]{1,4,3,2,0:T(8,128)}) fusion(f32[4,64,8,16,64]{1,4,3,2,0:T(8,128)S(1)} %fusion.14), kind=kLoop, calls=%fused_computation.263 | loop fusion | bytes 33030144 | tf_op jit(solution)/shard_map/jit(_roll_static)/slice | solution.py:54
  263.0 26.0 %fusion.32 = (bf16[4,64,8,16,64]{1,4,3,2,0:T(8,128)(2,1)}, f32[4,8,16,64,64]{4,3,2,1,0:T(8,128)}) fusion(f32[64,8,16,64]{0,3,2,1:T(8,128)S(1)} %get-tuple-element.40, bf16[64,64]{1,0:T(8,128)(2,1)S(1)} %copy-done, f32[4,64,8,16,63]{1,4,3,2,0:T(8,128)} %get-tuple-element.20, f32[4,64,8,16,1]{1,4,3,2,0:T(1,128)S(1)} %get-tuple-element.22, ...), kind=kOutput, calls=%fused_computation.72 | convolution fusion | flops 289406976 | bytes 39854848 | tf_op jit(solution)/shard_map/oc,vczyx->vozyx/dot_general | solution.py:65
  295.8 10.4 %collective-permute-done.16 = bf16[4,64,8,1,64]{1,4,3,2,0:T(8,128)(2,1)S(1)} collective-permute-done((bf16[4,64,8,1,64]{1,4,3,2,0:T(8,128)(2,1)S(1)}, bf16[4,64,8,1,64]{1,4,3,2,0:T(8,128)(2,1)S(1)}, u32[]{:S(2)}, u32[]{:S(2)}) %collective-permute-start.16) | collective-permute-done | bytes 262176 | tf_op jit(solution)/shard_map/ppermute | solution.py:19
  325.3 21.7 %collective-permute-done.18 = bf16[4,64,1,18,64]{1,4,3,2,0:T(8,128)(2,1)} collective-permute-done((bf16[4,64,1,18,64]{1,4,3,2,0:T(8,128)(2,1)}, bf16[4,64,1,18,64]{1,4,3,2,0:T(8,128)(2,1)}, u32[]{:S(2)}, u32[]{:S(2)}) %collective-permute-start.18) | collective-permute-done | bytes 589856 | tf_op jit(solution)/shard_map/ppermute | solution.py:19
  353.9 9.9 %fusion.4 = f32[4,64,8,18,64]{1,4,3,2,0:T(8,128)} fusion(f32[4,64,10,18,64]{1,4,3,2,0:T(8,128)S(1)} %maximum_convert_fusion.1, f32[64]{0:T(128)S(1)} %get-tuple-element.69, f32[64]{0:T(128)S(1)} %get-tuple-element.70, f32[64]{0:T(128)S(1)} %get-tuple-element.73), kind=kLoop, calls=%fused_computation.16 | loop fusion | flops 11796480 | bytes 37749504 | tf_op jit(solution)/shard_map/add | solution.py:42
  363.8 17.2 %fusion.12 = f32[4,64,8,16,64]{1,4,3,2,0:T(8,128)S(1)} fusion(f32[4,64,8,18,64]{1,4,3,2,0:T(8,128)} %fusion.4, f32[64]{0:T(128)S(1)} %get-tuple-element.76, f32[64]{0:T(128)S(1)} %get-tuple-element.71, f32[64]{0:T(128)S(1)} %get-tuple-element.74), kind=kLoop, calls=%fused_computation.36 | loop fusion | flops 10485760 | bytes 33555200 | tf_op jit(solution)/shard_map/add | solution.py:47
  381.5 13.1 %fusion.130 = (f32[4,64,8,16,63]{1,4,3,2,0:T(8,128)}, f32[4,64,8,16,63]{1,4,3,2,0:T(8,128)}) fusion(f32[4,64,8,16,64]{1,4,3,2,0:T(8,128)S(1)} %fusion.12), kind=kLoop, calls=%fused_computation.261 | loop fusion | bytes 33030144 | tf_op jit(solution)/shard_map/jit(_roll_static)/slice | solution.py:54
  396.9 22.3 %convert_bitcast_fusion.1 = bf16[4,64,8,16,64]{1,4,3,2,0:T(8,128)(2,1)} fusion(f32[64,8,16,64]{0,3,2,1:T(8,128)} %fusion.61, f32[4,64,8,16,63]{1,4,3,2,0:T(8,128)} %get-tuple-element.16, f32[4,64,8,16,1]{1,4,3,2,0:T(1,128)S(1)} %get-tuple-element.18, f32[4,64,8,16,1]{1,4,3,2,0:T(1,128)S(1)} %get-tuple-element.17, ...), kind=kOutput, calls=%fused_computation.78 | convolution fusion | flops 559939584 | bytes 31466240 | tf_op jit(solution)/shard_map/co,vczyx->vozyx/dot_general | solution.py:69
  450.6 19.0 %collective-permute-done.22 = bf16[4,64,1,18,64]{1,4,3,2,0:T(8,128)(2,1)S(1)} collective-permute-done((bf16[4,64,1,18,64]{1,4,3,2,0:T(8,128)(2,1)S(1)}, bf16[4,64,1,18,64]{1,4,3,2,0:T(8,128)(2,1)S(1)}, u32[]{:S(2)}, u32[]{:S(2)}) %collective-permute-start.22) | collective-permute-done | bytes 589856 | tf_op jit(solution)/shard_map/ppermute | solution.py:19
  477.5 9.9 %fusion.2 = f32[4,64,8,18,64]{1,4,3,2,0:T(8,128)} fusion(f32[4,64,10,18,64]{1,4,3,2,0:T(8,128)S(1)} %maximum_convert_fusion.2, f32[64]{0:T(128)S(1)} %get-tuple-element.69, f32[64]{0:T(128)S(1)} %get-tuple-element.70, f32[64]{0:T(128)S(1)} %get-tuple-element.73), kind=kLoop, calls=%fused_computation.11 | loop fusion | flops 11796480 | bytes 37749504 | tf_op jit(solution)/shard_map/add | solution.py:42
  487.4 17.2 %fusion.10 = f32[4,64,8,16,64]{1,4,3,2,0:T(8,128)S(1)} fusion(f32[4,64,8,18,64]{1,4,3,2,0:T(8,128)} %fusion.2, f32[64]{0:T(128)S(1)} %get-tuple-element.76, f32[64]{0:T(128)S(1)} %get-tuple-element.71, f32[64]{0:T(128)S(1)} %get-tuple-element.74), kind=kLoop, calls=%fused_computation.31 | loop fusion | flops 10485760 | bytes 33555200 | tf_op jit(solution)/shard_map/add | solution.py:47
  505.1 13.1 %fusion.128 = (f32[4,64,8,16,63]{1,4,3,2,0:T(8,128)}, f32[4,64,8,16,63]{1,4,3,2,0:T(8,128)}) fusion(f32[4,64,8,16,64]{1,4,3,2,0:T(8,128)S(1)} %fusion.10), kind=kLoop, calls=%fused_computation.259 | loop fusion | bytes 33030144 | tf_op jit(solution)/shard_map/jit(_roll_static)/slice | solution.py:54
  520.4 29.6 %convert_bitcast_fusion = bf16[4,64,8,16,64]{1,4,3,2,0:T(8,128)(2,1)} fusion(f32[4,64,8,16,63]{1,4,3,2,0:T(8,128)} %get-tuple-element.12, f32[4,64,8,16,1]{1,4,3,2,0:T(1,128)S(1)} %get-tuple-element.14, f32[4,64,8,16,1]{1,4,3,2,0:T(1,128)S(1)} %get-tuple-element.13, f32[4,64,8,16,63]{1,4,3,2,0:T(8,128)} %get-tuple-element.11, ...), kind=kOutput, calls=%fused_computation.77 | convolution fusion | flops 295698432 | bytes 44049152 | tf_op jit(solution)/shard_map/co,vczyx->vozyx/dot_general | solution.py:69
  554.4 12.8 %collective-permute-done.24 = bf16[4,64,8,1,64]{1,4,3,2,0:T(8,128)(2,1)S(1)} collective-permute-done((bf16[4,64,8,1,64]{1,4,3,2,0:T(8,128)(2,1)S(1)}, bf16[4,64,8,1,64]{1,4,3,2,0:T(8,128)(2,1)S(1)}, u32[]{:S(2)}, u32[]{:S(2)}) %collective-permute-start.24) | collective-permute-done | bytes 262176 | tf_op jit(solution)/shard_map/ppermute | solution.py:19
  581.3 26.1 %collective-permute-done.26 = bf16[4,64,1,18,64]{1,4,3,2,0:T(8,128)(2,1)S(1)} collective-permute-done((bf16[4,64,1,18,64]{1,4,3,2,0:T(8,128)(2,1)S(1)}, bf16[4,64,1,18,64]{1,4,3,2,0:T(8,128)(2,1)S(1)}, u32[]{:S(2)}, u32[]{:S(2)}) %collective-permute-start.26) | collective-permute-done | bytes 589856 | tf_op jit(solution)/shard_map/ppermute | solution.py:19
  607.4 10.3 %maximum_convert_fusion.3 = f32[4,64,10,18,64]{1,4,3,2,0:T(8,128)} fusion(bf16[4,64,1,18,64]{1,4,3,2,0:T(8,128)(2,1)S(1)} %collective-permute-done.27, bf16[4,64,8,1,64]{1,4,3,2,0:T(8,128)(2,1)S(1)} %collective-permute-done.25, bf16[4,64,8,16,64]{1,4,3,2,0:T(8,128)(2,1)S(1)} %copy-done.8, bf16[4,64,8,1,64]{1,4,3,2,0:T(8,128)(2,1)S(1)} %collective-permute-done.24, ...), kind=kLoop, calls=%fused_computation.76 | loop fusion | flops 14745600 | bytes 17694720 | tf_op jit(solution)/shard_map/convert_element_type | solution.py:61
  617.8 18.6 %fusion = f32[4,64,8,18,64]{1,4,3,2,0:T(8,128)S(1)} fusion(f32[4,64,10,18,64]{1,4,3,2,0:T(8,128)} %maximum_convert_fusion.3, f32[64]{0:T(128)S(1)} %copy-done.50, f32[64]{0:T(128)S(1)} %copy-done.52, f32[64]{0:T(128)S(1)} %copy-done.54), kind=kLoop, calls=%fused_computation.6 | loop fusion | flops 11796480 | bytes 37749504 | tf_op jit(solution)/shard_map/add | solution.py:42
  636.5 11.4 %fusion.8 = f32[4,64,8,16,64]{1,4,3,2,0:T(8,128)} fusion(f32[4,64,8,18,64]{1,4,3,2,0:T(8,128)S(1)} %fusion, f32[64]{0:T(128)S(1)} %copy-done.47, f32[64]{0:T(128)S(1)} %copy-done.43, f32[64]{0:T(128)S(1)} %copy-done.45), kind=kLoop, calls=%fused_computation.26 | loop fusion | flops 10485760 | bytes 33555200 | tf_op jit(solution)/shard_map/add | solution.py:47
  650.6 24.9 %fusion.126 = (f32[4,64,8,16,63]{1,4,3,2,0:T(8,128)}, f32[4,64,8,16,63]{1,4,3,2,0:T(8,128)}) fusion(f32[4,64,8,16,64]{1,4,3,2,0:T(8,128)} %fusion.8), kind=kLoop, calls=%fused_computation.257 | loop fusion | bytes 33030144 | tf_op jit(solution)/shard_map/jit(_roll_static)/slice | solution.py:54
  675.5 31.4 %fusion.29 = bf16[4,64,8,16,64]{1,4,3,2,0:T(8,128)(2,1)} fusion(f32[4,64,8,16,63]{1,4,3,2,0:T(8,128)} %get-tuple-element.8, f32[4,64,8,16,1]{1,4,3,2,0:T(1,128)S(1)} %get-tuple-element.10, f32[4,64,8,16,1]{1,4,3,2,0:T(1,128)S(1)} %get-tuple-element.9, f32[4,64,8,16,63]{1,4,3,2,0:T(8,128)} %get-tuple-element.7, f32[64]{0:T(128)S(1)} %copy-done.41, ...), kind=kLoop, calls=%fused_computation.65 | loop fusion | flops 27262976 | bytes 46138880 | tf_op jit(solution)/shard_map/convert_element_type | solution.py:133
  706.8 11.1 %copy.48 = bf16[4,64,8,16,64]{1,0,4,3,2:T(4,128)(2,1)} copy(bf16[4,64,8,16,64]{1,4,3,2,0:T(8,128)(2,1)} %fusion.29) | data formatting | bytes 8388608 | tf_op jit(solution)/shard_map/reshape | solution.py:133
  717.9 12.7 %reshape.609 = bf16[256,8192]{0,1:T(8,128)(2,1)} reshape(bf16[4,64,8,16,64]{1,0,4,3,2:T(4,128)(2,1)} %copy.48) | data formatting | bytes 8388608 | tf_op jit(solution)/shard_map/reshape | solution.py:133
  730.7 15.7 %gather_fusion = bf16[4096,256]{1,0:T(8,128)(2,1)S(1)} fusion(bf16[256,8192]{0,1:T(8,128)(2,1)} %reshape.609, s32[4096]{0:T(1024)S(1)} %broadcast_clamp_fusion), kind=kCustom, calls=%fused_computation | custom fusion | bytes 4210688 | tf_op jit(solution)/shard_map/jit(_take)/gather | solution.py:134
  751.7 20.4 %all-to-all-done.2 = bf16[256,4,1024]{0,2,1:T(8,128)(2,1)S(1)} async-done(((bf16[256,4,1024]{0,2,1:T(8,128)(2,1)}), bf16[256,4,1024]{0,2,1:T(8,128)(2,1)S(1)}, u32[]{:S(2)}, u32[]{:S(2)}) %all-to-all-start.2) | async-done | bytes 2097184 | tf_op jit(solution)/shard_map/all_to_all | solution.py:137
  772.2 9.0 %gather_fusion.1 = bf16[2048,256]{1,0:T(8,128)(2,1)} fusion(bf16[256,4096]{0,1:T(8,128)(2,1)S(1)} %bitcast.235, s32[2048]{0:T(1024)S(1)} %broadcast_clamp_fusion.1), kind=kCustom, calls=%fused_computation.1 | custom fusion | bytes 2105344 | tf_op jit(solution)/shard_map/jit(_take)/gather | solution.py:140
  (259 shorter events, 234.5 us)
Async XLA Ops:
  13.2 23.9 %all-to-all-start = ((s32[1,4,1024]{2,0,1:T(1,128)}), s32[1,4,1024]{2,0,1:T(1,128)S(1)}, u32[]{:S(2)}, u32[]{:S(2)}) async-start(s32[1,4,1024]{2,0,1:T(1,128)} %bitcast.5), calls=%async_computation | async-start | bytes 32768 | tf_op jit(solution)/shard_map/all_to_all | solution.py:112
  37.1 34.3 %all-to-all-start.1 = ((bf16[320,4,1024]{2,0,1:T(8,128)(2,1)}), bf16[320,4,1024]{2,0,1:T(8,128)(2,1)S(1)}, u32[]{:S(2)}, u32[]{:S(2)}) async-start(bf16[320,4,1024]{2,0,1:T(8,128)(2,1)} %copy.34), calls=%async_computation.1 | async-start | bytes 5242880 | tf_op jit(solution)/shard_map/all_to_all | solution.py:111
  41.6 221.4 %copy-start.36 = (f32[64]{0:T(128)}, f32[64]{0:T(128)S(1)}, u32[]{:S(2)}) copy-start(f32[64]{0:T(128)S(1)} %get-tuple-element.77) | copy-start | bytes 772
  119.9 20.0 %collective-permute-start = (bf16[1,64,8,1,64]{1,4,3,2,0:T(8,128)(2,1)S(1)}, bf16[1,64,8,1,64]{1,4,3,2,0:T(8,128)(2,1)S(1)}, u32[]{:S(2)}, u32[]{:S(2)}) collective-permute-start(bf16[1,64,8,1,64]{1,4,3,2,0:T(8,128)(2,1)S(1)} %get-tuple-element.64), channel_id=1, source_target_pairs={{0,1},{1,2},{2,3},{3,0},{4,5},{5,6},{6,7},{7,4},{8,9},{9,10},{10,1... | collective-permute-start | bytes 196616 | tf_op jit(solution)/shard_map/ppermute | solution.py:19
  122.0 18.0 %collective-permute-start.1 = (bf16[1,64,8,1,64]{1,4,3,2,0:T(8,128)(2,1)S(1)}, bf16[1,64,8,1,64]{1,4,3,2,0:T(8,128)(2,1)S(1)}, u32[]{:S(2)}, u32[]{:S(2)}) collective-permute-start(bf16[1,64,8,1,64]{1,4,3,2,0:T(8,128)(2,1)S(1)} %get-tuple-element.65), channel_id=1, source_target_pairs={{1,0},{2,1},{3,2},{0,3},{5,4},{6,5},{7,6},{4,7},{9,8},{10,9},{11,1... | collective-permute-start | bytes 196616 | tf_op jit(solution)/shard_map/ppermute | solution.py:20
  140.1 8.9 %collective-permute-start.2 = (bf16[1,64,1,18,64]{1,4,3,2,0:T(8,128)(2,1)S(1)}, bf16[1,64,1,18,64]{1,4,3,2,0:T(8,128)(2,1)S(1)}, u32[]{:S(2)}, u32[]{:S(2)}) collective-permute-start(bf16[1,64,1,18,64]{1,4,3,2,0:T(8,128)(2,1)S(1)} %get-tuple-element.58), channel_id=1, source_target_pairs={{0,4},{4,8},{8,12},{12,16},{16,20},{20,24},{24,28},{28,0},{1,5},{5... | collective-permute-start | bytes 442376 | tf_op jit(solution)/shard_map/ppermute | solution.py:19
  140.2 8.8 %collective-permute-start.3 = (bf16[1,64,1,18,64]{1,4,3,2,0:T(8,128)(2,1)S(1)}, bf16[1,64,1,18,64]{1,4,3,2,0:T(8,128)(2,1)S(1)}, u32[]{:S(2)}, u32[]{:S(2)}) collective-permute-start(bf16[1,64,1,18,64]{1,4,3,2,0:T(8,128)(2,1)S(1)} %get-tuple-element.59), channel_id=1, source_target_pairs={{4,0},{8,4},{12,8},{16,12},{20,16},{24,20},{28,24},{0,28},{5,1},{9... | collective-permute-start | bytes 442376 | tf_op jit(solution)/shard_map/ppermute | solution.py:20
  145.5 18.2 %collective-permute-start.4 = (bf16[4,64,8,1,64]{1,4,3,2,0:T(8,128)(2,1)S(1)}, bf16[4,64,8,1,64]{1,4,3,2,0:T(8,128)(2,1)S(1)}, u32[]{:S(2)}, u32[]{:S(2)}) collective-permute-start(bf16[4,64,8,1,64]{1,4,3,2,0:T(8,128)(2,1)S(1)} %copy.60), channel_id=1, source_target_pairs={{0,1},{1,2},{2,3},{3,0},{4,5},{5,6},{6,7},{7,4},{8,9},{9,10},{10,1... | collective-permute-start | bytes 786440 | tf_op jit(solution)/shard_map/ppermute | solution.py:19
  146.7 26.9 %collective-permute-start.5 = (bf16[4,64,8,1,64]{1,4,3,2,0:T(8,128)(2,1)S(1)}, bf16[4,64,8,1,64]{1,4,3,2,0:T(8,128)(2,1)S(1)}, u32[]{:S(2)}, u32[]{:S(2)}) collective-permute-start(bf16[4,64,8,1,64]{1,4,3,2,0:T(8,128)(2,1)S(1)} %copy.61), channel_id=1, source_target_pairs={{1,0},{2,1},{3,2},{0,3},{5,4},{6,5},{7,6},{4,7},{9,8},{10,9},{11,1... | collective-permute-start | bytes 786440 | tf_op jit(solution)/shard_map/ppermute | solution.py:20
  160.8 13.8 %collective-permute-start.8 = (bf16[1,64,8,1,64]{1,4,3,2,0:T(8,128)(2,1)S(1)}, bf16[1,64,8,1,64]{1,4,3,2,0:T(8,128)(2,1)S(1)}, u32[]{:S(2)}, u32[]{:S(2)}) collective-permute-start(bf16[1,64,8,1,64]{1,4,3,2,0:T(8,128)(2,1)S(1)} %get-tuple-element.62), channel_id=1, source_target_pairs={{0,1},{1,2},{2,3},{3,0},{4,5},{5,6},{6,7},{7,4},{8,9},{9,10},{10,1... | collective-permute-start | bytes 196616 | tf_op jit(solution)/shard_map/ppermute | solution.py:19
  162.0 12.6 %collective-permute-start.9 = (bf16[1,64,8,1,64]{1,4,3,2,0:T(8,128)(2,1)S(1)}, bf16[1,64,8,1,64]{1,4,3,2,0:T(8,128)(2,1)S(1)}, u32[]{:S(2)}, u32[]{:S(2)}) collective-permute-start(bf16[1,64,8,1,64]{1,4,3,2,0:T(8,128)(2,1)S(1)} %get-tuple-element.63), channel_id=1, source_target_pairs={{1,0},{2,1},{3,2},{0,3},{5,4},{6,5},{7,6},{4,7},{9,8},{10,9},{11,1... | collective-permute-start | bytes 196616 | tf_op jit(solution)/shard_map/ppermute | solution.py:20
  175.7 11.2 %collective-permute-start.10 = (bf16[1,64,1,18,64]{1,4,3,2,0:T(8,128)(2,1)S(1)}, bf16[1,64,1,18,64]{1,4,3,2,0:T(8,128)(2,1)S(1)}, u32[]{:S(2)}, u32[]{:S(2)}) collective-permute-start(bf16[1,64,1,18,64]{1,4,3,2,0:T(8,128)(2,1)S(1)} %get-tuple-element.56), channel_id=1, source_target_pairs={{0,4},{4,8},{8,12},{12,16},{16,20},{20,24},{24,28},{28,0},{1,5},{5... | collective-permute-start | bytes 442376 | tf_op jit(solution)/shard_map/ppermute | solution.py:19
  177.6 9.4 %collective-permute-start.11 = (bf16[1,64,1,18,64]{1,4,3,2,0:T(8,128)(2,1)S(1)}, bf16[1,64,1,18,64]{1,4,3,2,0:T(8,128)(2,1)S(1)}, u32[]{:S(2)}, u32[]{:S(2)}) collective-permute-start(bf16[1,64,1,18,64]{1,4,3,2,0:T(8,128)(2,1)S(1)} %get-tuple-element.57), channel_id=1, source_target_pairs={{4,0},{8,4},{12,8},{16,12},{20,16},{24,20},{28,24},{0,28},{5,1},{9... | collective-permute-start | bytes 442376 | tf_op jit(solution)/shard_map/ppermute | solution.py:20
  183.0 29.0 %collective-permute-start.6 = (bf16[4,64,1,18,64]{1,4,3,2,0:T(8,128)(2,1)}, bf16[4,64,1,18,64]{1,4,3,2,0:T(8,128)(2,1)S(1)}, u32[]{:S(2)}, u32[]{:S(2)}) collective-permute-start(bf16[4,64,1,18,64]{1,4,3,2,0:T(8,128)(2,1)} %get-tuple-element.29), channel_id=1, source_target_pairs={{0,4},{4,8},{8,12},{12,16},{16,20},{20,24},{24,28},{28,0},{1,5},{5... | collective-permute-start | bytes 1769480 | tf_op jit(solution)/shard_map/ppermute | solution.py:19
  183.0 30.0 %collective-permute-start.7 = (bf16[4,64,1,18,64]{1,4,3,2,0:T(8,128)(2,1)}, bf16[4,64,1,18,64]{1,4,3,2,0:T(8,128)(2,1)}, u32[]{:S(2)}, u32[]{:S(2)}) collective-permute-start(bf16[4,64,1,18,64]{1,4,3,2,0:T(8,128)(2,1)} %get-tuple-element.30), channel_id=1, source_target_pairs={{4,0},{8,4},{12,8},{16,12},{20,16},{24,20},{28,24},{0,28},{5,1},{9... | collective-permute-start | bytes 1769480 | tf_op jit(solution)/shard_map/ppermute | solution.py:20
  195.4 7.3 collective-permute-start.12
  195.7 8.6 %collective-permute-start.13 = (bf16[1,64,8,1,64]{1,4,3,2,0:T(8,128)(2,1)S(1)}, bf16[1,64,8,1,64]{1,4,3,2,0:T(8,128)(2,1)S(1)}, u32[]{:S(2)}, u32[]{:S(2)}) collective-permute-start(bf16[1,64,8,1,64]{1,4,3,2,0:T(8,128)(2,1)S(1)} %get-tuple-element.61), channel_id=1, source_target_pairs={{1,0},{2,1},{3,2},{0,3},{5,4},{6,5},{7,6},{4,7},{9,8},{10,9},{11,1... | collective-permute-start | bytes 196616 | tf_op jit(solution)/shard_map/ppermute | solution.py:20
  205.3 88.1 %collective-permute-start.14 = (bf16[1,64,1,18,64]{1,4,3,2,0:T(8,128)(2,1)}, bf16[1,64,1,18,64]{1,4,3,2,0:T(8,128)(2,1)}, u32[]{:S(2)}, u32[]{:S(2)}) collective-permute-start(bf16[1,64,1,18,64]{1,4,3,2,0:T(8,128)(2,1)} %get-tuple-element.54), channel_id=1, source_target_pairs={{0,4},{4,8},{8,12},{12,16},{16,20},{20,24},{24,28},{28,0},{1,5},{5... | collective-permute-start | bytes 442376 | tf_op jit(solution)/shard_map/ppermute | solution.py:19
  205.3 88.1 %collective-permute-start.15 = (bf16[1,64,1,18,64]{1,4,3,2,0:T(8,128)(2,1)}, bf16[1,64,1,18,64]{1,4,3,2,0:T(8,128)(2,1)}, u32[]{:S(2)}, u32[]{:S(2)}) collective-permute-start(bf16[1,64,1,18,64]{1,4,3,2,0:T(8,128)(2,1)} %get-tuple-element.55), channel_id=1, source_target_pairs={{4,0},{8,4},{12,8},{16,12},{20,16},{24,20},{28,24},{0,28},{5,1},{9... | collective-permute-start | bytes 442376 | tf_op jit(solution)/shard_map/ppermute | solution.py:20
  290.4 15.8 %collective-permute-start.16 = (bf16[4,64,8,1,64]{1,4,3,2,0:T(8,128)(2,1)S(1)}, bf16[4,64,8,1,64]{1,4,3,2,0:T(8,128)(2,1)S(1)}, u32[]{:S(2)}, u32[]{:S(2)}) collective-permute-start(bf16[4,64,8,1,64]{1,4,3,2,0:T(8,128)(2,1)S(1)} %get-tuple-element.35), channel_id=1, source_target_pairs={{0,1},{1,2},{2,3},{3,0},{4,5},{5,6},{6,7},{7,4},{8,9},{9,10},{10,1... | collective-permute-start | bytes 786440 | tf_op jit(solution)/shard_map/ppermute | solution.py:19
  290.4 24.5 %collective-permute-start.17 = (bf16[4,64,8,1,64]{1,4,3,2,0:T(8,128)(2,1)S(1)}, bf16[4,64,8,1,64]{1,4,3,2,0:T(8,128)(2,1)S(1)}, u32[]{:S(2)}, u32[]{:S(2)}) collective-permute-start(bf16[4,64,8,1,64]{1,4,3,2,0:T(8,128)(2,1)S(1)} %get-tuple-element.36), channel_id=1, source_target_pairs={{1,0},{2,1},{3,2},{0,3},{5,4},{6,5},{7,6},{4,7},{9,8},{10,9},{11,1... | collective-permute-start | bytes 786440 | tf_op jit(solution)/shard_map/ppermute | solution.py:20
  316.9 30.1 %collective-permute-start.18 = (bf16[4,64,1,18,64]{1,4,3,2,0:T(8,128)(2,1)}, bf16[4,64,1,18,64]{1,4,3,2,0:T(8,128)(2,1)}, u32[]{:S(2)}, u32[]{:S(2)}) collective-permute-start(bf16[4,64,1,18,64]{1,4,3,2,0:T(8,128)(2,1)} %get-tuple-element.27), channel_id=1, source_target_pairs={{0,4},{4,8},{8,12},{12,16},{16,20},{20,24},{24,28},{28,0},{1,5},{5... | collective-permute-start | bytes 1769480 | tf_op jit(solution)/shard_map/ppermute | solution.py:19
  316.9 30.1 %collective-permute-start.19 = (bf16[4,64,1,18,64]{1,4,3,2,0:T(8,128)(2,1)}, bf16[4,64,1,18,64]{1,4,3,2,0:T(8,128)(2,1)}, u32[]{:S(2)}, u32[]{:S(2)}) collective-permute-start(bf16[4,64,1,18,64]{1,4,3,2,0:T(8,128)(2,1)} %get-tuple-element.28), channel_id=1, source_target_pairs={{4,0},{8,4},{12,8},{16,12},{20,16},{24,20},{28,24},{0,28},{5,1},{9... | collective-permute-start | bytes 1769480 | tf_op jit(solution)/shard_map/ppermute | solution.py:20
  420.5 15.2 %collective-permute-start.20 = (bf16[4,64,8,1,64]{1,4,3,2,0:T(8,128)(2,1)S(1)}, bf16[4,64,8,1,64]{1,4,3,2,0:T(8,128)(2,1)S(1)}, u32[]{:S(2)}, u32[]{:S(2)}) collective-permute-start(bf16[4,64,8,1,64]{1,4,3,2,0:T(8,128)(2,1)S(1)} %get-tuple-element.33), channel_id=1, source_target_pairs={{0,1},{1,2},{2,3},{3,0},{4,5},{5,6},{6,7},{7,4},{8,9},{9,10},{10,1... | collective-permute-start | bytes 786440 | tf_op jit(solution)/shard_map/ppermute | solution.py:19
  420.7 21.3 %collective-permute-start.21 = (bf16[4,64,8,1,64]{1,4,3,2,0:T(8,128)(2,1)S(1)}, bf16[4,64,8,1,64]{1,4,3,2,0:T(8,128)(2,1)S(1)}, u32[]{:S(2)}, u32[]{:S(2)}) collective-permute-start(bf16[4,64,8,1,64]{1,4,3,2,0:T(8,128)(2,1)S(1)} %get-tuple-element.34), channel_id=1, source_target_pairs={{1,0},{2,1},{3,2},{0,3},{5,4},{6,5},{7,6},{4,7},{9,8},{10,9},{11,1... | collective-permute-start | bytes 786440 | tf_op jit(solution)/shard_map/ppermute | solution.py:20
  442.8 26.8 %collective-permute-start.22 = (bf16[4,64,1,18,64]{1,4,3,2,0:T(8,128)(2,1)S(1)}, bf16[4,64,1,18,64]{1,4,3,2,0:T(8,128)(2,1)S(1)}, u32[]{:S(2)}, u32[]{:S(2)}) collective-permute-start(bf16[4,64,1,18,64]{1,4,3,2,0:T(8,128)(2,1)S(1)} %get-tuple-element.25), channel_id=1, source_target_pairs={{0,4},{4,8},{8,12},{12,16},{16,20},{20,24},{24,28},{28,0},{1,5},{5... | collective-permute-start | bytes 1769480 | tf_op jit(solution)/shard_map/ppermute | solution.py:19
  442.8 27.8 %collective-permute-start.23 = (bf16[4,64,1,18,64]{1,4,3,2,0:T(8,128)(2,1)S(1)}, bf16[4,64,1,18,64]{1,4,3,2,0:T(8,128)(2,1)}, u32[]{:S(2)}, u32[]{:S(2)}) collective-permute-start(bf16[4,64,1,18,64]{1,4,3,2,0:T(8,128)(2,1)S(1)} %get-tuple-element.26), channel_id=1, source_target_pairs={{4,0},{8,4},{12,8},{16,12},{20,16},{24,20},{28,24},{0,28},{5,1},{9... | collective-permute-start | bytes 1769480 | tf_op jit(solution)/shard_map/ppermute | solution.py:20
  551.4 15.8 %collective-permute-start.24 = (bf16[4,64,8,1,64]{1,4,3,2,0:T(8,128)(2,1)S(1)}, bf16[4,64,8,1,64]{1,4,3,2,0:T(8,128)(2,1)S(1)}, u32[]{:S(2)}, u32[]{:S(2)}) collective-permute-start(bf16[4,64,8,1,64]{1,4,3,2,0:T(8,128)(2,1)S(1)} %get-tuple-element.31), channel_id=1, source_target_pairs={{0,1},{1,2},{2,3},{3,0},{4,5},{5,6},{6,7},{7,4},{8,9},{9,10},{10,1... | collective-permute-start | bytes 786440 | tf_op jit(solution)/shard_map/ppermute | solution.py:19
  552.4 23.1 %collective-permute-start.25 = (bf16[4,64,8,1,64]{1,4,3,2,0:T(8,128)(2,1)S(1)}, bf16[4,64,8,1,64]{1,4,3,2,0:T(8,128)(2,1)S(1)}, u32[]{:S(2)}, u32[]{:S(2)}) collective-permute-start(bf16[4,64,8,1,64]{1,4,3,2,0:T(8,128)(2,1)S(1)} %get-tuple-element.32), channel_id=1, source_target_pairs={{1,0},{2,1},{3,2},{0,3},{5,4},{6,5},{7,6},{4,7},{9,8},{10,9},{11,1... | collective-permute-start | bytes 786440 | tf_op jit(solution)/shard_map/ppermute | solution.py:20
  577.6 29.8 %collective-permute-start.26 = (bf16[4,64,1,18,64]{1,4,3,2,0:T(8,128)(2,1)S(1)}, bf16[4,64,1,18,64]{1,4,3,2,0:T(8,128)(2,1)S(1)}, u32[]{:S(2)}, u32[]{:S(2)}) collective-permute-start(bf16[4,64,1,18,64]{1,4,3,2,0:T(8,128)(2,1)S(1)} %get-tuple-element.23), channel_id=1, source_target_pairs={{0,4},{4,8},{8,12},{12,16},{16,20},{20,24},{24,28},{28,0},{1,5},{5... | collective-permute-start | bytes 1769480 | tf_op jit(solution)/shard_map/ppermute | solution.py:19
  577.7 29.7 %collective-permute-start.27 = (bf16[4,64,1,18,64]{1,4,3,2,0:T(8,128)(2,1)S(1)}, bf16[4,64,1,18,64]{1,4,3,2,0:T(8,128)(2,1)S(1)}, u32[]{:S(2)}, u32[]{:S(2)}) collective-permute-start(bf16[4,64,1,18,64]{1,4,3,2,0:T(8,128)(2,1)S(1)} %get-tuple-element.24), channel_id=1, source_target_pairs={{4,0},{8,4},{12,8},{16,12},{20,16},{24,20},{28,24},{0,28},{5,1},{9... | collective-permute-start | bytes 1769480 | tf_op jit(solution)/shard_map/ppermute | solution.py:20
  748.1 24.1 %all-to-all-start.2 = ((bf16[256,4,1024]{0,2,1:T(8,128)(2,1)}), bf16[256,4,1024]{0,2,1:T(8,128)(2,1)S(1)}, u32[]{:S(2)}, u32[]{:S(2)}) async-start(bf16[256,4,1024]{0,2,1:T(8,128)(2,1)} %broadcast_select_fusion), calls=%async_computation.2 | async-start | bytes 4194304 | tf_op jit(solution)/shard_map/all_to_all | solution.py:137
  (63 other events, 2821.1 us)
where the time goes:
time: 793 us; the launch traced here: 785 us
  other arithmetic  250 us (32%)
  local copies, waits for them, and re-layouts  210 us (26%)
  waiting for transfers between devices  175 us (22%)
  matrix products  87.7 us (11%)
  starting transfers between devices  60.2 us (8%)
    ppermute x14, waiting for transfers between devices, extended(): before = lax.ppermute(last, axis, up)  99.8 us
    slice x14, local copies, waits for them, and re-layouts, sweep(): jnp.roll(across, -1, 4)  77.7 us
    add x7, other arithmetic, sweep(): weight(1, 0) * along_z[:, :, :, :-2] + weight(1, 1) * along_z[:, :, :, 1:-1]  67.5 us
    dot_general x3, matrix products, mixing_back(): jnp.einsum('co,vczyx->vozyx', point, field, preferred_element_type=jnp.fl...  53.7 us
    add x7, other arithmetic, sweep(): weight(0, 0) * padded[:, :, :-2] + weight(0, 1) * padded[:, :, 1:-1]  52.2 us
    ppermute x14, starting transfers between devices, extended(): after = lax.ppermute(leading, axis, down)  39.1 us
    convert_element_type x7, other arithmetic, depth(): return sweep(padded.astype(jnp.float32), taps, flip)  35.7 us
    scatter-add x1, other arithmetic, shards(): grid.at[:, flat_labels]  33.1 us
  transfers between devices with their start and end apart: 31, of which 16 were waited for; matrix products, arithmetic and copies ran while one was open for 21% of the time, Pallas kernels for 0%

commit v1 on v0

v1 whole, which is shorter than its diff:
```python
import functools

import jax
import jax.numpy as jnp
from jax import lax
from jax.experimental import pallas as pl
from jax.experimental.pallas import tpu as pltpu
from jax.sharding import PartitionSpec as P

NG = 64
CH = 64
NT = 4
KSETS = 8
LANES = 2 * CH
HALF = NG // 2
GROUP = 4
VMEM_LIMIT = 56 * 1024 * 1024
F32 = jnp.float32
BF16 = jnp.bfloat16


def params():
    return pltpu.CompilerParams(vmem_limit_bytes=VMEM_LIMIT)


def cost(flops, nbytes):
    return pl.CostEstimate(flops=flops, bytes_accessed=nbytes, transcendentals=0)


def vmem():
    return pl.BlockSpec(memory_space=pltpu.VMEM)


def smem():
    return pl.BlockSpec(memory_space=pltpu.SMEM)


def deposits_kernel(peers, me_ref, feat_ref, tan_ref, sten_ref, table_ref, tab_ref, *outs):
    me = me_ref[0]
    count = feat_ref.shape[1]
    step = min(256, count)
    columns = [table_ref[:, s : s + 1] for s in range(KSETS)]
    for start in range(0, count, step):
        at = pl.ds(start, step)
        kinds = jnp.broadcast_to(sten_ref[:, at], (CH, step))
        tab = jnp.zeros((CH, step), F32)
        for s in range(KSETS):
            tab = jnp.where(kinds == s, columns[s], tab)
        tab_ref[:, at] = tab
        first = (feat_ref[:, at].astype(F32) * tab).astype(BF16)
        for j in range(peers):
            outs[j][:CH, at] = first
            own = tan_ref[lax.rem(lax.bitwise_xor(me, j), NT), :, at]
            outs[j][CH:, at] = (own.astype(F32) * tab).astype(BF16)


def make_deposits(me, features, tangents, stencil, table, peers):
    count = features.shape[1]
    out_shape = [jax.ShapeDtypeStruct((CH, count), F32)]
    out_shape += [jax.ShapeDtypeStruct((LANES, count), BF16)] * peers
    return pl.pallas_call(
        functools.partial(deposits_kernel, peers),
        out_shape=out_shape,
        in_specs=[smem()] + [vmem()] * 4,
        out_specs=[vmem()] * (peers + 1),
        compiler_params=params(),
        name="deposits",
    )(me, features, tangents, stencil.reshape(1, count), table.T)


def charge_kernel(peers, depth, *refs):
    cells, chunks = refs[:peers], refs[peers : 2 * peers]
    q_ref, low_ref, high_ref, grid_ref, rows_ref = refs[2 * peers :]
    step = pl.program_id(0)
    count = rows_ref.shape[0]
    unroll = 8

    @pl.when(step == 0)
    def _():
        def clear(i, carry):
            grid_ref[pl.ds(pl.multiple_of(i * 256, 256), 256), :] = jnp.zeros((256, LANES), F32)
            return carry

        lax.fori_loop(0, grid_ref.shape[0] // 256, clear, 0)
        for j in range(peers):
            for start in range(0, count, 256):
                block = chunks[j][:, start : start + 256].astype(F32)
                rows_ref[start : start + 256, :] = block.T

            def add(i, carry, j=j):
                for t in range(unroll):
                    atom = i * unroll + t
                    cell = cells[j][atom]
                    grid_ref[pl.ds(cell, 1), :] += rows_ref[pl.ds(atom, 1), :]
                return carry

            lax.fori_loop(0, count // unroll, add, 0)

    @pl.when(step > 0)
    def _():
        layer = step - 1

        def finish(y, carry):
            at = pl.multiple_of((layer * NG + y) * NG, NG)
            q_ref[0, y] = grid_ref[pl.ds(at, NG), :].astype(BF16)
            return carry

        lax.fori_loop(0, NG, finish, 0)

        @pl.when(layer == 0)
        def _():
            low_ref[...] = q_ref[...]

        @pl.when(layer == depth - 1)
        def _():
            high_ref[...] = q_ref[...]


def make_charge(cells, chunks, depth):
    peers = len(chunks)
    count = chunks[0].shape[1]
    layer = (1, NG, NG, LANES)
    edge = pl.BlockSpec(layer, lambda s: (0, 0, 0, 0))
    return pl.pallas_call(
        functools.partial(charge_kernel, peers, depth),
        grid=(depth + 1,),
        out_shape=[
            jax.ShapeDtypeStruct((depth, NG, NG, LANES), BF16),
            jax.ShapeDtypeStruct(layer, BF16),
            jax.ShapeDtypeStruct(layer, BF16),
        ],
        in_specs=[smem()] * peers + [vmem()] * peers,
        out_specs=[
            pl.BlockSpec(layer, lambda s: (jnp.maximum(s - 1, 0), 0, 0, 0)),
            edge,
            edge,
        ],
        scratch_shapes=[
            pltpu.VMEM((depth * NG * NG, LANES), F32),
            pltpu.VMEM((count, LANES), F32),
        ],
        compiler_params=params(),
        name="charge",
    )(*cells, *chunks)


def spread(weights, value):
    rows = value.shape[0]
    return (value.reshape(rows // 8, 8, LANES) * weights[None]).reshape(rows, LANES)


def taps_of(w_ref, axis):
    return [w_ref[3 * axis + t] for t in range(3)]


def weigh(w, low, mid, high):
    return spread(w[0], low) + spread(w[1], mid) + spread(w[2], high)


def along_z(w, low, mid, high, u_ref, rows, offset):
    def body(y, carry):
        u_ref[y + offset] = weigh(
            w, low[0, y].astype(F32), mid[0, y].astype(F32), high[0, y].astype(F32)
        )
        return carry

    lax.fori_loop(0, rows, body, 0, unroll=2)


def wrap_halves(u_ref):
    u_ref[0] = pltpu.roll(u_ref[HALF], CH, 1)
    u_ref[HALF + 1] = pltpu.roll(u_ref[1], CH, 1)


def along_yx(wy, wx, u_ref, before, here, after):
    v = weigh(wy, u_ref[before], u_ref[here], u_ref[after])
    return weigh(wx, pltpu.roll(v, 1, 0), v, pltpu.roll(v, NG - 1, 0))


def sigmoid(v):
    return 1.0 / (1.0 + jnp.exp(-v))


def first_stage(refs, u_refs, outs):
    w_ref, mix_ref, bias_ref = refs
    (u_ref,) = u_refs
    h_ref, m_ref, a_ref, b_ref = outs
    wy, wx = taps_of(w_ref, 1), taps_of(w_ref, 2)

    def body(i, carry):
        rows = []
        for t in range(GROUP):
            y = i * GROUP + t
            top = along_yx(wy, wx, u_ref, jnp.bitwise_and(y + NG - 1, NG - 1), y, y + 1)
            z = y + HALF
            end = along_yx(wy, wx, u_ref, z - 1, z, jnp.bitwise_and(z + 1, NG - 1))
            rows.append(jnp.concatenate([top.astype(BF16), end.astype(BF16)], 1))
        mixed = jnp.dot(jnp.concatenate(rows, 0), mix_ref[...], preferred_element_type=F32)
        for t in range(GROUP):
            y = i * GROUP + t
            part = mixed[t * NG : (t + 1) * NG]
            pre = part[:, :LANES] + bias_ref[...]
            tangent = part[:, LANES:]
            sg = sigmoid(pre)
            rest = 1.0 - sg
            slope = sg * (1.0 + pre * rest)
            curve = sg * rest * (2.0 + pre * (1.0 - 2.0 * sg))
            h_ref[0, y] = (pre * sg).astype(BF16)
            m_ref[0, y] = (slope * tangent).astype(BF16)
            a_ref[0, y] = curve * tangent
            b_ref[0, y] = slope
        return carry

    lax.fori_loop(0, HALF // GROUP, body, 0)


def second_stage(refs, u_refs, outs):
    w_ref, mix_ref, back_ref, bias_ref, scale_ref = refs
    uh_ref, um_ref = u_refs
    rh_ref, rm_ref = outs
    wy, wx = taps_of(w_ref, 1), taps_of(w_ref, 2)

    def body(i, carry):
        rows = []
        for t in range(GROUP):
            y = i * GROUP + t
            sh = along_yx(wy, wx, uh_ref, y, y + 1, y + 2)
            sm = along_yx(wy, wx, um_ref, y, y + 1, y + 2)
            rows.append(jnp.concatenate([sh.astype(BF16), sm.astype(BF16)], 1))
        mixed = jnp.dot(jnp.concatenate(rows, 0), mix_ref[...], preferred_element_type=F32)
        pre = mixed[:, :LANES] + bias_ref[...]
        sg = sigmoid(pre)
        rest = 1.0 - sg
        scale = scale_ref[...]
        grad = sg * (1.0 + pre * rest) * scale
        bend = sg * rest * (2.0 + pre * (1.0 - 2.0 * sg)) * scale * mixed[:, LANES:]
        both = jnp.concatenate([grad.astype(BF16), bend.astype(BF16)], 1)
        back = jnp.dot(both, back_ref[...], preferred_element_type=F32).astype(BF16)
        for t in range(GROUP):
            y = i * GROUP + t
            rh_ref[0, y] = back[t * NG : (t + 1) * NG, :LANES]
            rm_ref[0, y] = back[t * NG : (t + 1) * NG, LANES:]
        return carry

    lax.fori_loop(0, HALF // GROUP, body, 0)


def third_stage(refs, u_refs, outs):
    w_ref, back_ref, a_ref, b_ref = refs
    uh_ref, um_ref = u_refs
    (y_ref,) = outs
    wy, wx = taps_of(w_ref, 1), taps_of(w_ref, 2)

    def body(i, carry):
        rows = []
        for t in range(GROUP):
            y = i * GROUP + t
            g = along_yx(wy, wx, uh_ref, y, y + 1, y + 2)
            dg = along_yx(wy, wx, um_ref, y, y + 1, y + 2)
            rows.append((a_ref[0, y] * g + b_ref[0, y] * dg).astype(BF16))
        back = jnp.dot(jnp.concatenate(rows, 0), back_ref[...], preferred_element_type=F32)
        for t in range(GROUP):
            y_ref[0, i * GROUP + t] = back[t * NG : (t + 1) * NG].astype(BF16)
        return carry

    lax.fori_loop(0, HALF // GROUP, body, 0)


def fourth_stage(refs, u_refs, outs):
    (w_ref,) = refs
    (u_ref,) = u_refs
    (f_ref,) = outs
    wy, wx = taps_of(w_ref, 1), taps_of(w_ref, 2)

    def body(i, carry):
        for t in range(2):
            y = i * 2 + t
            f_ref[0, y] = along_yx(wy, wx, u_ref, y, y + 1, y + 2).astype(BF16).astype(F32)
        return carry

    lax.fori_loop(0, HALF // 2, body, 0)


STAGES = {
    "first": (first_stage, NG, (BF16, BF16, F32, F32), (0, 1)),
    "second": (second_stage, HALF, (BF16, BF16), (0, 1)),
    "third": (third_stage, HALF, (BF16,), (0,)),
    "fourth": (fourth_stage, HALF, (F32,), ()),
}


def stage_kernel(stage, edges, n_field, n_const, n_local, refs):
    body, rows, kinds, sent = STAGES[stage]
    refs = list(refs)

    def take(n):
        got = refs[:n]
        del refs[:n]
        return got

    consts = take(n_const)
    fields = [take(4 if edges else 3) for _ in range(n_field)]
    local = take(n_local)
    if edges:
        take(len(kinds))
    outs = take(len(kinds))
    sends = [take(2) for _ in sent] if edges else []
    u_refs = refs
    offset = 0 if rows == NG else 1
    wz = taps_of(consts[0], 0)
    for field, u_ref in zip(fields, u_refs):
        if edges:
            step = pl.program_id(0)
            below, here, inner, above = field

            @pl.when(step == 0)
            def _():
                along_z(wz, below, here, inner, u_ref, rows, offset)

            @pl.when(step == 1)
            def _():
                along_z(wz, inner, here, above, u_ref, rows, offset)
        else:
            along_z(wz, *field, u_ref, rows, offset)
        if offset:
            wrap_halves(u_ref)
    body(consts + local, u_refs, outs)
    for index, (low_ref, high_ref) in zip(sent, sends):

        @pl.when(step == 0)
        def _():
            low_ref[...] = outs[index][...]

        @pl.when(step == 1)
        def _():
            high_ref[...] = outs[index][...]


def run_stage(stage, depth, consts, fields, local, edge_halos=None, previous=None):
    body, rows, kinds, sent = STAGES[stage]
    edges = edge_halos is not None
    last = depth - 1
    in_layer = (1, rows, NG, LANES)
    out_layer = (1, HALF, NG, LANES)

    def whole(array):
        nil = (0,) * array.ndim
        return pl.BlockSpec(array.shape, lambda s: nil)

    def layer(shape, where):
        return pl.BlockSpec(shape, lambda s: (where(s), 0, 0, 0))

    def fixed(shape):
        return pl.BlockSpec(shape, lambda s: (0, 0, 0, 0))

    args, specs = list(consts), [whole(c) for c in consts]
    if edges:
        at = lambda s: s * last
        for field, (below, above) in zip(fields, edge_halos):
            args += [below, field, field, above]
            specs += [
                fixed(in_layer),
                layer(in_layer, at),
                layer(in_layer, lambda s: 1 + s * (last - 2)),
                fixed(in_layer),
            ]
        steps = 2
    else:
        at = lambda s: s + 1
        for field in fields:
            args += [field, field, field]
            specs += [
                layer(in_layer, lambda s: s),
                layer(in_layer, lambda s: s + 1),
                layer(in_layer, lambda s: s + 2),
            ]
        steps = depth - 2
    for array in local:
        args.append(array)
        specs.append(layer(out_layer, at))
    aliases = {}
    if edges:
        for i, array in enumerate(previous):
            aliases[len(args)] = i
            args.append(array)
            specs.append(pl.BlockSpec(memory_space=pl.ANY))
    out_shape = [jax.ShapeDtypeStruct((depth, HALF, NG, LANES), k) for k in kinds]
    out_specs = [layer(out_layer, at) for _ in kinds]
    if edges:
        for index in sent:
            out_shape += [jax.ShapeDtypeStruct(out_layer, kinds[index])] * 2
            out_specs += [fixed(out_layer)] * 2
    u_rows = NG if rows == NG else HALF + 2
    outs = pl.pallas_call(
        lambda *refs: stage_kernel(stage, edges, len(fields), len(consts), len(local), refs),
        grid=(steps,),
        out_shape=out_shape,
        in_specs=specs,
        out_specs=out_specs,
        scratch_shapes=[pltpu.VMEM((u_rows, NG, LANES), F32) for _ in fields],
        input_output_aliases=aliases,
        compiler_params=params(),
        cost_estimate=cost(steps * 4_000_000_000, steps * 6_000_000),
        name=stage + ("_edges" if edges else "_inner"),
    )(*args)
    full = list(outs[: len(kinds)])
    if not edges:
        return full
    sends = outs[len(kinds) :]
    return full, [(sends[2 * i], sends[2 * i + 1]) for i in range(len(sent))]


def exchange(pairs):
    size = lax.axis_size("slab")
    up = [(i, (i + 1) % size) for i in range(size)]
    down = [(j, i) for i, j in up]
    return [
        (lax.ppermute(high, "slab", up), lax.ppermute(low, "slab", down)) for low, high in pairs
    ]


def gather_kernel(peers, *refs):
    spots, halves = refs[:peers], refs[peers : 2 * peers]
    f_ref = refs[2 * peers]
    outs = refs[2 * peers + 1 : 3 * peers + 1]
    rows_ref = refs[-1]
    count = rows_ref.shape[0]
    unroll = 16
    eye = jnp.where(
        lax.broadcasted_iota(jnp.int32, (LANES, LANES), 0)
        == lax.broadcasted_iota(jnp.int32, (LANES, LANES), 1),
        1.0,
        0.0,
    ).astype(BF16)
    for j in range(peers):

        def pick(i, carry, j=j):
            for t in range(unroll):
                atom = i * unroll + t
                rows_ref[pl.ds(atom, 1), :] = f_ref[pl.ds(spots[j][atom], 1), :]
            return carry

        lax.fori_loop(0, count // unroll, pick, 0)
        for start in range(0, count, 256):
            block = rows_ref[start : start + 256, :].astype(BF16)
            turned = lax.dot_general(
                eye, block, (((1,), (1,)), ((), ())), preferred_element_type=F32
            )
            later = jnp.broadcast_to(halves[j][:, start : start + 256], (CH, 256)) == 1
            outs[j][:, start : start + 256] = jnp.where(later, turned[CH:], turned[:CH]).astype(
                BF16
            )


def make_gather(spots, halves, field):
    peers = len(spots)
    count = spots[0].shape[0]
    return pl.pallas_call(
        functools.partial(gather_kernel, peers),
        out_shape=[jax.ShapeDtypeStruct((CH, count), BF16)] * peers,
        in_specs=[smem()] * peers + [vmem()] * (peers + 1),
        out_specs=[vmem()] * peers,
        scratch_shapes=[pltpu.VMEM((count, LANES), F32)],
        compiler_params=params(),
        name="gather",
    )(*spots, *[h.reshape(1, count) for h in halves], field)


def finish_kernel(peers, me_ref, tab_ref, *refs):
    out_ref = refs[peers]
    me = me_ref[0]
    for j in range(peers):
        k = lax.rem(lax.bitwise_xor(me, j), NT)
        out_ref[k] = refs[j][...].astype(F32) * tab_ref[...]


def make_output(me, tab, returned):
    return pl.pallas_call(
        functools.partial(finish_kernel, len(returned)),
        out_shape=jax.ShapeDtypeStruct((NT,) + tab.shape, F32),
        in_specs=[smem()] + [vmem()] * (len(returned) + 1),
        out_specs=vmem(),
        compiler_params=params(),
        name="finish",
    )(me, tab, *returned)


def swap(array, j):
    if j == 0:
        return array
    size = lax.axis_size("brick")
    return lax.ppermute(array, "brick", [(i, i ^ j) for i in range(size)])


def lane_taps(taps, flip):
    kernel = taps[:, ::-1, :] if flip else taps
    tiled = jnp.concatenate([kernel, kernel], -1).reshape(9, 1, LANES)
    return jnp.broadcast_to(tiled, (9, 8, LANES))


def twice(vector):
    return jnp.concatenate([vector, vector]).reshape(1, LANES)


def shards(
    features,
    tangents,
    route,
    cell_local,
    stencil,
    stencil_table,
    taps1,
    taps2,
    point1,
    point2,
    bias1,
    bias2,
    readout,
):
    bricks = lax.axis_size("brick")
    depth = NG // lax.axis_size("slab")
    width = NG // bricks
    me = lax.axis_index("brick").astype(jnp.int32)
    mine = me.reshape(1)

    z_part = cell_local // (width * NG)
    y_part = route[:, 0] * width + (cell_local // NG) % width
    x_part = cell_local % NG
    cell = (z_part * NG + y_part) * NG + x_part
    cells = [swap(cell, j) for j in range(bricks)]

    tab, *blocks = make_deposits(mine, features, tangents, stencil, stencil_table, bricks)
    chunks = [swap(block, j) for j, block in enumerate(blocks)]
    charge, q_low, q_high = make_charge(cells, chunks, depth)

    zero = jnp.zeros((CH, CH), BF16)
    p1t, p2t = point1.T, point2.T
    mix1 = jnp.block(
        [
            [p1t, zero, zero, zero],
            [zero, zero, p1t, zero],
            [zero, p1t, zero, zero],
            [zero, zero, zero, p1t],
        ]
    )
    eye4 = jnp.eye(4, dtype=BF16)
    mix2 = jnp.kron(eye4, p2t)
    back2 = jnp.kron(eye4, point2)
    back1 = jnp.kron(eye4[:2, :2], point1)
    w1, w2 = lane_taps(taps1, False), lane_taps(taps2, False)
    w1t, w2t = lane_taps(taps1, True), lane_taps(taps2, True)

    def both(stage, consts, fields, local, edges):
        halos = exchange(edges)
        inner = run_stage(stage, depth, consts, fields, local)
        return run_stage(stage, depth, consts, fields, local, halos, inner)

    consts = [w1, mix1, twice(bias1)]
    (h, m, bend, slope), sends = both("first", consts, [charge], [], [(q_low, q_high)])
    consts = [w2, mix2, back2, twice(bias2), twice(readout)]
    (rh, rm), sends = both("second", consts, [h, m], [], sends)
    (y,), sends = both("third", [w2t, back1], [rh, rm], [bend, slope], sends)
    (field,), _ = both("fourth", [w1t], [y], [], sends)

    y_of = [(c // NG) % NG for c in cells[:NT]]
    spots = [
        ((c // (NG * NG)) * HALF + yy % HALF) * NG + c % NG for c, yy in zip(cells[:NT], y_of)
    ]
    halves = [yy // HALF for yy in y_of]
    picked = make_gather(spots, halves, field.reshape(-1, LANES))
    returned = [swap(block, j) for j, block in enumerate(picked)]
    return make_output(mine, tab, returned)


def solution(mesh):
    placed = (
        P(None, ("slab", "brick")),
        P(None, None, ("slab", "brick")),
        P(("slab", "brick"), None),
        P(("slab", "brick")),
        P(("slab", "brick")),
        P(),
        P(),
        P(),
        P(),
        P(),
        P(),
        P(),
        P(),
    )
    return jax.shard_map(
        shards,
        mesh=mesh,
        in_specs=placed,
        out_specs=P(None, None, ("slab", "brick")),
        check_vma=False,
    )
```

time: 793 us -> 264 us (0.33)
  other arithmetic: 250 us -> 11.6 us
  local copies, waits for them, and re-layouts: 210 us -> 16.9 us
  Pallas kernels: 0 us -> 182 us
  waiting for transfers between devices: 175 us -> 19.3 us
  matrix products: 87.7 us -> 0 us
  starting transfers between devices: 60.2 us -> 32.9 us
    pallas_call x0 -> x12, Pallas kernels: none -> 182 us  [the longest x8 121 us: run_stage(): pl.pallas_call(lambda *refs: stage_kernel(stage, edges, len(fields), len(...]
    add x14 -> x1, other arithmetic: 120 us -> 0.62 us  [shards(): (c // (NG * NG) * HALF + yy % HALF) * NG + c % NG]
    ppermute x28 -> x21, waiting for transfers between devices: 126 us -> 19.3 us  [the longest x9 19.3 us: swap(): return lax.ppermute(array, 'brick', [(i, i ^ j) for i in range(size)])]
    slice x25 -> x1, local copies, waits for them, and re-layouts: 104 us -> 0.01 us  [shards(): back1 = jnp.kron(eye4[:2, :2], point1)]
    dot_general x7 -> x0, matrix products: 87.7 us -> none  [the longest x3 53.7 us: mixing_back(): jnp.einsum('co,vczyx->vozyx', point, field, preferred_element_type=jnp.fl...]
    convert_element_type x10 -> x1, other arithmetic: 69.3 us -> 0.01 us  [shards(): eye4 = jnp.eye(4, dtype=BF16)]
    all_to_all x3 -> x0, waiting for transfers between devices: 49.6 us -> none  [the longest x1 29.2 us: shards(): lax.all_to_all(outgoing, 'brick', split_axis=1, concat_axis=1, tiled=True)]
    scatter-add x1 -> x0, other arithmetic: 33.1 us -> none  [shards(): grid.at[:, flat_labels]]
  transfers between devices with their start and end apart: 31 -> 21, of which waited for: 16 -> 3; matrix products, arithmetic and copies ran while one was open for 21% -> 7% of each run, Pallas kernels for 0% -> 33%
where the time goes in v1:
time: 264 us; the launch traced here: 263 us
  Pallas kernels  182 us (69%)
  starting transfers between devices  32.9 us (12%)
  waiting for transfers between devices  19.3 us (7%)
  local copies, waits for them, and re-layouts  16.9 us (6%)
  other arithmetic  11.6 us (4%)
    pallas_call x8, Pallas kernels, run_stage(): pl.pallas_call(lambda *refs: stage_kernel(stage, edges, len(fields), len(...  121 us
    pallas_call x1, Pallas kernels, make_charge(): pl.pallas_call(functools.partial(charge_kernel, peers, depth), grid=(dept...  40.7 us
    ppermute x6, starting transfers between devices, exchange(): lax.ppermute(low, 'slab', down)  20.4 us
    ppermute x9, waiting for transfers between devices, swap(): return lax.ppermute(array, 'brick', [(i, i ^ j) for i in range(size)])  19.3 us
    pallas_call x1, Pallas kernels, make_gather(): pl.pallas_call(functools.partial(gather_kernel, peers), out_shape=[jax.Sh...  14.3 us
    ppermute x9, starting transfers between devices, swap(): return lax.ppermute(array, 'brick', [(i, i ^ j) for i in range(size)])  11.5 us
    unnamed x46, local copies, waits for them, and re-layouts  9.75 us
  transfers between devices with their start and end apart: 21, of which 3 were waited for; matrix products, arithmetic and copies ran while one was open for 7% of the time, Pallas kernels for 33%

profile of v1, /device:TPU:0, one launch (start us, length us, event | category | flops | bytes accessed | tf_op | source)
XLA Modules:
  0.0 263.4 jit_solution(11262611609326628610)
XLA Ops:
  0.7 1.3 add_select_fusion.3
  2.0 2.9 %collective-permute-start = (s32[2048]{0:T(1024)S(1)}, s32[2048]{0:T(1024)S(1)}, u32[]{:S(2)}, u32[]{:S(2)}) collective-permute-start(s32[2048]{0:T(1024)S(1)} %get-tuple-element.76.refs_0_), channel_id=1, source_target_pairs={{0,1},{1,0},{2,3},{3,2},{4,5},{5,4},{6,7},{7,6},{8,9},{9,8},{10,11... | collective-permute-start | bytes 24584 | tf_op jit(solution)/shard_map/ppermute | solution.py:492
  5.0 1.5 collective-permute-start.1
  6.5 1.4 copy.22
  7.9 3.3 %deposits.1 = (f32[64,2048]{1,0:T(8,128)}, bf16[128,2048]{1,0:T(8,128)(2,1)}, bf16[128,2048]{1,0:T(8,128)(2,1)}, bf16[128,2048]{1,0:T(8,128)(2,1)}, bf16[128,2048]{1,0:T(8,128)(2,1)}) custom-call(s32[1]{0:T(128)} %bitcast.me_ref, bf16[64,2048]{1,0:T(8,128)(2,1)} %feat_ref.1, bf16[4,64,2048]{2,1,0:T(8,128)(2,1)} %tan_ref.1, s32[1,2048]{1,0:T(1,128)} %bitcast.26, ...), custom_call_target="tpu_custom_call" | custom-call | tf_op jit(solution)/shard_map/deposits/pallas_call | solution.py:61
  11.2 2.0 collective-permute-start.3
  13.2 1.5 collective-permute-start.4
  20.1 1.0 broadcast_multiply_fusion
  22.8 1.3 maximum_bitcast_fusion
  24.2 1.3 maximum_bitcast_fusion.2.refs_2_
  29.9 11.5 %collective-permute-done.5.refs_7_ = bf16[128,2048]{1,0:T(8,128)(2,1)S(1)} collective-permute-done((bf16[128,2048]{1,0:T(8,128)(2,1)}, bf16[128,2048]{1,0:T(8,128)(2,1)S(1)}, u32[]{:S(2)}, u32[]{:S(2)}) %collective-permute-start.5) | collective-permute-done | bytes 524320 | tf_op jit(solution)/shard_map/ppermute | solution.py:492
  42.2 40.7 %charge.1 = (bf16[8,64,64,128]{3,2,1,0:T(8,128)(2,1)}, bf16[1,64,64,128]{3,2,1,0:T(8,128)(2,1)}, bf16[1,64,64,128]{3,2,1,0:T(8,128)(2,1)}) custom-call(s32[2048]{0:T(1024)} %copy-done.12, s32[2048]{0:T(1024)} %copy-done.13, s32[2048]{0:T(1024)} %copy-done.14, s32[2048]{0:T(1024)} %copy-done.15, bf16[128,2048]{1,0:T(8,128)(2,1)} %get-tuple-element.41.refs_4_, ...), custom_call_target="tpu_custom_call" | custom-call | tf_op jit(solution)/shard_map/charge/pallas_call | solution.py:124
  82.9 3.5 %collective-permute-start.7 = (bf16[1,64,64,128]{3,2,1,0:T(8,128)(2,1)}, bf16[1,64,64,128]{3,2,1,0:T(8,128)(2,1)S(1)}, u32[]{:S(2)}, u32[]{:S(2)}) collective-permute-start(bf16[1,64,64,128]{3,2,1,0:T(8,128)(2,1)} %get-tuple-element.47), channel_id=1, source_target_pairs={{4,0},{8,4},{12,8},{16,12},{20,16},{24,20},{28,24},{0,28},{5,1},{9... | collective-permute-start | bytes 3145736 | tf_op jit(solution)/shard_map/ppermute | solution.py:418
  87.1 21.9 %first_inner.1 = (bf16[8,32,64,128]{3,2,1,0:T(8,128)(2,1)}, bf16[8,32,64,128]{3,2,1,0:T(8,128)(2,1)}, f32[8,32,64,128]{3,2,1,0:T(8,128)}, f32[8,32,64,128]{3,2,1,0:T(8,128)}) custom-call(f32[9,8,128]{2,1,0:T(8,128)} %broadcast_in_dim.48.refs_0_, bf16[256,256]{1,0:T(8,128)(2,1)} %maximum_maximum_fusion.refs_1_, f32[1,128]{1,0:T(1,128)} %maximum_bitcast_fusion.2.refs_2_, ...), custom_call_target="tpu_custom_call" | custom-call | flops 24000000000 | bytes 36000000 | tf_op jit(solution)/shard_map/first_inner/pallas_call | solution.py:394
  109.0 0.9 copy-done
  110.3 10.9 %first_edges.1 = (bf16[8,32,64,128]{3,2,1,0:T(8,128)(2,1)}, bf16[8,32,64,128]{3,2,1,0:T(8,128)(2,1)}, f32[8,32,64,128]{3,2,1,0:T(8,128)}, f32[8,32,64,128]{3,2,1...) custom-call(f32[9,8,128]{2,1,0:T(8,128)} %broadcast_in_dim.48.refs_0, ...), custom_call_target="tpu_custom_call", output_to_operand_aliasing={{0}: (7, {}), {1}: (8, {}), {2}: (9, {}), {3}: (10, {})} | custom-call | flops 8000000000 | bytes 12000000 | tf_op jit(solution)/shard_map/first_edges/pallas_call | solution.py:394
  122.1 2.7 %collective-permute-start.11 = (bf16[1,32,64,128]{3,2,1,0:T(8,128)(2,1)}, bf16[1,32,64,128]{3,2,1,0:T(8,128)(2,1)S(1)}, u32[]{:S(2)}, u32[]{:S(2)}) collective-permute-start(bf16[1,32,64,128]{3,2,1,0:T(8,128)(2,1)} %get-tuple-element.57), channel_id=1, source_target_pairs={{4,0},{8,4},{12,8},{16,12},{20,16},{24,20},{28,24},{0,28},{5,1},{9... | collective-permute-start | bytes 1572872 | tf_op jit(solution)/shard_map/ppermute | solution.py:418
  124.8 3.5 %collective-permute-start.9 = (bf16[1,32,64,128]{3,2,1,0:T(8,128)(2,1)}, bf16[1,32,64,128]{3,2,1,0:T(8,128)(2,1)S(1)}, u32[]{:S(2)}, u32[]{:S(2)}) collective-permute-start(bf16[1,32,64,128]{3,2,1,0:T(8,128)(2,1)} %get-tuple-element.54), channel_id=1, source_target_pairs={{4,0},{8,4},{12,8},{16,12},{20,16},{24,20},{28,24},{0,28},{5,1},{9... | collective-permute-start | bytes 1572872 | tf_op jit(solution)/shard_map/ppermute | solution.py:418
  128.9 28.1 %second_inner.1 = (bf16[8,32,64,128]{3,2,1,0:T(8,128)(2,1)}, bf16[8,32,64,128]{3,2,1,0:T(8,128)(2,1)}) custom-call(f32[9,8,128]{2,1,0:T(8,128)} %broadcast_in_dim.46.refs_0_, bf16[256,256]{1,0:T(8,128)(2,1)} %mul.127.refs_1_, bf16[256,256]{1,0:T(8,128)(2,1)} %mul.130.refs_2_, f32[1,128]{1,0:T(1,128)} %get-tuple-element.85.refs_3_, ...), custom_call_target="tpu_custom_call" | custom-call | flops 24000000000 | bytes 36000000 | tf_op jit(solution)/shard_map/second_inner/pallas_call | solution.py:394
  158.3 12.6 %second_edges.1 = (bf16[8,32,64,128]{3,2,1,0:T(8,128)(2,1)}, bf16[8,32,64,128]{3,2,1,0:T(8,128)(2,1)}, bf16[1,32,64,128]{3,2,1,0:T(8,128)(2,1)}, bf16[1,32,64,12...) custom-call(f32[9,8,128]{2,1,0:T(8,128)} %broadcast_in_dim.46.refs_0, ...), custom_call_target="tpu_custom_call", output_to_operand_aliasing={{0}: (13, {}), {1}: (14, {})} | custom-call | flops 8000000000 | bytes 12000000 | tf_op jit(solution)/shard_map/second_edges/pallas_call | solution.py:394
  171.0 3.5 %collective-permute-start.13 = (bf16[1,32,64,128]{3,2,1,0:T(8,128)(2,1)}, bf16[1,32,64,128]{3,2,1,0:T(8,128)(2,1)S(1)}, u32[]{:S(2)}, u32[]{:S(2)}) collective-permute-start(bf16[1,32,64,128]{3,2,1,0:T(8,128)(2,1)} %get-tuple-element.62), channel_id=1, source_target_pairs={{4,0},{8,4},{12,8},{16,12},{20,16},{24,20},{28,24},{0,28},{5,1},{9... | collective-permute-start | bytes 1572872 | tf_op jit(solution)/shard_map/ppermute | solution.py:418
  174.5 3.5 %collective-permute-start.15 = (bf16[1,32,64,128]{3,2,1,0:T(8,128)(2,1)}, bf16[1,32,64,128]{3,2,1,0:T(8,128)(2,1)S(1)}, u32[]{:S(2)}, u32[]{:S(2)}) collective-permute-start(bf16[1,32,64,128]{3,2,1,0:T(8,128)(2,1)} %get-tuple-element.65), channel_id=1, source_target_pairs={{4,0},{8,4},{12,8},{16,12},{20,16},{24,20},{28,24},{0,28},{5,1},{9... | collective-permute-start | bytes 1572872 | tf_op jit(solution)/shard_map/ppermute | solution.py:418
  178.7 21.9 %third_inner.1.refs_12_ = bf16[8,32,64,128]{3,2,1,0:T(8,128)(2,1)} custom-call(f32[9,8,128]{2,1,0:T(8,128)} %broadcast_in_dim.44.refs_0_, bf16[128,128]{1,0:T(8,128)(2,1)} %mul.123.refs_1_, bf16[8,32,64,128]{3,2,1,0:T(8,128)(2,1)} %get-tuple-element.61.refs_2_.refs_3_.refs_4_, bf16[8,32,64,128]{3,2,1,0:T(8,128)(2,1)} %get-tuple-element.61.refs_2_.refs_3_.refs_4_, ...), custom_call_target="tpu_custom_call" | custom-call | flops 24000000000 | bytes 36000000 | tf_op jit(solution)/shard_map/third_inner/pallas_call | solution.py:394
  202.5 10.4 %third_edges.1 = (bf16[8,32,64,128]{3,2,1,0:T(8,128)(2,1)}, bf16[1,32,64,128]{3,2,1,0:T(8,128)(2,1)}, bf16[1,32,64,128]{3,2,1,0:T(8,128)(2,1)}) custom-call(f32[9,8,128]{2,1,0:T(8,128)} %broadcast_in_dim.44.refs_0_, bf16[128,128]{1,0:T(8,128)(2,1)} %mul.123.refs_1_, bf16[1,32,64,128]{3,2,1,0:T(8,128)(2,1)} %copy-done.2, ...), custom_call_target="tpu_custom_call", output_to_operand_aliasing={{0}: (12, {})} | custom-call | flops 8000000000 | bytes 12000000 | tf_op jit(solution)/shard_map/third_edges/pallas_call | solution.py:394
  213.0 3.5 %collective-permute-start.17 = (bf16[1,32,64,128]{3,2,1,0:T(8,128)(2,1)}, bf16[1,32,64,128]{3,2,1,0:T(8,128)(2,1)S(1)}, u32[]{:S(2)}, u32[]{:S(2)}) collective-permute-start(bf16[1,32,64,128]{3,2,1,0:T(8,128)(2,1)} %get-tuple-element.70), channel_id=1, source_target_pairs={{4,0},{8,4},{12,8},{16,12},{20,16},{24,20},{28,24},{0,28},{5,1},{9... | collective-permute-start | bytes 1572872 | tf_op jit(solution)/shard_map/ppermute | solution.py:418
  217.1 10.6 %fourth_inner.1.refs_5_ = f32[8,32,64,128]{3,2,1,0:T(8,128)} custom-call(f32[9,8,128]{2,1,0:T(8,128)} %broadcast_in_dim.42.refs_0_, bf16[8,32,64,128]{3,2,1,0:T(8,128)(2,1)} %get-tuple-element.69.refs_1_.refs_2_.refs_3_, bf16[8,32,64,128]{3,2,1,0:T(8,128)(2,1)} %get-tuple-element.69.refs_1_.refs_2_.refs_3_, ...), custom_call_target="tpu_custom_call" | custom-call | flops 24000000000 | bytes 36000000 | tf_op jit(solution)/shard_map/fourth_inner/pallas_call | solution.py:394
  229.4 4.8 %fourth_edges.1 = f32[8,32,64,128]{3,2,1,0:T(8,128)} custom-call(f32[9,8,128]{2,1,0:T(8,128)} %broadcast_in_dim.42.refs_0_, bf16[1,32,64,128]{3,2,1,0:T(8,128)(2,1)} %copy-done.20, bf16[8,32,64,128]{3,2,1,0:T(8,128)(2,1)} %get-tuple-element.69.refs_1_.refs_2_.refs_3_, ...), custom_call_target="tpu_custom_call", output_to_operand_aliasing={{}: (5, {})} | custom-call | flops 8000000000 | bytes 12000000 | tf_op jit(solution)/shard_map/fourth_edges/pallas_call | solution.py:394
  234.2 14.3 %gather.1 = (bf16[64,2048]{1,0:T(8,128)(2,1)}, bf16[64,2048]{1,0:T(8,128)(2,1)}, bf16[64,2048]{1,0:T(8,128)(2,1)}, bf16[64,2048]{1,0:T(8,128)(2,1)}) custom-call(s32[2048]{0:T(1024)} %fusion.11.refs_0_, s32[2048]{0:T(1024)} %get-tuple-element.82.refs_1_, s32[2048]{0:T(1024)} %get-tuple-element.80.refs_2_, s32[2048]{0:T(1024)} %get-tuple-element.78.refs_3_, ...), custom_call_target="tpu_custom_call" | custom-call | tf_op jit(solution)/shard_map/gather/pallas_call | solution.py:458
  249.3 2.6 %collective-permute-start.20 = (bf16[64,2048]{1,0:T(8,128)(2,1)}, bf16[64,2048]{1,0:T(8,128)(2,1)S(1)}, u32[]{:S(2)}, u32[]{:S(2)}) collective-permute-start(bf16[64,2048]{1,0:T(8,128)(2,1)} %get-tuple-element.74), channel_id=1, source_target_pairs={{0,3},{1,2},{2,1},{3,0},{4,7},{5,6},{6,5},{7,4},{8,11},{9,10},{10,... | collective-permute-start | bytes 786440 | tf_op jit(solution)/shard_map/ppermute | solution.py:492
  251.9 4.8 %collective-permute-done.18.refs_1_ = bf16[64,2048]{1,0:T(8,128)(2,1)S(1)} collective-permute-done((bf16[64,2048]{1,0:T(8,128)(2,1)}, bf16[64,2048]{1,0:T(8,128)(2,1)S(1)}, u32[]{:S(2)}, u32[]{:S(2)}) %collective-permute-start.18) | collective-permute-done | bytes 262176 | tf_op jit(solution)/shard_map/ppermute | solution.py:492
  256.7 3.1 %collective-permute-done.19.refs_2_ = bf16[64,2048]{1,0:T(8,128)(2,1)S(1)} collective-permute-done((bf16[64,2048]{1,0:T(8,128)(2,1)}, bf16[64,2048]{1,0:T(8,128)(2,1)S(1)}, u32[]{:S(2)}, u32[]{:S(2)}) %collective-permute-start.19) | collective-permute-done | bytes 262176 | tf_op jit(solution)/shard_map/ppermute | solution.py:492
  260.6 2.8 %finish.1 = f32[4,64,2048]{2,1,0:T(8,128)} custom-call(s32[1]{0:T(128)} %bitcast.me_ref, f32[64,2048]{1,0:T(8,128)} %get-tuple-element.40.tab_ref, bf16[64,2048]{1,0:T(8,128)(2,1)} %get-tuple-element.71.refs_0_, bf16[64,2048]{1,0:T(8,128)(2,1)} %copy-done.9, bf16[64,2048]{1,0:T(8,128)(2,1)} %copy-done.10, bf16[64,2048]{1,0:T(8,128)(2,1)} %copy-done.11), custom_call_target="tpu_custom_call" | custom-call | tf_op jit(solution)/shard_map/finish/pallas_call | solution.py:478
  (100 shorter events, 23.2 us)
Async XLA Ops:
  2.0 39.3 %copy-start.12 = (s32[2048]{0:T(1024)}, s32[2048]{0:T(1024)S(1)}, u32[]{:S(2)}) copy-start(s32[2048]{0:T(1024)S(1)} %get-tuple-element.76.refs_0_) | copy-start | bytes 24580
  2.0 25.9 %collective-permute-start = (s32[2048]{0:T(1024)S(1)}, s32[2048]{0:T(1024)S(1)}, u32[]{:S(2)}, u32[]{:S(2)}) collective-permute-start(s32[2048]{0:T(1024)S(1)} %get-tuple-element.76.refs_0_), channel_id=1, source_target_pairs={{0,1},{1,0},{2,3},{3,2},{4,5},{5,4},{6,7},{7,6},{8,9},{9,8},{10,11... | collective-permute-start | bytes 24584 | tf_op jit(solution)/shard_map/ppermute | solution.py:492
  5.0 23.7 %collective-permute-start.1 = (s32[2048]{0:T(1024)S(1)}, s32[2048]{0:T(1024)S(1)}, u32[]{:S(2)}, u32[]{:S(2)}) collective-permute-start(s32[2048]{0:T(1024)S(1)} %get-tuple-element.76.refs_0_), channel_id=1, source_target_pairs={{0,2},{1,3},{2,0},{3,1},{4,6},{5,7},{6,4},{7,5},{8,10},{9,11},{10,... | collective-permute-start | bytes 24584 | tf_op jit(solution)/shard_map/ppermute | solution.py:492
  6.5 22.8 %collective-permute-start.2 = (s32[2048]{0:T(1024)S(1)}, s32[2048]{0:T(1024)S(1)}, u32[]{:S(2)}, u32[]{:S(2)}) collective-permute-start(s32[2048]{0:T(1024)S(1)} %get-tuple-element.76.refs_0_), channel_id=1, source_target_pairs={{0,3},{1,2},{2,1},{3,0},{4,7},{5,6},{6,5},{7,4},{8,11},{9,10},{10,... | collective-permute-start | bytes 24584 | tf_op jit(solution)/shard_map/ppermute | solution.py:492
  11.2 18.7 %collective-permute-start.3 = (bf16[128,2048]{1,0:T(8,128)(2,1)}, bf16[128,2048]{1,0:T(8,128)(2,1)S(1)}, u32[]{:S(2)}, u32[]{:S(2)}) collective-permute-start(bf16[128,2048]{1,0:T(8,128)(2,1)} %get-tuple-element.42), channel_id=1, source_target_pairs={{0,1},{1,0},{2,3},{3,2},{4,5},{5,4},{6,7},{7,6},{8,9},{9,8},{10,11... | collective-permute-start | bytes 1572872 | tf_op jit(solution)/shard_map/ppermute | solution.py:492
  13.2 16.7 %collective-permute-start.4 = (bf16[128,2048]{1,0:T(8,128)(2,1)}, bf16[128,2048]{1,0:T(8,128)(2,1)S(1)}, u32[]{:S(2)}, u32[]{:S(2)}) collective-permute-start(bf16[128,2048]{1,0:T(8,128)(2,1)} %get-tuple-element.43), channel_id=1, source_target_pairs={{0,2},{1,3},{2,0},{3,1},{4,6},{5,7},{6,4},{7,5},{8,10},{9,11},{10,... | collective-permute-start | bytes 1572872 | tf_op jit(solution)/shard_map/ppermute | solution.py:492
  27.9 13.5 %copy-start.13 = (s32[2048]{0:T(1024)}, s32[2048]{0:T(1024)S(1)}, u32[]{:S(2)}) copy-start(s32[2048]{0:T(1024)S(1)} %collective-permute-done.refs_1_) | copy-start | bytes 24580
  27.9 13.4 %collective-permute-start.5 = (bf16[128,2048]{1,0:T(8,128)(2,1)}, bf16[128,2048]{1,0:T(8,128)(2,1)S(1)}, u32[]{:S(2)}, u32[]{:S(2)}) collective-permute-start(bf16[128,2048]{1,0:T(8,128)(2,1)} %get-tuple-element.44), channel_id=1, source_target_pairs={{0,3},{1,2},{2,1},{3,0},{4,7},{5,6},{6,5},{7,4},{8,11},{9,10},{10,... | collective-permute-start | bytes 1572872 | tf_op jit(solution)/shard_map/ppermute | solution.py:492
  28.7 12.7 %copy-start.14 = (s32[2048]{0:T(1024)}, s32[2048]{0:T(1024)S(1)}, u32[]{:S(2)}) copy-start(s32[2048]{0:T(1024)S(1)} %collective-permute-done.1.refs_2_) | copy-start | bytes 24580
  29.3 12.1 %copy-start.15 = (s32[2048]{0:T(1024)}, s32[2048]{0:T(1024)S(1)}, u32[]{:S(2)}) copy-start(s32[2048]{0:T(1024)S(1)} %collective-permute-done.2.refs_3_) | copy-start | bytes 24580
  29.9 11.5 %copy-start.6 = (bf16[128,2048]{1,0:T(8,128)(2,1)}, bf16[128,2048]{1,0:T(8,128)(2,1)S(1)}, u32[]{:S(2)}) copy-start(bf16[128,2048]{1,0:T(8,128)(2,1)S(1)} %collective-permute-done.3.refs_5_) | copy-start | bytes 1572868
  29.9 11.5 %copy-start.7 = (bf16[128,2048]{1,0:T(8,128)(2,1)}, bf16[128,2048]{1,0:T(8,128)(2,1)S(1)}, u32[]{:S(2)}) copy-start(bf16[128,2048]{1,0:T(8,128)(2,1)S(1)} %collective-permute-done.4.refs_6_) | copy-start | bytes 1572868
  82.9 26.1 %collective-permute-start.6 = (bf16[1,64,64,128]{3,2,1,0:T(8,128)(2,1)}, bf16[1,64,64,128]{3,2,1,0:T(8,128)(2,1)S(1)}, u32[]{:S(2)}, u32[]{:S(2)}) collective-permute-start(bf16[1,64,64,128]{3,2,1,0:T(8,128)(2,1)} %get-tuple-element.45), channel_id=1, source_target_pairs={{0,4},{4,8},{8,12},{12,16},{16,20},{20,24},{24,28},{28,0},{1,5},{5... | collective-permute-start | bytes 3145736 | tf_op jit(solution)/shard_map/ppermute | solution.py:418
  82.9 26.1 %collective-permute-start.7 = (bf16[1,64,64,128]{3,2,1,0:T(8,128)(2,1)}, bf16[1,64,64,128]{3,2,1,0:T(8,128)(2,1)S(1)}, u32[]{:S(2)}, u32[]{:S(2)}) collective-permute-start(bf16[1,64,64,128]{3,2,1,0:T(8,128)(2,1)} %get-tuple-element.47), channel_id=1, source_target_pairs={{4,0},{8,4},{12,8},{16,12},{20,16},{24,20},{28,24},{0,28},{5,1},{9... | collective-permute-start | bytes 3145736 | tf_op jit(solution)/shard_map/ppermute | solution.py:418
  109.0 1.3 copy-start.1
  121.2 35.8 %collective-permute-start.10 = (bf16[1,32,64,128]{3,2,1,0:T(8,128)(2,1)}, bf16[1,32,64,128]{3,2,1,0:T(8,128)(2,1)S(1)}, u32[]{:S(2)}, u32[]{:S(2)}) collective-permute-start(bf16[1,32,64,128]{3,2,1,0:T(8,128)(2,1)} %get-tuple-element.55), channel_id=1, source_target_pairs={{0,4},{4,8},{8,12},{12,16},{16,20},{20,24},{24,28},{28,0},{1,5},{5... | collective-permute-start | bytes 1572872 | tf_op jit(solution)/shard_map/ppermute | solution.py:418
  122.1 34.9 %collective-permute-start.11 = (bf16[1,32,64,128]{3,2,1,0:T(8,128)(2,1)}, bf16[1,32,64,128]{3,2,1,0:T(8,128)(2,1)S(1)}, u32[]{:S(2)}, u32[]{:S(2)}) collective-permute-start(bf16[1,32,64,128]{3,2,1,0:T(8,128)(2,1)} %get-tuple-element.57), channel_id=1, source_target_pairs={{4,0},{8,4},{12,8},{16,12},{20,16},{24,20},{28,24},{0,28},{5,1},{9... | collective-permute-start | bytes 1572872 | tf_op jit(solution)/shard_map/ppermute | solution.py:418
  124.8 32.3 %collective-permute-start.8 = (bf16[1,32,64,128]{3,2,1,0:T(8,128)(2,1)}, bf16[1,32,64,128]{3,2,1,0:T(8,128)(2,1)S(1)}, u32[]{:S(2)}, u32[]{:S(2)}) collective-permute-start(bf16[1,32,64,128]{3,2,1,0:T(8,128)(2,1)} %get-tuple-element.52), channel_id=1, source_target_pairs={{0,4},{4,8},{8,12},{12,16},{16,20},{20,24},{24,28},{28,0},{1,5},{5... | collective-permute-start | bytes 1572872 | tf_op jit(solution)/shard_map/ppermute | solution.py:418
  124.8 32.3 %collective-permute-start.9 = (bf16[1,32,64,128]{3,2,1,0:T(8,128)(2,1)}, bf16[1,32,64,128]{3,2,1,0:T(8,128)(2,1)S(1)}, u32[]{:S(2)}, u32[]{:S(2)}) collective-permute-start(bf16[1,32,64,128]{3,2,1,0:T(8,128)(2,1)} %get-tuple-element.54), channel_id=1, source_target_pairs={{4,0},{8,4},{12,8},{16,12},{20,16},{24,20},{28,24},{0,28},{5,1},{9... | collective-permute-start | bytes 1572872 | tf_op jit(solution)/shard_map/ppermute | solution.py:418
  157.0 1.1 copy-start.18
  157.1 1.2 copy-start.19
  170.9 29.7 %collective-permute-start.12 = (bf16[1,32,64,128]{3,2,1,0:T(8,128)(2,1)}, bf16[1,32,64,128]{3,2,1,0:T(8,128)(2,1)S(1)}, u32[]{:S(2)}, u32[]{:S(2)}) collective-permute-start(bf16[1,32,64,128]{3,2,1,0:T(8,128)(2,1)} %get-tuple-element.60), channel_id=1, source_target_pairs={{0,4},{4,8},{8,12},{12,16},{16,20},{20,24},{24,28},{28,0},{1,5},{5... | collective-permute-start | bytes 1572872 | tf_op jit(solution)/shard_map/ppermute | solution.py:418
  171.0 29.6 %collective-permute-start.13 = (bf16[1,32,64,128]{3,2,1,0:T(8,128)(2,1)}, bf16[1,32,64,128]{3,2,1,0:T(8,128)(2,1)S(1)}, u32[]{:S(2)}, u32[]{:S(2)}) collective-permute-start(bf16[1,32,64,128]{3,2,1,0:T(8,128)(2,1)} %get-tuple-element.62), channel_id=1, source_target_pairs={{4,0},{8,4},{12,8},{16,12},{20,16},{24,20},{28,24},{0,28},{5,1},{9... | collective-permute-start | bytes 1572872 | tf_op jit(solution)/shard_map/ppermute | solution.py:418
  174.5 26.1 %collective-permute-start.14 = (bf16[1,32,64,128]{3,2,1,0:T(8,128)(2,1)}, bf16[1,32,64,128]{3,2,1,0:T(8,128)(2,1)S(1)}, u32[]{:S(2)}, u32[]{:S(2)}) collective-permute-start(bf16[1,32,64,128]{3,2,1,0:T(8,128)(2,1)} %get-tuple-element.63), channel_id=1, source_target_pairs={{0,4},{4,8},{8,12},{12,16},{16,20},{20,24},{24,28},{28,0},{1,5},{5... | collective-permute-start | bytes 1572872 | tf_op jit(solution)/shard_map/ppermute | solution.py:418
  174.5 26.1 %collective-permute-start.15 = (bf16[1,32,64,128]{3,2,1,0:T(8,128)(2,1)}, bf16[1,32,64,128]{3,2,1,0:T(8,128)(2,1)S(1)}, u32[]{:S(2)}, u32[]{:S(2)}) collective-permute-start(bf16[1,32,64,128]{3,2,1,0:T(8,128)(2,1)} %get-tuple-element.65), channel_id=1, source_target_pairs={{4,0},{8,4},{12,8},{16,12},{20,16},{24,20},{28,24},{0,28},{5,1},{9... | collective-permute-start | bytes 1572872 | tf_op jit(solution)/shard_map/ppermute | solution.py:418
  200.6 1.1 copy-start.4
  212.9 14.9 %collective-permute-start.16 = (bf16[1,32,64,128]{3,2,1,0:T(8,128)(2,1)}, bf16[1,32,64,128]{3,2,1,0:T(8,128)(2,1)S(1)}, u32[]{:S(2)}, u32[]{:S(2)}) collective-permute-start(bf16[1,32,64,128]{3,2,1,0:T(8,128)(2,1)} %get-tuple-element.68), channel_id=1, source_target_pairs={{0,4},{4,8},{8,12},{12,16},{16,20},{20,24},{24,28},{28,0},{1,5},{5... | collective-permute-start | bytes 1572872 | tf_op jit(solution)/shard_map/ppermute | solution.py:418
  213.0 14.8 %collective-permute-start.17 = (bf16[1,32,64,128]{3,2,1,0:T(8,128)(2,1)}, bf16[1,32,64,128]{3,2,1,0:T(8,128)(2,1)S(1)}, u32[]{:S(2)}, u32[]{:S(2)}) collective-permute-start(bf16[1,32,64,128]{3,2,1,0:T(8,128)(2,1)} %get-tuple-element.70), channel_id=1, source_target_pairs={{4,0},{8,4},{12,8},{16,12},{20,16},{24,20},{28,24},{0,28},{5,1},{9... | collective-permute-start | bytes 1572872 | tf_op jit(solution)/shard_map/ppermute | solution.py:418
  248.4 8.3 %collective-permute-start.18 = (bf16[64,2048]{1,0:T(8,128)(2,1)}, bf16[64,2048]{1,0:T(8,128)(2,1)S(1)}, u32[]{:S(2)}, u32[]{:S(2)}) collective-permute-start(bf16[64,2048]{1,0:T(8,128)(2,1)} %get-tuple-element.72), channel_id=1, source_target_pairs={{0,1},{1,0},{2,3},{3,2},{4,5},{5,4},{6,7},{7,6},{8,9},{9,8},{10,11... | collective-permute-start | bytes 786440 | tf_op jit(solution)/shard_map/ppermute | solution.py:492
  249.0 10.8 %collective-permute-start.19 = (bf16[64,2048]{1,0:T(8,128)(2,1)}, bf16[64,2048]{1,0:T(8,128)(2,1)S(1)}, u32[]{:S(2)}, u32[]{:S(2)}) collective-permute-start(bf16[64,2048]{1,0:T(8,128)(2,1)} %get-tuple-element.73), channel_id=1, source_target_pairs={{0,2},{1,3},{2,0},{3,1},{4,6},{5,7},{6,4},{7,5},{8,10},{9,11},{10,... | collective-permute-start | bytes 786440 | tf_op jit(solution)/shard_map/ppermute | solution.py:492
  249.3 10.5 %collective-permute-start.20 = (bf16[64,2048]{1,0:T(8,128)(2,1)}, bf16[64,2048]{1,0:T(8,128)(2,1)S(1)}, u32[]{:S(2)}, u32[]{:S(2)}) collective-permute-start(bf16[64,2048]{1,0:T(8,128)(2,1)} %get-tuple-element.74), channel_id=1, source_target_pairs={{0,3},{1,2},{2,1},{3,0},{4,7},{5,6},{6,5},{7,4},{8,11},{9,10},{10,... | collective-permute-start | bytes 786440 | tf_op jit(solution)/shard_map/ppermute | solution.py:492
  256.7 3.1 %copy-start.9 = (bf16[64,2048]{1,0:T(8,128)(2,1)}, bf16[64,2048]{1,0:T(8,128)(2,1)S(1)}, u32[]{:S(2)}) copy-start(bf16[64,2048]{1,0:T(8,128)(2,1)S(1)} %collective-permute-done.18.refs_1_) | copy-start | bytes 786436
  (11 other events, 9.2 us)

commit v2 on v0

v2 whole, which is shorter than its diff:
```python
import functools

import jax
import jax.numpy as jnp
from jax import lax
from jax.experimental import pallas as pl
from jax.experimental.pallas import tpu as pltpu
from jax.sharding import PartitionSpec as P

NG = 64
CH = 64
NT = 4
KSETS = 8
LANES = 2 * CH
HALF = NG // 2
GROUP = 4
RUN = 8
BLOCK = 256
MIB = 1024 * 1024
F32 = jnp.float32
BF16 = jnp.bfloat16


def params(mib):
    return pltpu.CompilerParams(vmem_limit_bytes=mib * MIB)


def cost(flops, nbytes):
    return pl.CostEstimate(flops=flops, bytes_accessed=nbytes, transcendentals=0)


def vmem():
    return pl.BlockSpec(memory_space=pltpu.VMEM)


def smem():
    return pl.BlockSpec(memory_space=pltpu.SMEM)


def deposits_kernel(peers, me_ref, feat_ref, tan_ref, sten_ref, table_ref, tab_ref, *outs):
    me = me_ref[0]
    count = feat_ref.shape[1]
    step = min(256, count)
    table = table_ref[...].T
    columns = [table[:, s : s + 1] for s in range(KSETS)]
    for start in range(0, count, step):
        at = pl.ds(start, step)
        kinds = jnp.broadcast_to(sten_ref[:, at], (CH, step))
        tab = jnp.zeros((CH, step), F32)
        for s in range(KSETS):
            tab = jnp.where(kinds == s, columns[s], tab)
        tab_ref[:, at] = tab
        first = (feat_ref[:, at].astype(F32) * tab).astype(BF16)
        for j in range(peers):
            outs[j][:CH, at] = first
            own = tan_ref[lax.rem(lax.bitwise_xor(me, j), NT), :, at]
            outs[j][CH:, at] = (own.astype(F32) * tab).astype(BF16)


def make_deposits(me, features, tangents, stencil, table, peers):
    count = features.shape[1]
    out_shape = [jax.ShapeDtypeStruct((CH, count), F32)]
    out_shape += [jax.ShapeDtypeStruct((LANES, count), BF16)] * peers
    return pl.pallas_call(
        functools.partial(deposits_kernel, peers),
        out_shape=out_shape,
        in_specs=[smem()] + [vmem()] * 4,
        out_specs=[vmem()] * (peers + 1),
        compiler_params=params(8),
        name="deposits",
    )(me, features, tangents, stencil.reshape(1, count), table)


def charge_kernel(peers, *refs):
    cells, chunks = refs[:peers], refs[peers : 2 * peers]
    marks = refs[2 * peers : 3 * peers]
    low_ref, mid_ref, high_ref, one_ref, two_ref, rows_ref, early_ref = refs[3 * peers :]
    count = rows_ref.shape[0]
    width = early_ref.shape[0]
    middle = count // 2

    def clear(i, carry):
        at = pl.ds(pl.multiple_of(i * 256, 256), 256)
        one_ref[at, :] = jnp.zeros((256, LANES), F32)
        two_ref[at, :] = jnp.zeros((256, LANES), F32)
        return carry

    lax.fori_loop(0, one_ref.shape[0] // 256, clear, 0)
    row = lax.broadcasted_iota(jnp.int32, (width, width), 0)
    column = lax.broadcasted_iota(jnp.int32, (width, width), 1)
    early = (column <= row) & (row // RUN == column // RUN)
    early_ref[...] = jnp.where(early, 1.0, 0.0)
    for j in range(peers):

        def turn(i, carry, j=j):
            at = pl.ds(pl.multiple_of(i * width, width), width)
            here = jnp.broadcast_to(marks[j][:, at].astype(F32), (width, width))
            taken = jnp.where(here.T == here, early_ref[...], 0.0).astype(BF16)
            rows_ref[at, :] = lax.dot_general(
                taken, chunks[j][:, at], (((1,), (1,)), ((), ())), preferred_element_type=F32
            )
            return carry

        lax.fori_loop(0, count // width, turn, 0)

        def add(i, carry, j=j):
            for group in range(2):
                at = (i * 2 + group) * RUN
                firsts = ((one_ref, at), (two_ref, middle + at))
                where = [[cells[j][first + t] for t in range(RUN)] for _, first in firsts]
                sums = [
                    [
                        ref[pl.ds(cell, 1), :] + rows_ref[pl.ds(first + t, 1), :]
                        for t, cell in enumerate(spots)
                    ]
                    for (ref, first), spots in zip(firsts, where)
                ]
                for (ref, _), spots, values in zip(firsts, where, sums):
                    for cell, value in zip(spots, values):
                        ref[pl.ds(cell, 1), :] = value
            return carry

        lax.fori_loop(0, middle // (2 * RUN), add, 0)

    def finish(base, out_ref, index):
        def body(y, carry):
            at = pl.ds(pl.multiple_of(base + y * NG, NG), NG)
            out_ref[index, y] = (one_ref[at, :] + two_ref[at, :]).astype(BF16)
            return carry

        lax.fori_loop(0, NG, body, 0, unroll=4)

    inner = mid_ref.shape[0]
    finish(0, low_ref, 0)
    finish((inner + 1) * NG * NG, high_ref, 0)

    def between(z, carry):
        finish((z + 1) * NG * NG, mid_ref, z)
        return carry

    lax.fori_loop(0, inner, between, 0)


def make_charge(cells, chunks, depth):
    peers = len(chunks)
    count = chunks[0].shape[1]
    width = min(BLOCK, count)
    layers = [
        jax.ShapeDtypeStruct((n, NG, NG, LANES), BF16) for n in (1, depth - 2, 1)
    ]
    slab = pltpu.VMEM((depth * NG * NG, LANES), F32)
    return pl.pallas_call(
        functools.partial(charge_kernel, peers),
        out_shape=layers,
        in_specs=[smem()] * peers + [vmem()] * (2 * peers),
        out_specs=[vmem()] * 3,
        scratch_shapes=[
            slab,
            slab,
            pltpu.VMEM((count, LANES), F32),
            pltpu.VMEM((width, width), F32),
        ],
        compiler_params=params(40),
        name="charge",
    )(*cells, *chunks, *[c.reshape(1, count) for c in cells])


ROW_BIAS1, ROW_BIAS2, ROW_SCALE, ROW_HALF = 18, 19, 20, 21


def weights_kernel(p1_ref, p2_ref, t1_ref, t2_ref, b1_ref, b2_ref, r_ref, *outs):
    mix1_ref, mix2_ref, back2_ref, back1_ref, lanes_ref = outs
    p1, p2 = p1_ref[...].astype(F32), p2_ref[...].astype(F32)
    p1t, p2t = 0.5 * p1.T, 0.5 * p2.T
    zero = jnp.zeros((CH, CH), F32)

    def fill(ref, block, order):
        for i, place in enumerate(order):
            parts = [block if j == place else zero for j in range(len(order))]
            ref[i * CH : (i + 1) * CH, :] = jnp.concatenate(parts, 1).astype(BF16)

    fill(mix1_ref, p1t, (0, 2, 1, 3))
    fill(mix2_ref, p2t, (0, 1, 2, 3))
    fill(back2_ref, p2, (0, 1, 2, 3))
    fill(back1_ref, p1, (0, 1))

    def put(row, value):
        lanes_ref[row : row + 1, :] = jnp.concatenate([value, value], 1)

    for axis in range(3):
        for t in range(3):
            put(3 * axis + t, t1_ref[axis, t : t + 1, :])
            put(9 + 3 * axis + t, t2_ref[axis, t : t + 1, :])
    for t in range(3):
        put(ROW_HALF + t, 0.5 * t2_ref[2, t : t + 1, :])
    put(ROW_BIAS1, 0.5 * b1_ref[...])
    put(ROW_BIAS2, 0.5 * b2_ref[...])
    put(ROW_SCALE, r_ref[...])


def make_weights(point1, point2, taps1, taps2, bias1, bias2, readout):
    wide = jax.ShapeDtypeStruct((2 * LANES, 2 * LANES), BF16)
    return pl.pallas_call(
        weights_kernel,
        out_shape=[
            wide,
            wide,
            wide,
            jax.ShapeDtypeStruct((LANES, LANES), BF16),
            jax.ShapeDtypeStruct((24, LANES), F32),
        ],
        in_specs=[vmem()] * 7,
        out_specs=[vmem()] * 5,
        compiler_params=params(4),
        name="weights",
    )(point1, point2, taps1, taps2, *[v.reshape(1, CH) for v in (bias1, bias2, readout)])


def spread(weights, value):
    rows = value.shape[0]
    return (value.reshape(rows // 8, 8, LANES) * weights[None]).reshape(rows, LANES)


def lane_row(w_ref, row):
    return jnp.broadcast_to(w_ref[row : row + 1, :], (8, LANES))


def taps_of(w_ref, start, flip):
    order = (2, 1, 0) if flip else (0, 1, 2)
    return [lane_row(w_ref, start + t) for t in order]


def weigh(w, low, mid, high):
    return spread(w[0], low) + spread(w[1], mid) + spread(w[2], high)


def along_z(w, around, u_ref, rows, offset):
    def body(y, carry):
        low, mid, high = (ref[index, y].astype(F32) for ref, index in around)
        u_ref[y + offset] = weigh(w, low, mid, high)
        return carry

    lax.fori_loop(0, rows, body, 0, unroll=2)


def keep_layer(new, slot, ring_ref, rows):
    ref, index = new

    def body(y, carry):
        ring_ref[slot, y] = ref[index, y].astype(F32)
        return carry

    lax.fori_loop(0, rows, body, 0, unroll=2)


def along_z_ring(w, new, step, ring_ref, u_ref, rows, offset):
    ref, index = new
    low, mid, high = (lax.rem(jnp.int32(step + t), jnp.int32(3)) for t in (1, 2, 0))

    def body(y, carry):
        last = ref[index, y].astype(F32)
        ring_ref[high, y] = last
        u_ref[y + offset] = weigh(w, ring_ref[low, y], ring_ref[mid, y], last)
        return carry

    lax.fori_loop(0, rows, body, 0, unroll=2)


def wrap_halves(u_ref):
    u_ref[0] = pltpu.roll(u_ref[HALF], CH, 1)
    u_ref[HALF + 1] = pltpu.roll(u_ref[1], CH, 1)


def along_y(wy, u_ref, before, here, after):
    return weigh(wy, u_ref[before], u_ref[here], u_ref[after])


def along_x(wx, value, v_ref, slot):
    v_ref[slot, 8 : 8 + NG] = value
    v_ref[slot, 7:8] = value[NG - 1 :]
    v_ref[slot, 8 + NG : 9 + NG] = value[:1]
    return weigh(wx, v_ref[slot, 7 : 7 + NG], value, v_ref[slot, 9 : 9 + NG])


def silu_terms(half):
    t = jnp.tanh(half)
    product = half * t
    bump = 1.0 - t * t
    return half + product, (1.0 + t) + half * bump, bump * (1.0 - product)


def first_stage(refs, u_refs, v_ref, outs, at):
    w_ref, mix_ref = refs
    (u_ref,) = u_refs
    h_ref, m_ref, a_ref, b_ref = outs
    wy, wx = taps_of(w_ref, 3, False), taps_of(w_ref, 6, False)
    bias = w_ref[ROW_BIAS1 : ROW_BIAS1 + 1, :]

    def body(i, carry):
        rows = []
        for t in range(GROUP):
            y = i * GROUP + t
            z = y + HALF
            top = along_y(wy, u_ref, jnp.bitwise_and(y + NG - 1, NG - 1), y, y + 1)
            end = along_y(wy, u_ref, z - 1, z, jnp.bitwise_and(z + 1, NG - 1))
            top = along_x(wx, top, v_ref, 2 * t).astype(BF16)
            end = along_x(wx, end, v_ref, 2 * t + 1).astype(BF16)
            rows.append(jnp.concatenate([top, end], 1))
        mixed = jnp.dot(jnp.concatenate(rows, 0), mix_ref[...], preferred_element_type=F32)
        for t in range(GROUP):
            y = i * GROUP + t
            part = mixed[t * NG : (t + 1) * NG]
            tangent = part[:, LANES:]
            value, slope, curve = silu_terms(part[:, :LANES] + bias)
            h_ref[at, y] = value.astype(BF16)
            m_ref[at, y] = (slope * tangent).astype(BF16)
            a_ref[at, y] = (curve * tangent).astype(a_ref.dtype)
            b_ref[at, y] = slope.astype(b_ref.dtype)
        return carry

    lax.fori_loop(0, HALF // GROUP, body, 0)


def second_stage(refs, u_refs, v_ref, outs, at):
    w_ref, mix_ref, back_ref = refs
    uh_ref, um_ref = u_refs
    rh_ref, rm_ref = outs
    wy, wx = taps_of(w_ref, 12, False), taps_of(w_ref, 15, False)
    bias = w_ref[ROW_BIAS2 : ROW_BIAS2 + 1, :]
    scale = w_ref[ROW_SCALE : ROW_SCALE + 1, :]

    def body(i, carry):
        rows = []
        for t in range(GROUP):
            y = i * GROUP + t
            sh = along_x(wx, along_y(wy, uh_ref, y, y + 1, y + 2), v_ref, 2 * t).astype(BF16)
            sm = along_x(wx, along_y(wy, um_ref, y, y + 1, y + 2), v_ref, 2 * t + 1).astype(BF16)
            rows.append(jnp.concatenate([sh, sm], 1))
        mixed = jnp.dot(jnp.concatenate(rows, 0), mix_ref[...], preferred_element_type=F32)
        _, slope, curve = silu_terms(mixed[:, :LANES] + bias)
        grad = slope * (0.5 * scale)
        bend = curve * scale * mixed[:, LANES:]
        both = jnp.concatenate([grad.astype(BF16), bend.astype(BF16)], 1)
        back = jnp.dot(both, back_ref[...], preferred_element_type=F32).astype(BF16)
        for t in range(GROUP):
            y = i * GROUP + t
            rh_ref[at, y] = back[t * NG : (t + 1) * NG, :LANES]
            rm_ref[at, y] = back[t * NG : (t + 1) * NG, LANES:]
        return carry

    lax.fori_loop(0, HALF // GROUP, body, 0)


def third_stage(refs, u_refs, v_ref, outs, at):
    w_ref, back_ref, a_ref, b_ref = refs
    uh_ref, um_ref = u_refs
    (y_ref,) = outs
    wy, wx = taps_of(w_ref, 12, True), taps_of(w_ref, 15, True)
    wx_half = taps_of(w_ref, ROW_HALF, True)

    def body(i, carry):
        rows = []
        for t in range(GROUP):
            y = i * GROUP + t
            g = along_x(wx, along_y(wy, uh_ref, y, y + 1, y + 2), v_ref, 2 * t)
            dg = along_x(wx_half, along_y(wy, um_ref, y, y + 1, y + 2), v_ref, 2 * t + 1)
            term = a_ref[at, y].astype(F32) * g + b_ref[at, y].astype(F32) * dg
            rows.append(term.astype(BF16))
        back = jnp.dot(jnp.concatenate(rows, 0), back_ref[...], preferred_element_type=F32)
        for t in range(GROUP):
            y_ref[at, i * GROUP + t] = back[t * NG : (t + 1) * NG].astype(BF16)
        return carry

    lax.fori_loop(0, HALF // GROUP, body, 0)


def fourth_rows(w_ref, u_ref, v_ref, put):
    wy, wx = taps_of(w_ref, 3, True), taps_of(w_ref, 6, True)

    def body(i, carry):
        for t in range(GROUP):
            y = i * GROUP + t
            out = along_x(wx, along_y(wy, u_ref, y, y + 1, y + 2), v_ref, t)
            put(y, out.astype(BF16).astype(F32))
        return carry

    lax.fori_loop(0, HALF // GROUP, body, 0)


def fourth_stage(refs, u_refs, v_ref, outs, at):
    def put(y, row):
        outs[0][at, y] = row

    fourth_rows(refs[0], u_refs[0], v_ref, put)


STAGES = {
    "first": (first_stage, NG, (BF16, BF16, F32, F32), (0, 1), (0, False)),
    "second": (second_stage, HALF, (BF16, BF16), (0, 1), (9, False)),
    "third": (third_stage, HALF, (BF16,), (0,), (9, True)),
    "fourth": (fourth_stage, HALF, (F32,), (), (0, True)),
}


def taker(refs):
    left = list(refs)

    def take(n):
        got = left[:n]
        del left[:n]
        return got

    return take


def inner_kernel(stage, n_const, n_field, n_local, *refs):
    body, rows, kinds, _, (start, flip) = STAGES[stage]
    take = taker(refs)
    consts = take(n_const)
    fields = [take(3) for _ in range(n_field)]
    local, outs = take(n_local), take(len(kinds))
    u_refs, ring_refs = take(n_field), take(n_field)
    (v_ref,) = take(1)
    offset = 0 if rows == NG else 1
    wz = taps_of(consts[0], start, flip)
    inner = fields[0][1].shape[0]

    def layer(step, which, index):
        for field, u_ref, ring_ref in zip(fields, u_refs, ring_refs):
            along_z_ring(wz, (field[which], index), step, ring_ref, u_ref, rows, offset)
            if offset:
                wrap_halves(u_ref)
        body(consts + local, u_refs, v_ref, outs, step - 2)

    def loop(step, carry):
        layer(step, 1, step - 1)
        return carry

    for (low_ref, mid_ref, _), ring_ref in zip(fields, ring_refs):
        keep_layer((low_ref, 0), 0, ring_ref, rows)
        keep_layer((mid_ref, 0), 1, ring_ref, rows)
    lax.fori_loop(2, inner + 1, loop, 0)
    layer(inner + 1, 2, 0)


def edge_kernel(stage, n_const, n_field, n_local, places, *refs):
    body, rows, kinds, _, (start, flip) = STAGES[stage]
    take = taker(refs)
    consts = take(n_const)
    fields = [take(3) for _ in range(n_field)]
    local, outs, u_refs = take(n_local), take(len(kinds)), take(n_field)
    (v_ref,) = take(1)
    offset = 0 if rows == NG else 1
    wz = taps_of(consts[0], start, flip)
    for field, u_ref in zip(fields, u_refs):
        along_z(wz, list(zip(field, places)), u_ref, rows, offset)
        if offset:
            wrap_halves(u_ref)
    body(consts + local, u_refs, v_ref, outs, 0)


def field_scratch(stage, n_field, ring):
    rows = STAGES[stage][1]
    u_rows = NG if rows == NG else HALF + 2
    scratch = [pltpu.VMEM((u_rows, NG, LANES), F32)] * n_field
    if ring:
        scratch += [pltpu.VMEM((3, rows, NG, LANES), F32)] * n_field
    return scratch + [pltpu.VMEM((2 * GROUP, NG + 16, LANES), F32)]


def call_stage(kernel, name, layers, mib, kinds, args, scratch):
    return pl.pallas_call(
        kernel,
        out_shape=[jax.ShapeDtypeStruct((layers, HALF, NG, LANES), k) for k in kinds],
        in_specs=[vmem()] * len(args),
        out_specs=[vmem()] * len(kinds),
        scratch_shapes=scratch,
        compiler_params=params(mib),
        cost_estimate=cost(layers * 4_000_000_000, layers * 6_000_000),
        name=name,
    )(*args)


def run_inner(stage, consts, fields, local):
    kernel = functools.partial(inner_kernel, stage, len(consts), len(fields), len(local))
    args = [*consts, *[ref for field in fields for ref in field], *[x[1] for x in local]]
    scratch = field_scratch(stage, len(fields), True)
    layers = fields[0][1].shape[0]
    return call_stage(kernel, stage + "_inner", layers, 16, STAGES[stage][2], args, scratch)


def run_edge(stage, consts, fields, local, halos, side):
    inner = fields[0][1].shape[0]
    around, places = [], (0, 0, 0) if side == 0 else (inner - 1, 0, 0)
    for (low, mid, high), (below, above) in zip(fields, halos):
        around += [below, low, mid] if side == 0 else [mid, high, above]
    kernel = functools.partial(
        edge_kernel, stage, len(consts), len(fields), len(local), places
    )
    args = [*consts, *around, *[x[2 * side] for x in local]]
    scratch = field_scratch(stage, len(fields), False)
    name = stage + ("_low", "_high")[side]
    return call_stage(kernel, name, 1, 8, STAGES[stage][2], args, scratch)


def exchange(fields):
    size = lax.axis_size("slab")
    up = [(i, (i + 1) % size) for i in range(size)]
    down = [(j, i) for i, j in up]
    return [
        (lax.ppermute(high, "slab", up), lax.ppermute(low, "slab", down))
        for low, _, high in fields
    ]


def gather_kernel(peers, depth, *refs):
    spots, halves = refs[:peers], refs[peers : 2 * peers]
    w_ref, below_ref, low_ref, mid_ref, high_ref, above_ref, inner_ref = refs[
        2 * peers : 2 * peers + 7
    ]
    outs = refs[2 * peers + 7 : 3 * peers + 7]
    f_ref, rows_ref, u_ref, v_ref, sem = refs[3 * peers + 7 :]
    count = rows_ref.shape[0]
    unroll = 16
    layer = HALF * NG
    fetch = pltpu.make_async_copy(inner_ref, f_ref.at[pl.ds(layer, (depth - 2) * layer)], sem)
    fetch.start()
    wz = taps_of(w_ref, 0, True)
    for base, around in (
        (0, ((below_ref, 0), (low_ref, 0), (mid_ref, 0))),
        ((depth - 1) * layer, ((mid_ref, depth - 3), (high_ref, 0), (above_ref, 0))),
    ):
        along_z(wz, around, u_ref, HALF, 1)
        wrap_halves(u_ref)

        def put(y, row, base=base):
            f_ref[pl.ds(pl.multiple_of(base + y * NG, NG), NG), :] = row

        fourth_rows(w_ref, u_ref, v_ref, put)
    fetch.wait()
    eye = jnp.where(
        lax.broadcasted_iota(jnp.int32, (LANES, LANES), 0)
        == lax.broadcasted_iota(jnp.int32, (LANES, LANES), 1),
        1.0,
        0.0,
    ).astype(BF16)
    width = min(256, count)
    for j in range(peers):

        def pick(i, carry, j=j):
            for t in range(unroll):
                atom = i * unroll + t
                rows_ref[pl.ds(atom, 1), :] = f_ref[pl.ds(spots[j][atom], 1), :]
            return carry

        lax.fori_loop(0, count // unroll, pick, 0)
        for start in range(0, count, width):
            at = slice(start, start + width)
            turned = lax.dot_general(
                eye,
                rows_ref[at, :].astype(BF16),
                (((1,), (1,)), ((), ())),
                preferred_element_type=F32,
            )
            later = jnp.broadcast_to(halves[j][:, at], (CH, width)) == 1
            outs[j][:, at] = jnp.where(later, turned[CH:], turned[:CH]).astype(BF16)


def make_gather(spots, halves, taps, y, halos, inner):
    peers = len(spots)
    count = spots[0].shape[0]
    low, mid, high = y
    below, above = halos
    depth = mid.shape[0] + 2
    return pl.pallas_call(
        functools.partial(gather_kernel, peers, depth),
        out_shape=[jax.ShapeDtypeStruct((CH, count), BF16)] * peers,
        in_specs=[smem()] * peers
        + [vmem()] * (peers + 6)
        + [pl.BlockSpec(memory_space=pl.ANY)],
        out_specs=[vmem()] * peers,
        scratch_shapes=[
            pltpu.VMEM((depth * HALF * NG, LANES), F32),
            pltpu.VMEM((count, LANES), F32),
            pltpu.VMEM((HALF + 2, NG, LANES), F32),
            pltpu.VMEM((2 * GROUP, NG + 16, LANES), F32),
            pltpu.SemaphoreType.DMA,
        ],
        compiler_params=params(16),
        name="gather",
    )(
        *spots,
        *[h.reshape(1, count) for h in halves],
        taps,
        below,
        low,
        mid,
        high,
        above,
        inner.reshape(-1, LANES),
    )


def finish_kernel(peers, me_ref, tab_ref, *refs):
    out_ref = refs[peers]
    me = me_ref[0]
    for j in range(peers):
        k = lax.rem(lax.bitwise_xor(me, j), NT)
        out_ref[k] = refs[j][...].astype(F32) * tab_ref[...]


def make_output(me, tab, returned):
    return pl.pallas_call(
        functools.partial(finish_kernel, len(returned)),
        out_shape=jax.ShapeDtypeStruct((NT,) + tab.shape, F32),
        in_specs=[smem()] + [vmem()] * (len(returned) + 1),
        out_specs=vmem(),
        compiler_params=params(8),
        name="finish",
    )(me, tab, *returned)


def swap(array, j):
    if j == 0:
        return array
    size = lax.axis_size("brick")
    return lax.ppermute(array, "brick", [(i, i ^ j) for i in range(size)])


def shards(
    features,
    tangents,
    route,
    cell_local,
    stencil,
    stencil_table,
    taps1,
    taps2,
    point1,
    point2,
    bias1,
    bias2,
    readout,
):
    bricks = lax.axis_size("brick")
    depth = NG // lax.axis_size("slab")
    width = NG // bricks
    me = lax.axis_index("brick").astype(jnp.int32)
    mine = me.reshape(1)

    tab, *blocks = make_deposits(mine, features, tangents, stencil, stencil_table, bricks)
    blocks, route, cell_local = lax.optimization_barrier((blocks, route, cell_local))
    chunks = [swap(block, j) for j, block in enumerate(blocks)]
    z_part = cell_local // (width * NG)
    y_part = route[:, 0] * width + (cell_local // NG) % width
    x_part = cell_local % NG
    cell = (z_part * NG + y_part) * NG + x_part
    cells = []
    for j in range(bricks):
        if j >= 3:
            cells[1], cell = lax.optimization_barrier((cells[1], cell))
        cells.append(swap(cell, j))
    charge = make_charge(cells, chunks, depth)

    mix1, mix2, back2, back1, lanes = make_weights(
        point1, point2, taps1, taps2, bias1, bias2, readout
    )

    def both(stage, consts, fields, local, halos):
        middle = run_inner(stage, consts, fields, local)
        lows = run_edge(stage, consts, fields, local, halos, 0)
        highs = run_edge(stage, consts, fields, local, halos, 1)
        return list(zip(lows, middle, highs))

    h, m, bend, slope = both("first", [lanes, mix1], [charge], [], exchange([charge]))
    rh, rm = both("second", [lanes, mix2, back2], [h, m], [], exchange([h, m]))
    (y,) = both("third", [lanes, back1], [rh, rm], [bend, slope], exchange([rh, rm]))
    ((below, above),) = exchange([y])
    (inner,) = run_inner("fourth", [lanes], [y], [])

    y_of = [(c // NG) % NG for c in cells[:NT]]
    spots = [
        ((c // (NG * NG)) * HALF + yy % HALF) * NG + c % NG for c, yy in zip(cells[:NT], y_of)
    ]
    halves = [yy // HALF for yy in y_of]
    picked = make_gather(spots, halves, lanes, y, (below, above), inner)
    returned = [swap(block, j) for j, block in enumerate(picked)]
    return make_output(mine, tab, returned)


def solution(mesh):
    placed = (
        P(None, ("slab", "brick")),
        P(None, None, ("slab", "brick")),
        P(("slab", "brick"), None),
        P(("slab", "brick")),
        P(("slab", "brick")),
        P(),
        P(),
        P(),
        P(),
        P(),
        P(),
        P(),
        P(),
    )
    return jax.shard_map(
        shards,
        mesh=mesh,
        in_specs=placed,
        out_specs=P(None, None, ("slab", "brick")),
        check_vma=False,
    )
```

time: 793 us -> 195 us (0.25)
  other arithmetic: 250 us -> 1.56 us
  local copies, waits for them, and re-layouts: 210 us -> 11 us
  waiting for transfers between devices: 175 us -> 28 us
  Pallas kernels: 0 us -> 125 us
  matrix products: 87.7 us -> 0 us
  starting transfers between devices: 60.2 us -> 27.3 us
    pallas_call x0 -> x15, Pallas kernels: none -> 125 us  [the longest x10 86.2 us: call_stage(): pl.pallas_call(kernel, out_shape=[jax.ShapeDtypeStruct((layers, HALF, NG,...]
    add x14 -> x1, other arithmetic: 120 us -> 0.03 us  [shards(): (c // (NG * NG) * HALF + yy % HALF) * NG + c % NG]
    slice x25 -> x0, local copies, waits for them, and re-layouts: 104 us -> none  [the longest x14 77.7 us: sweep(): jnp.roll(across, -1, 4)]
    ppermute x28 -> x21, waiting for transfers between devices: 126 us -> 28 us  [the longest x9 26.5 us: swap(): return lax.ppermute(array, 'brick', [(i, i ^ j) for i in range(size)])]
    dot_general x7 -> x0, matrix products: 87.7 us -> none  [the longest x3 53.7 us: mixing_back(): jnp.einsum('co,vczyx->vozyx', point, field, preferred_element_type=jnp.fl...]
    convert_element_type x10 -> x0, other arithmetic: 69.3 us -> none  [the longest x7 35.7 us: depth(): return sweep(padded.astype(jnp.float32), taps, flip)]
    all_to_all x3 -> x0, waiting for transfers between devices: 49.6 us -> none  [the longest x1 29.2 us: shards(): lax.all_to_all(outgoing, 'brick', split_axis=1, concat_axis=1, tiled=True)]
    scatter-add x1 -> x0, other arithmetic: 33.1 us -> none  [shards(): grid.at[:, flat_labels]]
  transfers between devices with their start and end apart: 31 -> 21, of which waited for: 16 -> 7; matrix products, arithmetic and copies ran while one was open for 21% -> 0% of each run, Pallas kernels for 0% -> 45%
where the time goes in v2:
time: 195 us; the launch traced here: 193 us
  Pallas kernels  125 us (64%)
  waiting for transfers between devices  28 us (14%)
  starting transfers between devices  27.3 us (14%)
  local copies, waits for them, and re-layouts  11 us (6%)
    pallas_call x10, Pallas kernels, call_stage(): pl.pallas_call(kernel, out_shape=[jax.ShapeDtypeStruct((layers, HALF, NG,...  86.2 us
    ppermute x9, waiting for transfers between devices, swap(): return lax.ppermute(array, 'brick', [(i, i ^ j) for i in range(size)])  26.5 us
    pallas_call x1, Pallas kernels, make_charge(): pl.pallas_call(functools.partial(charge_kernel, peers), out_shape=layers,...  22.7 us
    ppermute x6, starting transfers between devices, exchange(): lax.ppermute(low, 'slab', down)  15.2 us
    pallas_call x1, Pallas kernels, make_gather(): pl.pallas_call(functools.partial(gather_kernel, peers, depth), out_shape=...  13.6 us
    ppermute x9, starting transfers between devices, swap(): return lax.ppermute(array, 'brick', [(i, i ^ j) for i in range(size)])  11.7 us
    unnamed x28, local copies, waits for them, and re-layouts  11 us
  transfers between devices with their start and end apart: 21, of which 7 were waited for; matrix products, arithmetic and copies ran while one was open for 0% of the time, Pallas kernels for 45%

profile of v2, /device:TPU:0, one launch (start us, length us, event | category | flops | bytes accessed | tf_op | source)
XLA Modules:
  0.0 193.0 jit_solution(13325722248100449946)
XLA Ops:
  0.0 1.2 copy-done
  1.2 0.9 copy-done.1
  4.9 0.7 add_select_fusion.3
  5.6 3.0 %collective-permute-start = (s32[2048]{0:T(1024)S(1)}, s32[2048]{0:T(1024)S(1)}, u32[]{:S(2)}, u32[]{:S(2)}) collective-permute-start(s32[2048]{0:T(1024)S(1)} %get-tuple-element.56.refs_0_), channel_id=1, source_target_pairs={{0,1},{1,0},{2,3},{3,2},{4,5},{5,4},{6,7},{7,6},{8,9},{9,8},{10,11... | collective-permute-start | bytes 24584 | tf_op jit(solution)/shard_map/ppermute | solution.py:627
  8.6 1.5 collective-permute-start.1
  10.7 2.9 %collective-permute-start.5 = (bf16[128,2048]{1,0:T(8,128)(2,1)S(1)}, bf16[128,2048]{1,0:T(8,128)(2,1)S(1)}, u32[]{:S(2)}, u32[]{:S(2)}) collective-permute-start(bf16[128,2048]{1,0:T(8,128)(2,1)S(1)} %get-tuple-element.65), channel_id=1, source_target_pairs={{0,3},{1,2},{2,1},{3,0},{4,7},{5,6},{6,5},{7,4},{8,11},{9,10},{10,... | collective-permute-start | bytes 1572872 | tf_op jit(solution)/shard_map/ppermute | solution.py:627
  14.4 0.7 copy-done.3
  18.8 15.9 %collective-permute-done.2.refs_3_ = s32[2048]{0:T(1024)S(1)} collective-permute-done((s32[2048]{0:T(1024)S(1)}, s32[2048]{0:T(1024)S(1)}, u32[]{:S(2)}, u32[]{:S(2)}) %collective-permute-start.2) | collective-permute-done | bytes 8224 | tf_op jit(solution)/shard_map/ppermute | solution.py:627
  34.9 22.7 %charge.1 = (bf16[1,64,64,128]{3,2,1,0:T(8,128)(2,1)S(1)}, bf16[6,64,64,128]{3,2,1,0:T(8,128)(2,1)S(1)}, bf16[1,64,64,128]{3,2,1,0:T(8,128)(2,1)S(1)}) custom-call(s32[2048]{0:T(1024)S(1)} %get-tuple-element.56.refs_0_, s32[2048]{0:T(1024)S(1)} %collective-permute-done.refs_1_, s32[2048]{0:T(1024)S(1)} %collective-permute-done.1.refs_2_, ...), custom_call_target="tpu_custom_call" | custom-call | tf_op jit(solution)/shard_map/charge/pallas_call | solution.py:152
  57.7 3.5 %collective-permute-start.7 = (bf16[1,64,64,128]{3,2,1,0:T(8,128)(2,1)S(1)}, bf16[1,64,64,128]{3,2,1,0:T(8,128)(2,1)S(1)}, u32[]{:S(2)}, u32[]{:S(2)}) collective-permute-start(bf16[1,64,64,128]{3,2,1,0:T(8,128)(2,1)S(1)} %get-tuple-element.67.refs_3_.refs_2_), channel_id=1, source_target_pairs={{4,0},{8,4},{12,8},{16,12},{20,16},{24,20},{28,24},{0,28},{5,1},{9... | collective-permute-start | bytes 3145736 | tf_op jit(solution)/shard_map/ppermute | solution.py:511
  61.2 17.8 %first_inner.1 = (bf16[6,32,64,128]{3,2,1,0:T(8,128)(2,1)S(1)}, bf16[6,32,64,128]{3,2,1,0:T(8,128)(2,1)S(1)}, f32[6,32,64,128]{3,2,1,0:T(8,128)S(1)}, f32[6,32,64,128]{3,2,1,0:T(8,128)S(1)}) custom-call(f32[24,128]{1,0:T(8,128)S(1)} %get-tuple-element.57.refs_0_.refs_8_, bf16[256,256]{1,0:T(8,128)(2,1)S(1)} %get-tuple-element.61.refs_1_, ...), custom_call_target="tpu_custom_call" | custom-call | flops 24000000000 | bytes 36000000 | tf_op jit(solution)/shard_map/first_inner/pallas_call | solution.py:472
  79.0 2.7 %copy-done.11 = f32[6,32,64,128]{3,2,1,0:T(8,128)} copy-done((f32[6,32,64,128]{3,2,1,0:T(8,128)}, f32[6,32,64,128]{3,2,1,0:T(8,128)S(1)}, u32[]{:S(2)}) %copy-start.11) | copy-done | bytes 6291480
  81.7 1.1 collective-permute-done.6.refs_2_
  82.8 2.9 %first_low.1 = (bf16[1,32,64,128]{3,2,1,0:T(8,128)(2,1)S(1)}, bf16[1,32,64,128]{3,2,1,0:T(8,128)(2,1)S(1)}, f32[1,32,64,128]{3,2,1,0:T(8,128)S(1)}, f32[1,32,64,128]{3,2,1,0:T(8,128)S(1)}) custom-call(f32[24,128]{1,0:T(8,128)S(1)} %get-tuple-element.57.refs_0_.refs_8_, bf16[256,256]{1,0:T(8,128)(2,1)S(1)} %get-tuple-element.61.refs_1_, ...), custom_call_target="tpu_custom_call" | custom-call | flops 4000000000 | bytes 6000000 | tf_op jit(solution)/shard_map/first_low/pallas_call | solution.py:472
  85.7 4.1 %collective-permute-start.9 = (bf16[1,32,64,128]{3,2,1,0:T(8,128)(2,1)S(1)}, bf16[1,32,64,128]{3,2,1,0:T(8,128)(2,1)S(1)}, u32[]{:S(2)}, u32[]{:S(2)}) collective-permute-start(bf16[1,32,64,128]{3,2,1,0:T(8,128)(2,1)S(1)} %get-tuple-element.72.refs_6_.refs_7_), channel_id=1, source_target_pairs={{4,0},{8,4},{12,8},{16,12},{20,16},{24,20},{28,24},{0,28},{5,1},{9... | collective-permute-start | bytes 1572872 | tf_op jit(solution)/shard_map/ppermute | solution.py:511
  89.8 2.9 %first_high.1 = (bf16[1,32,64,128]{3,2,1,0:T(8,128)(2,1)S(1)}, bf16[1,32,64,128]{3,2,1,0:T(8,128)(2,1)S(1)}, f32[1,32,64,128]{3,2,1,0:T(8,128)S(1)}, f32[1,32,64,128]{3,2,1,0:T(8,128)S(1)}) custom-call(f32[24,128]{1,0:T(8,128)S(1)} %get-tuple-element.57.refs_0_.refs_8_, bf16[256,256]{1,0:T(8,128)(2,1)S(1)} %get-tuple-element.61.refs_1_, ...), custom_call_target="tpu_custom_call" | custom-call | flops 4000000000 | bytes 6000000 | tf_op jit(solution)/shard_map/first_high/pallas_call | solution.py:472
  92.8 24.3 %second_inner.1 = (bf16[6,32,64,128]{3,2,1,0:T(8,128)(2,1)S(1)}, bf16[6,32,64,128]{3,2,1,0:T(8,128)(2,1)S(1)}) custom-call(f32[24,128]{1,0:T(8,128)S(1)} %get-tuple-element.57.refs_0_.refs_8_, bf16[256,256]{1,0:T(8,128)(2,1)S(1)} %get-tuple-element.59.refs_1_, bf16[256,256]{1,0:T(8,128)(2,1)S(1)} %get-tuple-element.60.refs_2_, ...), custom_call_target="tpu_custom_call" | custom-call | flops 24000000000 | bytes 36000000 | tf_op jit(solution)/shard_map/second_inner/pallas_call | solution.py:472
  117.1 4.0 %second_low.1 = (bf16[1,32,64,128]{3,2,1,0:T(8,128)(2,1)S(1)}, bf16[1,32,64,128]{3,2,1,0:T(8,128)(2,1)S(1)}) custom-call(f32[24,128]{1,0:T(8,128)S(1)} %get-tuple-element.57.refs_0_.refs_8_, bf16[256,256]{1,0:T(8,128)(2,1)S(1)} %get-tuple-element.59.refs_1_, bf16[256,256]{1,0:T(8,128)(2,1)S(1)} %get-tuple-element.60.refs_2_, ...), custom_call_target="tpu_custom_call" | custom-call | flops 4000000000 | bytes 6000000 | tf_op jit(solution)/shard_map/second_low/pallas_call | solution.py:472
  121.1 3.6 %collective-permute-start.12 = (bf16[1,32,64,128]{3,2,1,0:T(8,128)(2,1)S(1)}, bf16[1,32,64,128]{3,2,1,0:T(8,128)(2,1)S(1)}, u32[]{:S(2)}, u32[]{:S(2)}) collective-permute-start(bf16[1,32,64,128]{3,2,1,0:T(8,128)(2,1)S(1)} %get-tuple-element.77.refs_3_.refs_2_), channel_id=1, source_target_pairs={{4,0},{8,4},{12,8},{16,12},{20,16},{24,20},{28,24},{0,28},{5,1},{9... | collective-permute-start | bytes 1572872 | tf_op jit(solution)/shard_map/ppermute | solution.py:511
  125.1 4.0 %second_high.1 = (bf16[1,32,64,128]{3,2,1,0:T(8,128)(2,1)S(1)}, bf16[1,32,64,128]{3,2,1,0:T(8,128)(2,1)S(1)}) custom-call(f32[24,128]{1,0:T(8,128)S(1)} %get-tuple-element.57.refs_0_.refs_8_, bf16[256,256]{1,0:T(8,128)(2,1)S(1)} %get-tuple-element.59.refs_1_, bf16[256,256]{1,0:T(8,128)(2,1)S(1)} %get-tuple-element.60.refs_2_, ...), custom_call_target="tpu_custom_call" | custom-call | flops 4000000000 | bytes 6000000 | tf_op jit(solution)/shard_map/second_high/pallas_call | solution.py:472
  129.3 18.3 %third_inner.1.refs_2_.refs_11_ = bf16[6,32,64,128]{3,2,1,0:T(8,128)(2,1)S(1)} custom-call(f32[24,128]{1,0:T(8,128)S(1)} %get-tuple-element.57.refs_0_.refs_8_, bf16[128,128]{1,0:T(8,128)(2,1)S(1)} %get-tuple-element.58.refs_1_, bf16[1,32,64,128]{3,2,1,0:T(8,128)(2,1)S(1)} %get-tuple-element.77.refs_3_.refs_2_, ...), custom_call_target="tpu_custom_call" | custom-call | flops 24000000000 | bytes 36000000 | tf_op jit(solution)/shard_map/third_inner/pallas_call | solution.py:472
  147.6 3.0 %third_high.1.refs_3_.refs_12_ = bf16[1,32,64,128]{3,2,1,0:T(8,128)(2,1)S(1)} custom-call(f32[24,128]{1,0:T(8,128)S(1)} %get-tuple-element.57.refs_0_.refs_8_, bf16[128,128]{1,0:T(8,128)(2,1)S(1)} %get-tuple-element.58.refs_1_, bf16[6,32,64,128]{3,2,1,0:T(8,128)(2,1)S(1)} %get-tuple-element.75.refs_2_.refs_4_.refs_3_, ...), custom_call_target="tpu_custom_call" | custom-call | flops 4000000000 | bytes 6000000 | tf_op jit(solution)/shard_map/third_high/pallas_call | solution.py:472
  150.7 3.0 %third_low.1.refs_1_.refs_10_ = bf16[1,32,64,128]{3,2,1,0:T(8,128)(2,1)S(1)} custom-call(f32[24,128]{1,0:T(8,128)S(1)} %get-tuple-element.57.refs_0_.refs_8_, bf16[128,128]{1,0:T(8,128)(2,1)S(1)} %get-tuple-element.58.refs_1_, bf16[1,32,64,128]{3,2,1,0:T(8,128)(2,1)S(1)} %collective-permute-done.15.refs_2_, ...), custom_call_target="tpu_custom_call" | custom-call | flops 4000000000 | bytes 6000000 | tf_op jit(solution)/shard_map/third_low/pallas_call | solution.py:472
  153.6 3.6 %collective-permute-start.17 = (bf16[1,32,64,128]{3,2,1,0:T(8,128)(2,1)S(1)}, bf16[1,32,64,128]{3,2,1,0:T(8,128)(2,1)S(1)}, u32[]{:S(2)}, u32[]{:S(2)}) collective-permute-start(bf16[1,32,64,128]{3,2,1,0:T(8,128)(2,1)S(1)} %third_low.1.refs_1_.refs_10_), channel_id=1, source_target_pairs={{4,0},{8,4},{12,8},{16,12},{20,16},{24,20},{28,24},{0,28},{5,1},{9... | collective-permute-start | bytes 1572872 | tf_op jit(solution)/shard_map/ppermute | solution.py:511
  157.2 6.3 %fourth_inner.1 = f32[6,32,64,128]{3,2,1,0:T(8,128)S(1)} custom-call(f32[24,128]{1,0:T(8,128)S(1)} %get-tuple-element.57.refs_0_.refs_8_, bf16[1,32,64,128]{3,2,1,0:T(8,128)(2,1)S(1)} %third_low.1.refs_1_.refs_10_, bf16[6,32,64,128]{3,2,1,0:T(8,128)(2,1)S(1)} %third_inner.1.refs_2_.refs_11_, bf16[1,32,64,128]{3,2,1,0:T(8,128)(2,1)S(1)} %third_high.1.refs_3_.refs_12_), custom_call_target="tpu_custom_call" | custom-call | flops 24000000000 | bytes 36000000 | tf_op jit(solution)/shard_map/fourth_inner/pallas_call | solution.py:472
  163.9 13.6 %gather.1 = (bf16[64,2048]{1,0:T(8,128)(2,1)S(1)}, bf16[64,2048]{1,0:T(8,128)(2,1)S(1)}, bf16[64,2048]{1,0:T(8,128)(2,1)S(1)}, bf16[64,2048]{1,0:T(8,128)(2,1)S(1)}) custom-call(s32[2048]{0:T(1024)S(1)} %fusion.11.refs_0_, s32[2048]{0:T(1024)S(1)} %get-tuple-element.98.refs_1_, s32[2048]{0:T(1024)S(1)} %get-tuple-element.96.refs_2_, ...), custom_call_target="tpu_custom_call" | custom-call | tf_op jit(solution)/shard_map/gather/pallas_call | solution.py:575
  177.5 1.5 collective-permute-start.18
  179.6 1.4 collective-permute-start.20
  181.0 4.0 %collective-permute-done.18.refs_1_ = bf16[64,2048]{1,0:T(8,128)(2,1)S(1)} collective-permute-done((bf16[64,2048]{1,0:T(8,128)(2,1)S(1)}, bf16[64,2048]{1,0:T(8,128)(2,1)S(1)}, u32[]{:S(2)}, u32[]{:S(2)}) %collective-permute-start.18) | collective-permute-done | bytes 262176 | tf_op jit(solution)/shard_map/ppermute | solution.py:627
  185.1 2.9 %collective-permute-done.19.refs_2_ = bf16[64,2048]{1,0:T(8,128)(2,1)S(1)} collective-permute-done((bf16[64,2048]{1,0:T(8,128)(2,1)S(1)}, bf16[64,2048]{1,0:T(8,128)(2,1)S(1)}, u32[]{:S(2)}, u32[]{:S(2)}) %collective-permute-start.19) | collective-permute-done | bytes 262176 | tf_op jit(solution)/shard_map/ppermute | solution.py:627
  187.9 3.5 %collective-permute-done.20.refs_3_ = bf16[64,2048]{1,0:T(8,128)(2,1)S(1)} collective-permute-done((bf16[64,2048]{1,0:T(8,128)(2,1)S(1)}, bf16[64,2048]{1,0:T(8,128)(2,1)S(1)}, u32[]{:S(2)}, u32[]{:S(2)}) %collective-permute-start.20) | collective-permute-done | bytes 262176 | tf_op jit(solution)/shard_map/ppermute | solution.py:627
  191.5 1.5 finish.1
  (60 shorter events, 9.8 us)
Async XLA Ops:
  0.0 1.2 copy-start
  1.2 0.9 copy-start.1
  2.2 0.7 copy-start.4
  2.9 0.7 copy-start.7
  5.6 13.0 %collective-permute-start = (s32[2048]{0:T(1024)S(1)}, s32[2048]{0:T(1024)S(1)}, u32[]{:S(2)}, u32[]{:S(2)}) collective-permute-start(s32[2048]{0:T(1024)S(1)} %get-tuple-element.56.refs_0_), channel_id=1, source_target_pairs={{0,1},{1,0},{2,3},{3,2},{4,5},{5,4},{6,7},{7,6},{8,9},{9,8},{10,11... | collective-permute-start | bytes 24584 | tf_op jit(solution)/shard_map/ppermute | solution.py:627
  8.6 10.1 %collective-permute-start.1 = (s32[2048]{0:T(1024)S(1)}, s32[2048]{0:T(1024)S(1)}, u32[]{:S(2)}, u32[]{:S(2)}) collective-permute-start(s32[2048]{0:T(1024)S(1)} %get-tuple-element.56.refs_0_), channel_id=1, source_target_pairs={{0,2},{1,3},{2,0},{3,1},{4,6},{5,7},{6,4},{7,5},{8,10},{9,11},{10,... | collective-permute-start | bytes 24584 | tf_op jit(solution)/shard_map/ppermute | solution.py:627
  10.1 24.6 %collective-permute-start.3 = (bf16[128,2048]{1,0:T(8,128)(2,1)S(1)}, bf16[128,2048]{1,0:T(8,128)(2,1)S(1)}, u32[]{:S(2)}, u32[]{:S(2)}) collective-permute-start(bf16[128,2048]{1,0:T(8,128)(2,1)S(1)} %get-tuple-element.63), channel_id=1, source_target_pairs={{0,1},{1,0},{2,3},{3,2},{4,5},{5,4},{6,7},{7,6},{8,9},{9,8},{10,11... | collective-permute-start | bytes 1572872 | tf_op jit(solution)/shard_map/ppermute | solution.py:627
  10.7 24.2 %collective-permute-start.4 = (bf16[128,2048]{1,0:T(8,128)(2,1)S(1)}, bf16[128,2048]{1,0:T(8,128)(2,1)S(1)}, u32[]{:S(2)}, u32[]{:S(2)}) collective-permute-start(bf16[128,2048]{1,0:T(8,128)(2,1)S(1)} %get-tuple-element.64), channel_id=1, source_target_pairs={{0,2},{1,3},{2,0},{3,1},{4,6},{5,7},{6,4},{7,5},{8,10},{9,11},{10,... | collective-permute-start | bytes 1572872 | tf_op jit(solution)/shard_map/ppermute | solution.py:627
  10.7 24.2 %collective-permute-start.5 = (bf16[128,2048]{1,0:T(8,128)(2,1)S(1)}, bf16[128,2048]{1,0:T(8,128)(2,1)S(1)}, u32[]{:S(2)}, u32[]{:S(2)}) collective-permute-start(bf16[128,2048]{1,0:T(8,128)(2,1)S(1)} %get-tuple-element.65), channel_id=1, source_target_pairs={{0,3},{1,2},{2,1},{3,0},{4,7},{5,6},{6,5},{7,4},{8,11},{9,10},{10,... | collective-permute-start | bytes 1572872 | tf_op jit(solution)/shard_map/ppermute | solution.py:627
  13.7 0.7 copy-start.2
  14.4 0.7 copy-start.3
  15.1 0.7 copy-start.5
  15.8 0.7 copy-start.6
  18.7 16.0 %collective-permute-start.2 = (s32[2048]{0:T(1024)S(1)}, s32[2048]{0:T(1024)S(1)}, u32[]{:S(2)}, u32[]{:S(2)}) collective-permute-start(s32[2048]{0:T(1024)S(1)} %get-tuple-element.56.refs_0_), channel_id=1, source_target_pairs={{0,3},{1,2},{2,1},{3,0},{4,7},{5,6},{6,5},{7,4},{8,11},{9,10},{10,... | collective-permute-start | bytes 24584 | tf_op jit(solution)/shard_map/ppermute | solution.py:627
  57.6 25.1 %collective-permute-start.6 = (bf16[1,64,64,128]{3,2,1,0:T(8,128)(2,1)S(1)}, bf16[1,64,64,128]{3,2,1,0:T(8,128)(2,1)S(1)}, u32[]{:S(2)}, u32[]{:S(2)}) collective-permute-start(bf16[1,64,64,128]{3,2,1,0:T(8,128)(2,1)S(1)} %get-tuple-element.66.refs_4_.refs_3_), channel_id=1, source_target_pairs={{0,4},{4,8},{8,12},{12,16},{16,20},{20,24},{24,28},{28,0},{1,5},{5... | collective-permute-start | bytes 3145736 | tf_op jit(solution)/shard_map/ppermute | solution.py:511
  57.7 32.1 %collective-permute-start.7 = (bf16[1,64,64,128]{3,2,1,0:T(8,128)(2,1)S(1)}, bf16[1,64,64,128]{3,2,1,0:T(8,128)(2,1)S(1)}, u32[]{:S(2)}, u32[]{:S(2)}) collective-permute-start(bf16[1,64,64,128]{3,2,1,0:T(8,128)(2,1)S(1)} %get-tuple-element.67.refs_3_.refs_2_), channel_id=1, source_target_pairs={{4,0},{8,4},{12,8},{16,12},{20,16},{24,20},{28,24},{0,28},{5,1},{9... | collective-permute-start | bytes 3145736 | tf_op jit(solution)/shard_map/ppermute | solution.py:511
  79.0 2.7 %copy-start.11 = (f32[6,32,64,128]{3,2,1,0:T(8,128)}, f32[6,32,64,128]{3,2,1,0:T(8,128)S(1)}, u32[]{:S(2)}) copy-start(f32[6,32,64,128]{3,2,1,0:T(8,128)S(1)} %get-tuple-element.86.refs_9_) | copy-start | bytes 18874372
  85.6 39.5 %collective-permute-start.8 = (bf16[1,32,64,128]{3,2,1,0:T(8,128)(2,1)S(1)}, bf16[1,32,64,128]{3,2,1,0:T(8,128)(2,1)S(1)}, u32[]{:S(2)}, u32[]{:S(2)}) collective-permute-start(bf16[1,32,64,128]{3,2,1,0:T(8,128)(2,1)S(1)} %get-tuple-element.69.refs_3_.refs_4_), channel_id=1, source_target_pairs={{4,0},{8,4},{12,8},{16,12},{20,16},{24,20},{28,24},{0,28},{5,1},{9... | collective-permute-start | bytes 1572872 | tf_op jit(solution)/shard_map/ppermute | solution.py:511
  85.7 39.4 %collective-permute-start.9 = (bf16[1,32,64,128]{3,2,1,0:T(8,128)(2,1)S(1)}, bf16[1,32,64,128]{3,2,1,0:T(8,128)(2,1)S(1)}, u32[]{:S(2)}, u32[]{:S(2)}) collective-permute-start(bf16[1,32,64,128]{3,2,1,0:T(8,128)(2,1)S(1)} %get-tuple-element.72.refs_6_.refs_7_), channel_id=1, source_target_pairs={{4,0},{8,4},{12,8},{16,12},{20,16},{24,20},{28,24},{0,28},{5,1},{9... | collective-permute-start | bytes 1572872 | tf_op jit(solution)/shard_map/ppermute | solution.py:511
  92.7 24.4 %collective-permute-start.10 = (bf16[1,32,64,128]{3,2,1,0:T(8,128)(2,1)S(1)}, bf16[1,32,64,128]{3,2,1,0:T(8,128)(2,1)S(1)}, u32[]{:S(2)}, u32[]{:S(2)}) collective-permute-start(bf16[1,32,64,128]{3,2,1,0:T(8,128)(2,1)S(1)} %get-tuple-element.71.refs_5_.refs_4_), channel_id=1, source_target_pairs={{0,4},{4,8},{8,12},{12,16},{16,20},{20,24},{24,28},{28,0},{1,5},{5... | collective-permute-start | bytes 1572872 | tf_op jit(solution)/shard_map/ppermute | solution.py:511
  92.7 24.4 %collective-permute-start.11 = (bf16[1,32,64,128]{3,2,1,0:T(8,128)(2,1)S(1)}, bf16[1,32,64,128]{3,2,1,0:T(8,128)(2,1)S(1)}, u32[]{:S(2)}, u32[]{:S(2)}) collective-permute-start(bf16[1,32,64,128]{3,2,1,0:T(8,128)(2,1)S(1)} %get-tuple-element.74.refs_8_.refs_7_), channel_id=1, source_target_pairs={{0,4},{4,8},{8,12},{12,16},{16,20},{20,24},{24,28},{28,0},{1,5},{5... | collective-permute-start | bytes 1572872 | tf_op jit(solution)/shard_map/ppermute | solution.py:511
  121.1 26.5 %collective-permute-start.12 = (bf16[1,32,64,128]{3,2,1,0:T(8,128)(2,1)S(1)}, bf16[1,32,64,128]{3,2,1,0:T(8,128)(2,1)S(1)}, u32[]{:S(2)}, u32[]{:S(2)}) collective-permute-start(bf16[1,32,64,128]{3,2,1,0:T(8,128)(2,1)S(1)} %get-tuple-element.77.refs_3_.refs_2_), channel_id=1, source_target_pairs={{4,0},{8,4},{12,8},{16,12},{20,16},{24,20},{28,24},{0,28},{5,1},{9... | collective-permute-start | bytes 1572872 | tf_op jit(solution)/shard_map/ppermute | solution.py:511
  124.7 4.6 %slice-start = ((s8[6291456]{0:T(1024)(128)(4,1)}), s8[4194304]{0:T(1024)(128)(4,1)S(1)}, s32[]{:S(2)}) async-start(s8[6291456]{0:T(1024)(128)(4,1)} %bitcast.28), calls=%async_computation | async-start | bytes 8388608
  124.7 4.6 %slice-start.1 = ((s8[6291456]{0:T(1024)(128)(4,1)}), s8[2097152]{0:T(1024)(128)(4,1)S(1)}, s32[]{:S(2)}) async-start(s8[6291456]{0:T(1024)(128)(4,1)} %bitcast.28), calls=%async_computation.1 | async-start | bytes 4194304
  124.7 22.9 %collective-permute-start.13 = (bf16[1,32,64,128]{3,2,1,0:T(8,128)(2,1)S(1)}, bf16[1,32,64,128]{3,2,1,0:T(8,128)(2,1)S(1)}, u32[]{:S(2)}, u32[]{:S(2)}) collective-permute-start(bf16[1,32,64,128]{3,2,1,0:T(8,128)(2,1)S(1)} %get-tuple-element.80.refs_6_.refs_5_), channel_id=1, source_target_pairs={{4,0},{8,4},{12,8},{16,12},{20,16},{24,20},{28,24},{0,28},{5,1},{9... | collective-permute-start | bytes 1572872 | tf_op jit(solution)/shard_map/ppermute | solution.py:511
  129.1 21.6 %collective-permute-start.15 = (bf16[1,32,64,128]{3,2,1,0:T(8,128)(2,1)S(1)}, bf16[1,32,64,128]{3,2,1,0:T(8,128)(2,1)S(1)}, u32[]{:S(2)}, u32[]{:S(2)}) collective-permute-start(bf16[1,32,64,128]{3,2,1,0:T(8,128)(2,1)S(1)} %get-tuple-element.76.refs_3_.refs_4_), channel_id=1, source_target_pairs={{0,4},{4,8},{8,12},{12,16},{16,20},{20,24},{24,28},{28,0},{1,5},{5... | collective-permute-start | bytes 1572872 | tf_op jit(solution)/shard_map/ppermute | solution.py:511
  129.2 21.5 %collective-permute-start.16 = (bf16[1,32,64,128]{3,2,1,0:T(8,128)(2,1)S(1)}, bf16[1,32,64,128]{3,2,1,0:T(8,128)(2,1)S(1)}, u32[]{:S(2)}, u32[]{:S(2)}) collective-permute-start(bf16[1,32,64,128]{3,2,1,0:T(8,128)(2,1)S(1)} %get-tuple-element.79.refs_6_.refs_7_), channel_id=1, source_target_pairs={{0,4},{4,8},{8,12},{12,16},{16,20},{20,24},{24,28},{28,0},{1,5},{5... | collective-permute-start | bytes 1572872 | tf_op jit(solution)/shard_map/ppermute | solution.py:511
  150.5 12.9 %collective-permute-start.14 = (bf16[1,32,64,128]{3,2,1,0:T(8,128)(2,1)S(1)}, bf16[1,32,64,128]{3,2,1,0:T(8,128)(2,1)S(1)}, u32[]{:S(2)}, u32[]{:S(2)}) collective-permute-start(bf16[1,32,64,128]{3,2,1,0:T(8,128)(2,1)S(1)} %third_high.1.refs_3_.refs_12_), channel_id=1, source_target_pairs={{0,4},{4,8},{8,12},{12,16},{16,20},{20,24},{24,28},{28,0},{1,5},{5... | collective-permute-start | bytes 1572872 | tf_op jit(solution)/shard_map/ppermute | solution.py:511
  153.6 10.3 %collective-permute-start.17 = (bf16[1,32,64,128]{3,2,1,0:T(8,128)(2,1)S(1)}, bf16[1,32,64,128]{3,2,1,0:T(8,128)(2,1)S(1)}, u32[]{:S(2)}, u32[]{:S(2)}) collective-permute-start(bf16[1,32,64,128]{3,2,1,0:T(8,128)(2,1)S(1)} %third_low.1.refs_1_.refs_10_), channel_id=1, source_target_pairs={{4,0},{8,4},{12,8},{16,12},{20,16},{24,20},{28,24},{0,28},{5,1},{9... | collective-permute-start | bytes 1572872 | tf_op jit(solution)/shard_map/ppermute | solution.py:511
  177.5 7.6 %collective-permute-start.18 = (bf16[64,2048]{1,0:T(8,128)(2,1)S(1)}, bf16[64,2048]{1,0:T(8,128)(2,1)S(1)}, u32[]{:S(2)}, u32[]{:S(2)}) collective-permute-start(bf16[64,2048]{1,0:T(8,128)(2,1)S(1)} %get-tuple-element.88), channel_id=1, source_target_pairs={{0,1},{1,0},{2,3},{3,2},{4,5},{5,4},{6,7},{7,6},{8,9},{9,8},{10,11... | collective-permute-start | bytes 786440 | tf_op jit(solution)/shard_map/ppermute | solution.py:627
  179.0 8.9 %collective-permute-start.19 = (bf16[64,2048]{1,0:T(8,128)(2,1)S(1)}, bf16[64,2048]{1,0:T(8,128)(2,1)S(1)}, u32[]{:S(2)}, u32[]{:S(2)}) collective-permute-start(bf16[64,2048]{1,0:T(8,128)(2,1)S(1)} %get-tuple-element.89), channel_id=1, source_target_pairs={{0,2},{1,3},{2,0},{3,1},{4,6},{5,7},{6,4},{7,5},{8,10},{9,11},{10,... | collective-permute-start | bytes 786440 | tf_op jit(solution)/shard_map/ppermute | solution.py:627
  179.6 11.9 %collective-permute-start.20 = (bf16[64,2048]{1,0:T(8,128)(2,1)S(1)}, bf16[64,2048]{1,0:T(8,128)(2,1)S(1)}, u32[]{:S(2)}, u32[]{:S(2)}) collective-permute-start(bf16[64,2048]{1,0:T(8,128)(2,1)S(1)} %get-tuple-element.90), channel_id=1, source_target_pairs={{0,3},{1,2},{2,1},{3,0},{4,7},{5,6},{6,5},{7,4},{8,11},{9,10},{10,... | collective-permute-start | bytes 786440 | tf_op jit(solution)/shard_map/ppermute | solution.py:627
  (3 other events, 2.0 us)

commit v3 on v2

v3 whole, which is shorter than its diff:
```python
import functools

import jax
import jax.numpy as jnp
from jax import lax
from jax.experimental import pallas as pl
from jax.experimental.pallas import tpu as pltpu
from jax.sharding import PartitionSpec as P

NG = 64
CH = 64
NT = 4
KSETS = 8
LANES = 2 * CH
HALF = NG // 2
GROUP = 8
ROWS = 4
RUN = 16
BLOCK = 256
MIB = 1024 * 1024
F32 = jnp.float32
BF16 = jnp.bfloat16


def params(mib):
    return pltpu.CompilerParams(vmem_limit_bytes=mib * MIB)


def cost(flops, nbytes):
    return pl.CostEstimate(flops=flops, bytes_accessed=nbytes, transcendentals=0)


def vmem():
    return pl.BlockSpec(memory_space=pltpu.VMEM)


def smem():
    return pl.BlockSpec(memory_space=pltpu.SMEM)


def deposits_kernel(peers, me_ref, feat_ref, tan_ref, sten_ref, table_ref, tab_ref, *refs):
    outs = refs[:peers]
    feat, tan, sten, rows, sems, small = refs[peers:]
    me = me_ref[0]
    parts, _, step = feat.shape
    kinds_copy = pltpu.make_async_copy(sten_ref, sten, small.at[0])
    table_copy = pltpu.make_async_copy(table_ref, rows, small.at[1])
    kinds_copy.start()
    table_copy.start()
    copies = []
    for p in range(parts):
        at = pl.ds(p * step, step)
        pair = (
            pltpu.make_async_copy(feat_ref.at[:, at], feat.at[p], sems.at[p, 0]),
            pltpu.make_async_copy(tan_ref.at[:, :, at], tan.at[p], sems.at[p, 1]),
        )
        for copy in pair:
            copy.start()
        copies.append(pair)
    kinds_copy.wait()
    table_copy.wait()
    table = rows[...].T
    for p in range(parts):
        at = pl.ds(p * step, step)
        kinds = jnp.broadcast_to(sten[:, at], (CH, step))
        tab = jnp.zeros((CH, step), F32)
        for s in range(KSETS):
            tab = jnp.where(kinds == s, table[:, s : s + 1], tab)
        tab_ref[:, at] = tab
        for copy in copies[p]:
            copy.wait()
        first = (feat[p].astype(F32) * tab).astype(BF16)
        for j in range(peers):
            outs[j][:CH, at] = first
            own = tan[p, lax.rem(lax.bitwise_xor(me, j), NT)]
            outs[j][CH:, at] = (own.astype(F32) * tab).astype(BF16)


def make_deposits(me, features, tangents, stencil, table, peers):
    count = features.shape[1]
    step = min(512, count)
    parts = count // step
    far = pl.BlockSpec(memory_space=pltpu.HBM)
    out_shape = [jax.ShapeDtypeStruct((CH, count), F32)]
    out_shape += [jax.ShapeDtypeStruct((LANES, count), BF16)] * peers
    return pl.pallas_call(
        functools.partial(deposits_kernel, peers),
        out_shape=out_shape,
        in_specs=[smem()] + [far] * 4,
        out_specs=[vmem()] * (peers + 1),
        scratch_shapes=[
            pltpu.VMEM((parts, CH, step), BF16),
            pltpu.VMEM((parts, NT, CH, step), BF16),
            pltpu.VMEM((1, count), jnp.int32),
            pltpu.VMEM(table.shape, F32),
            pltpu.SemaphoreType.DMA((parts, 2)),
            pltpu.SemaphoreType.DMA((2,)),
        ],
        compiler_params=params(8),
        name="deposits",
    )(me, features, tangents, stencil.reshape(1, count), table)


def clear(ref):
    def body(i, carry):
        at = pl.ds(pl.multiple_of(i * 256, 256), 256)
        ref[at, :] = jnp.zeros((256, LANES), F32)
        return carry

    lax.fori_loop(0, ref.shape[0] // 256, body, 0)


def scatter(cells, chunks, marks, sums_ref, rows_ref, early_ref):
    width = early_ref.shape[0]
    blocks = rows_ref.shape[0] // width
    row = lax.broadcasted_iota(jnp.int32, (width, width), 0)
    column = lax.broadcasted_iota(jnp.int32, (width, width), 1)
    early = (column <= row) & (row // RUN == column // RUN)
    early_ref[...] = jnp.where(early, 1.0, 0.0)
    for cell_ref, chunk_ref, mark_ref in zip(cells, chunks, marks):

        def turn(i, carry):
            at = pl.ds(pl.multiple_of(i * width, width), width)
            here = jnp.broadcast_to(mark_ref[:, at].astype(F32), (width, width))
            taken = jnp.where(here.T == here, early_ref[...], 0.0).astype(BF16)
            rows_ref[at, :] = lax.dot_general(
                taken, chunk_ref[:, at], (((1,), (1,)), ((), ())), preferred_element_type=F32
            )
            return carry

        lax.fori_loop(0, blocks, turn, 0, unroll=2)

        def add(i, carry):
            first = i * RUN
            where = [cell_ref[first + t] for t in range(RUN)]
            sums = [
                sums_ref[pl.ds(cell, 1), :] + rows_ref[pl.ds(first + t, 1), :]
                for t, cell in enumerate(where)
            ]
            for cell, value in zip(where, sums):
                sums_ref[pl.ds(cell, 1), :] = value
            return carry

        lax.fori_loop(0, blocks * width // RUN, add, 0)


def split_scatter(peers, refs):
    cells, chunks = refs[:peers], refs[peers : 2 * peers]
    return cells, chunks, refs[2 * peers : 3 * peers], refs[3 * peers :]


def first_sums_kernel(peers, *refs):
    cells, chunks, marks, (sums_ref, rows_ref, early_ref) = split_scatter(peers, refs)
    clear(sums_ref)
    scatter(cells, chunks, marks, sums_ref, rows_ref, early_ref)


def more_sums_kernel(peers, *refs):
    cells, chunks, marks, (_, sums_ref, rows_ref, early_ref) = split_scatter(peers, refs)
    scatter(cells, chunks, marks, sums_ref, rows_ref, early_ref)


def charge_kernel(peers, *refs):
    cells, chunks, marks, rest = split_scatter(peers, refs)
    _, sums_ref, low_ref, mid_ref, high_ref, rows_ref, early_ref = rest
    scatter(cells, chunks, marks, sums_ref, rows_ref, early_ref)

    def finish(base, out_ref, index):
        def body(y, carry):
            at = pl.ds(pl.multiple_of(base + y * NG, NG), NG)
            out_ref[index, y] = sums_ref[at, :].astype(BF16)
            return carry

        lax.fori_loop(0, NG, body, 0, unroll=4)

    inner = mid_ref.shape[0]
    finish(0, low_ref, 0)
    finish((inner + 1) * NG * NG, high_ref, 0)

    def between(z, carry):
        finish((z + 1) * NG * NG, mid_ref, z)
        return carry

    lax.fori_loop(0, inner, between, 0)


def run_scatter(kernel, name, cells, chunks, sums, depth):
    peers, count = len(cells), cells[0].shape[0]
    width = min(BLOCK, count)
    args = [*cells, *chunks, *[c.reshape(1, count) for c in cells]]
    specs = [smem()] * peers + [vmem()] * (2 * peers)
    out_shape = [jax.ShapeDtypeStruct((depth * NG * NG, LANES), F32)]
    aliases = {}
    if sums is not None:
        aliases[len(args)] = 0
        args.append(sums)
        specs.append(vmem())
    if kernel is charge_kernel:
        out_shape += [jax.ShapeDtypeStruct((n, NG, NG, LANES), BF16) for n in (1, depth - 2, 1)]
    return pl.pallas_call(
        functools.partial(kernel, peers),
        out_shape=out_shape,
        in_specs=specs,
        out_specs=[vmem()] * len(out_shape),
        scratch_shapes=[pltpu.VMEM((count, LANES), F32), pltpu.VMEM((width, width), F32)],
        input_output_aliases=aliases,
        compiler_params=params(6),
        cost_estimate=cost(peers * 4_000_000_000, peers * 8_000_000),
        name=name,
    )(*args)


ROW_BIAS1, ROW_BIAS2, ROW_SCALE, ROW_HALF = 18, 19, 20, 21


def weights_kernel(p1_ref, p2_ref, t1_ref, t2_ref, b1_ref, b2_ref, r_ref, *outs):
    mix1_ref, mix2_ref, back2_ref, back1_ref, lanes_ref = outs
    p1, p2 = p1_ref[...].astype(F32), p2_ref[...].astype(F32)
    p1t, p2t = 0.5 * p1.T, 0.5 * p2.T
    zero = jnp.zeros((CH, CH), F32)

    def fill(ref, block, order):
        for i, place in enumerate(order):
            parts = [block if j == place else zero for j in range(len(order))]
            ref[i * CH : (i + 1) * CH, :] = jnp.concatenate(parts, 1).astype(BF16)

    fill(mix1_ref, p1t, (0, 2, 1, 3))
    fill(mix2_ref, p2t, (0, 1, 2, 3))
    fill(back2_ref, p2, (0, 1, 2, 3))
    fill(back1_ref, p1, (0, 1))

    def put(row, value):
        lanes_ref[row : row + 1, :] = jnp.concatenate([value, value], 1)

    for axis in range(3):
        for t in range(3):
            put(3 * axis + t, t1_ref[axis, t : t + 1, :])
            put(9 + 3 * axis + t, t2_ref[axis, t : t + 1, :])
    for t in range(3):
        put(ROW_HALF + t, 0.5 * t2_ref[2, t : t + 1, :])
    put(ROW_BIAS1, 0.5 * b1_ref[...])
    put(ROW_BIAS2, 0.5 * b2_ref[...])
    put(ROW_SCALE, r_ref[...])


def make_weights(point1, point2, taps1, taps2, bias1, bias2, readout):
    wide = jax.ShapeDtypeStruct((2 * LANES, 2 * LANES), BF16)
    return pl.pallas_call(
        weights_kernel,
        out_shape=[
            wide,
            wide,
            wide,
            jax.ShapeDtypeStruct((LANES, LANES), BF16),
            jax.ShapeDtypeStruct((24, LANES), F32),
        ],
        in_specs=[vmem()] * 7,
        out_specs=[vmem()] * 5,
        compiler_params=params(4),
        name="weights",
    )(point1, point2, taps1, taps2, *[v.reshape(1, CH) for v in (bias1, bias2, readout)])


def spread(weights, value):
    rows = value.shape[0]
    return (value.reshape(rows // 8, 8, LANES) * weights[None]).reshape(rows, LANES)


def lane_row(w_ref, row):
    return jnp.broadcast_to(w_ref[row : row + 1, :], (8, LANES))


def taps_of(w_ref, start, flip):
    order = (2, 1, 0) if flip else (0, 1, 2)
    return [lane_row(w_ref, start + t) for t in order]


def weigh(w, low, mid, high):
    return spread(w[0], low) + spread(w[1], mid) + spread(w[2], high)


def by_rows(rows, work):
    def body(i, carry):
        for store in [work(i * ROWS + t) for t in range(ROWS)]:
            store()
        return carry

    lax.fori_loop(0, rows // ROWS, body, 0)


def along_z(w, around, u_ref, rows, offset):
    def work(y):
        low, mid, high = (ref[index, y].astype(F32) for ref, index in around)
        value = weigh(w, low, mid, high)

        def store():
            u_ref[y + offset] = value

        return store

    by_rows(rows, work)


def keep_layer(new, slot, ring_ref, rows):
    ref, index = new

    def work(y):
        value = ref[index, y].astype(F32)

        def store():
            ring_ref[slot, y] = value

        return store

    by_rows(rows, work)


def along_z_ring(w, new, step, ring_ref, u_ref, rows, offset):
    ref, index = new
    low, mid, high = (lax.rem(jnp.int32(step + t), jnp.int32(3)) for t in (1, 2, 0))

    def work(y):
        last = ref[index, y].astype(F32)
        value = weigh(w, ring_ref[low, y], ring_ref[mid, y], last)

        def store():
            ring_ref[high, y] = last
            u_ref[y + offset] = value

        return store

    by_rows(rows, work)


def wrap_halves(u_ref):
    u_ref[0] = pltpu.roll(u_ref[HALF], CH, 1)
    u_ref[HALF + 1] = pltpu.roll(u_ref[1], CH, 1)


def along_y(wy, u_ref, before, here, after):
    return weigh(wy, u_ref[before], u_ref[here], u_ref[after])


def along_x(wx, value, v_ref, slot):
    v_ref[slot, 8 : 8 + NG] = value
    v_ref[slot, 7:8] = value[NG - 1 :]
    v_ref[slot, 8 + NG : 9 + NG] = value[:1]
    return weigh(wx, v_ref[slot, 7 : 7 + NG], value, v_ref[slot, 9 : 9 + NG])


def silu_terms(half):
    t = jnp.tanh(half)
    product = half * t
    bump = 1.0 - t * t
    return half + product, (1.0 + t) + half * bump, bump * (1.0 - product)


def staggered(steps, groups):
    depth = len(steps)

    def turn(i, first, last):
        for n in reversed(range(first, last)):
            steps[n](i - n)

    for i in range(depth - 1):
        turn(i, 0, i + 1)

    def body(i, carry):
        turn(i, 0, depth)
        return carry

    lax.fori_loop(depth - 1, groups, body, 0)
    for i in range(groups, groups + depth - 1):
        turn(i, i - groups + 1, depth)


def part(t):
    return slice(t * NG, (t + 1) * NG)


def first_stage(refs, u_refs, work, outs, at):
    w_ref, mix_ref = refs
    (u_ref,) = u_refs
    v_ref, left_ref = work[:2]
    h_ref, m_ref, a_ref, b_ref = outs
    wy, wx = taps_of(w_ref, 3, False), taps_of(w_ref, 6, False)
    bias = w_ref[ROW_BIAS1 : ROW_BIAS1 + 1, :]

    def taps(i):
        for t in range(GROUP):
            y = i * GROUP + t
            z = y + HALF
            top = along_y(wy, u_ref, jnp.bitwise_and(y + NG - 1, NG - 1), y, y + 1)
            end = along_y(wy, u_ref, z - 1, z, jnp.bitwise_and(z + 1, NG - 1))
            left_ref[part(t), :LANES] = along_x(wx, top, v_ref, 2 * t).astype(BF16)
            left_ref[part(t), LANES:] = along_x(wx, end, v_ref, 2 * t + 1).astype(BF16)

    def mix(i):
        mixed = jnp.dot(left_ref[...], mix_ref[...], preferred_element_type=F32)
        for t in range(GROUP):
            y = i * GROUP + t
            tangent = mixed[part(t), LANES:]
            value, slope, curve = silu_terms(mixed[part(t), :LANES] + bias)
            h_ref[at, y] = value.astype(BF16)
            m_ref[at, y] = (slope * tangent).astype(BF16)
            a_ref[at, y] = curve * tangent
            b_ref[at, y] = slope

    staggered((taps, mix), HALF // GROUP)


def second_stage(refs, u_refs, work, outs, at):
    w_ref, mix_ref, back_ref = refs
    uh_ref, um_ref = u_refs
    v_ref, left_ref, next_ref = work
    rh_ref, rm_ref = outs
    wy, wx = taps_of(w_ref, 12, False), taps_of(w_ref, 15, False)
    bias = w_ref[ROW_BIAS2 : ROW_BIAS2 + 1, :]
    scale = w_ref[ROW_SCALE : ROW_SCALE + 1, :]

    def taps(i):
        for t in range(GROUP):
            y = i * GROUP + t
            sh = along_x(wx, along_y(wy, uh_ref, y, y + 1, y + 2), v_ref, 2 * t)
            sm = along_x(wx, along_y(wy, um_ref, y, y + 1, y + 2), v_ref, 2 * t + 1)
            left_ref[part(t), :LANES] = sh.astype(BF16)
            left_ref[part(t), LANES:] = sm.astype(BF16)

    def mix(i):
        mixed = jnp.dot(left_ref[...], mix_ref[...], preferred_element_type=F32)
        _, slope, curve = silu_terms(mixed[:, :LANES] + bias)
        next_ref[:, :LANES] = (slope * (0.5 * scale)).astype(BF16)
        next_ref[:, LANES:] = (curve * scale * mixed[:, LANES:]).astype(BF16)

    def back(i):
        mixed = jnp.dot(next_ref[...], back_ref[...], preferred_element_type=F32).astype(BF16)
        for t in range(GROUP):
            rh_ref[at, i * GROUP + t] = mixed[part(t), :LANES]
            rm_ref[at, i * GROUP + t] = mixed[part(t), LANES:]

    staggered((taps, mix, back), HALF // GROUP)


def third_stage(refs, u_refs, work, outs, at):
    w_ref, back_ref, a_ref, b_ref = refs
    uh_ref, um_ref = u_refs
    v_ref, left_ref = work[:2]
    (y_ref,) = outs
    wy, wx = taps_of(w_ref, 12, True), taps_of(w_ref, 15, True)
    wx_half = taps_of(w_ref, ROW_HALF, True)

    def taps(i):
        for t in range(GROUP):
            y = i * GROUP + t
            g = along_x(wx, along_y(wy, uh_ref, y, y + 1, y + 2), v_ref, 2 * t)
            dg = along_x(wx_half, along_y(wy, um_ref, y, y + 1, y + 2), v_ref, 2 * t + 1)
            left_ref[part(t), :LANES] = (a_ref[at, y] * g + b_ref[at, y] * dg).astype(BF16)

    def back(i):
        mixed = jnp.dot(left_ref[:, :LANES], back_ref[...], preferred_element_type=F32)
        for t in range(GROUP):
            y_ref[at, i * GROUP + t] = mixed[part(t)].astype(BF16)

    staggered((taps, back), HALF // GROUP)


def fourth_rows(w_ref, u_ref, v_ref, put):
    wy, wx = taps_of(w_ref, 3, True), taps_of(w_ref, 6, True)

    def body(i, carry):
        for t in range(GROUP):
            y = i * GROUP + t
            out = along_x(wx, along_y(wy, u_ref, y, y + 1, y + 2), v_ref, t)
            put(y, out.astype(BF16).astype(F32))
        return carry

    lax.fori_loop(0, HALF // GROUP, body, 0)


def fourth_stage(refs, u_refs, work, outs, at):
    def put(y, row):
        outs[0][at, y] = row

    fourth_rows(refs[0], u_refs[0], work[0], put)


STAGES = {
    "first": (first_stage, NG, (BF16, BF16, F32, F32), (0, 1), (0, False)),
    "second": (second_stage, HALF, (BF16, BF16), (0, 1), (9, False)),
    "third": (third_stage, HALF, (BF16,), (0,), (9, True)),
    "fourth": (fourth_stage, HALF, (F32,), (), (0, True)),
}


def taker(refs):
    left = list(refs)

    def take(n):
        got = left[:n]
        del left[:n]
        return got

    return take


def inner_kernel(stage, n_const, n_field, n_local, *refs):
    body, rows, kinds, _, (start, flip) = STAGES[stage]
    take = taker(refs)
    consts = take(n_const)
    fields = [take(3) for _ in range(n_field)]
    local, outs = take(n_local), take(len(kinds))
    u_refs, ring_refs = take(n_field), take(n_field)
    work = take(3)
    offset = 0 if rows == NG else 1
    wz = taps_of(consts[0], start, flip)
    inner = fields[0][1].shape[0]

    def layer(step, which, index):
        for field, u_ref, ring_ref in zip(fields, u_refs, ring_refs):
            along_z_ring(wz, (field[which], index), step, ring_ref, u_ref, rows, offset)
            if offset:
                wrap_halves(u_ref)
        body(consts + local, u_refs, work, outs, step - 2)

    def loop(step, carry):
        layer(step, 1, step - 1)
        return carry

    for (low_ref, mid_ref, _), ring_ref in zip(fields, ring_refs):
        keep_layer((low_ref, 0), 0, ring_ref, rows)
        keep_layer((mid_ref, 0), 1, ring_ref, rows)
    lax.fori_loop(2, inner + 1, loop, 0)
    layer(inner + 1, 2, 0)


def edge_kernel(stage, n_const, n_field, n_local, places, *refs):
    body, rows, kinds, _, (start, flip) = STAGES[stage]
    take = taker(refs)
    consts = take(n_const)
    fields = [take(3) for _ in range(n_field)]
    local, outs, u_refs = take(n_local), take(len(kinds)), take(n_field)
    work = take(3)
    offset = 0 if rows == NG else 1
    wz = taps_of(consts[0], start, flip)
    for field, u_ref in zip(fields, u_refs):
        along_z(wz, list(zip(field, places)), u_ref, rows, offset)
        if offset:
            wrap_halves(u_ref)
    body(consts + local, u_refs, work, outs, 0)


def field_scratch(stage, n_field, ring):
    rows = STAGES[stage][1]
    u_rows = NG if rows == NG else HALF + 2
    scratch = [pltpu.VMEM((u_rows, NG, LANES), F32)] * n_field
    if ring:
        scratch += [pltpu.VMEM((3, rows, NG, LANES), F32)] * n_field
    left = pltpu.VMEM((GROUP * NG, 2 * LANES), BF16)
    return scratch + [pltpu.VMEM((2 * GROUP, NG + 16, LANES), F32), left, left]


def call_stage(kernel, name, layers, mib, kinds, args, scratch):
    return pl.pallas_call(
        kernel,
        out_shape=[jax.ShapeDtypeStruct((layers, HALF, NG, LANES), k) for k in kinds],
        in_specs=[vmem()] * len(args),
        out_specs=[vmem()] * len(kinds),
        scratch_shapes=scratch,
        compiler_params=params(mib),
        cost_estimate=cost(layers * 4_000_000_000, layers * 6_000_000),
        name=name,
    )(*args)


def run_inner(stage, consts, fields, local):
    kernel = functools.partial(inner_kernel, stage, len(consts), len(fields), len(local))
    args = [*consts, *[ref for field in fields for ref in field], *[x[1] for x in local]]
    scratch = field_scratch(stage, len(fields), True)
    layers = fields[0][1].shape[0]
    return call_stage(kernel, stage + "_inner", layers, 16, STAGES[stage][2], args, scratch)


def run_edge(stage, consts, fields, local, halos, side):
    inner = fields[0][1].shape[0]
    around, places = [], (0, 0, 0) if side == 0 else (inner - 1, 0, 0)
    for (low, mid, high), (below, above) in zip(fields, halos):
        around += [below, low, mid] if side == 0 else [mid, high, above]
    kernel = functools.partial(
        edge_kernel, stage, len(consts), len(fields), len(local), places
    )
    args = [*consts, *around, *[x[2 * side] for x in local]]
    scratch = field_scratch(stage, len(fields), False)
    name = stage + ("_low", "_high")[side]
    return call_stage(kernel, name, 1, 8, STAGES[stage][2], args, scratch)


def exchange(fields):
    size = lax.axis_size("slab")
    up = [(i, (i + 1) % size) for i in range(size)]
    down = [(j, i) for i, j in up]
    return [
        (lax.ppermute(high, "slab", up), lax.ppermute(low, "slab", down))
        for low, _, high in fields
    ]


def ends_kernel(w_ref, below_ref, low_ref, mid_ref, high_ref, above_ref, inner_ref, f_ref, *work):
    u_ref, v_ref = work
    inner = mid_ref.shape[0]
    layer = HALF * NG

    def copy(i, carry):
        at = pl.multiple_of(i * 256, 256)
        f_ref[pl.ds(layer + at, 256), :] = inner_ref[pl.ds(at, 256), :]
        return carry

    lax.fori_loop(0, inner * layer // 256, copy, 0)
    wz = taps_of(w_ref, 0, True)
    for base, around in (
        (0, ((below_ref, 0), (low_ref, 0), (mid_ref, 0))),
        ((inner + 1) * layer, ((mid_ref, inner - 1), (high_ref, 0), (above_ref, 0))),
    ):
        along_z(wz, around, u_ref, HALF, 1)
        wrap_halves(u_ref)

        def put(y, row, base=base):
            f_ref[pl.ds(pl.multiple_of(base + y * NG, NG), NG), :] = row

        fourth_rows(w_ref, u_ref, v_ref, put)


def run_ends(lanes, y, halos, inner):
    low, mid, high = y
    below, above = halos
    rows = (mid.shape[0] + 2) * HALF * NG
    return pl.pallas_call(
        ends_kernel,
        out_shape=jax.ShapeDtypeStruct((rows, LANES), F32),
        in_specs=[vmem()] * 7,
        out_specs=vmem(),
        scratch_shapes=[
            pltpu.VMEM((HALF + 2, NG, LANES), F32),
            pltpu.VMEM((2 * GROUP, NG + 16, LANES), F32),
        ],
        compiler_params=params(8),
        name="ends",
    )(lanes, below, low, mid, high, above, inner.reshape(-1, LANES))


def gather_kernel(spots_ref, half_ref, f_ref, out_ref, rows_ref):
    count = rows_ref.shape[0]
    unroll = 16
    eye = jnp.where(
        lax.broadcasted_iota(jnp.int32, (LANES, LANES), 0)
        == lax.broadcasted_iota(jnp.int32, (LANES, LANES), 1),
        1.0,
        0.0,
    ).astype(BF16)

    def pick(i, carry):
        for t in range(unroll):
            atom = i * unroll + t
            rows_ref[pl.ds(atom, 1), :] = f_ref[pl.ds(spots_ref[atom], 1), :]
        return carry

    lax.fori_loop(0, count // unroll, pick, 0)
    width = min(BLOCK, count)
    for start in range(0, count, width):
        at = slice(start, start + width)
        turned = lax.dot_general(
            eye,
            rows_ref[at, :].astype(BF16),
            (((1,), (1,)), ((), ())),
            preferred_element_type=F32,
        )
        later = jnp.broadcast_to(half_ref[:, at], (CH, width)) == 1
        out_ref[:, at] = jnp.where(later, turned[CH:], turned[:CH]).astype(BF16)


def make_gather(spots, half, field):
    count = spots.shape[0]
    return pl.pallas_call(
        gather_kernel,
        out_shape=jax.ShapeDtypeStruct((CH, count), BF16),
        in_specs=[smem(), vmem(), vmem()],
        out_specs=vmem(),
        scratch_shapes=[pltpu.VMEM((count, LANES), F32)],
        compiler_params=params(6),
        cost_estimate=cost(4_000_000_000, 6_000_000),
        name="gather",
    )(spots, half.reshape(1, count), field)


def finish_kernel(peers, me_ref, tab_ref, *refs):
    out_ref = refs[peers]
    me = me_ref[0]
    for j in range(peers):
        k = lax.rem(lax.bitwise_xor(me, j), NT)
        out_ref[k] = refs[j][...].astype(F32) * tab_ref[...]


def make_output(me, tab, returned):
    return pl.pallas_call(
        functools.partial(finish_kernel, len(returned)),
        out_shape=jax.ShapeDtypeStruct((NT,) + tab.shape, F32),
        in_specs=[smem()] + [vmem()] * (len(returned) + 1),
        out_specs=vmem(),
        compiler_params=params(8),
        name="finish",
    )(me, tab, *returned)


def swap(array, j):
    if j == 0:
        return array
    size = lax.axis_size("brick")
    return lax.ppermute(array, "brick", [(i, i ^ j) for i in range(size)])


def shards(
    features,
    tangents,
    route,
    cell_local,
    stencil,
    stencil_table,
    taps1,
    taps2,
    point1,
    point2,
    bias1,
    bias2,
    readout,
):
    bricks = lax.axis_size("brick")
    depth = NG // lax.axis_size("slab")
    width = NG // bricks
    me = lax.axis_index("brick").astype(jnp.int32)
    mine = me.reshape(1)

    tab, *blocks = make_deposits(mine, features, tangents, stencil, stencil_table, bricks)
    blocks, point1, route, cell_local = lax.optimization_barrier(
        (blocks, point1, route, cell_local)
    )
    mix1, mix2, back2, back1, lanes = make_weights(
        point1, point2, taps1, taps2, bias1, bias2, readout
    )
    z_part = cell_local // (width * NG)
    y_part = route[:, 0] * width + (cell_local // NG) % width
    x_part = cell_local % NG
    cell = (z_part * NG + y_part) * NG + x_part

    chunks, cells = [blocks[0]], [cell]
    (sums,) = run_scatter(first_sums_kernel, "own_sums", cells, chunks, None, depth)
    for j in range(1, bricks):
        block = blocks[j]
        if j >= 3:
            chunks[j - 2], block = lax.optimization_barrier((chunks[j - 2], block))
            cells[j - 2], cell = lax.optimization_barrier((cells[j - 2], cell))
        chunks.append(swap(block, j))
        cells.append(swap(cell, j))
    (sums,) = run_scatter(more_sums_kernel, "more_sums", cells[1:-1], chunks[1:-1], sums, depth)
    _, *charge = run_scatter(charge_kernel, "charge", cells[-1:], chunks[-1:], sums, depth)

    def both(stage, consts, fields, local, halos):
        middle = run_inner(stage, consts, fields, local)
        lows = run_edge(stage, consts, fields, local, halos, 0)
        highs = run_edge(stage, consts, fields, local, halos, 1)
        return list(zip(lows, middle, highs))

    h, m, bend, slope = both("first", [lanes, mix1], [charge], [], exchange([charge]))
    rh, rm = both("second", [lanes, mix2, back2], [h, m], [], exchange([h, m]))
    (y,) = both("third", [lanes, back1], [rh, rm], [bend, slope], exchange([rh, rm]))
    ((below, above),) = exchange([y])
    (inner,) = run_inner("fourth", [lanes], [y], [])

    field = run_ends(lanes, y, (below, above), inner)
    returned = [None] * NT
    for j in (*range(NT - 1, 0, -1), 0):
        y_of = (cells[j] // NG) % NG
        spots = ((cells[j] // (NG * NG)) * HALF + y_of % HALF) * NG + cells[j] % NG
        returned[j] = swap(make_gather(spots, y_of // HALF, field), j)
    return make_output(mine, tab, returned)


def solution(mesh):
    placed = (
        P(None, ("slab", "brick")),
        P(None, None, ("slab", "brick")),
        P(("slab", "brick"), None),
        P(("slab", "brick")),
        P(("slab", "brick")),
        P(),
        P(),
        P(),
        P(),
        P(),
        P(),
        P(),
        P(),
    )
    return jax.shard_map(
        shards,
        mesh=mesh,
        in_specs=placed,
        out_specs=P(None, None, ("slab", "brick")),
        check_vma=False,
    )
```

time: 195 us -> 159 us (0.82)
  Pallas kernels: 125 us -> 106 us
  waiting for transfers between devices: 28 us -> 19.1 us
  local copies, waits for them, and re-layouts: 11 us -> 6.28 us
    pallas_call x10, Pallas kernels: 86.2 us -> 65.3 us  [call_stage(): pl.pallas_call(kernel, out_shape=[jax.ShapeDtypeStruct((layers, HALF, NG,...]
    ppermute x9, waiting for transfers between devices: 26.5 us -> 7.77 us  [swap(): return lax.ppermute(array, 'brick', [(i, i ^ j) for i in range(size)])]
    ppermute x6, starting transfers between devices: 15.2 us -> 6.28 us  [exchange(): lax.ppermute(low, 'slab', down)]
    ppermute x6, waiting for transfers between devices: 0.42 us -> 6.65 us  [exchange(): lax.ppermute(low, 'slab', down)]
    ppermute x6, starting transfers between devices: 0.45 us -> 5.68 us  [exchange(): lax.ppermute(high, 'slab', up)]
    unnamed x28, local copies, waits for them, and re-layouts: 11 us -> 6.28 us
    ppermute x6, waiting for transfers between devices: 1.07 us -> 4.72 us  [exchange(): lax.ppermute(high, 'slab', up)]
    pallas_call x2 -> x8, Pallas kernels: 36.3 us -> 37.7 us  [the longest x3 22.9 us: run_scatter(): pl.pallas_call(functools.partial(kernel, peers), out_shape=out_shape, in_...]
  transfers between devices with their start and end apart: 21 -> 21, of which waited for: 7 -> 8; matrix products, arithmetic and copies ran while one was open for 0% -> 0% of each run, Pallas kernels for 45% -> 58%
where the time goes in v3:
time: 159 us; the launch traced here: 158 us
  Pallas kernels  106 us (67%)
  starting transfers between devices  25.5 us (16%)
  waiting for transfers between devices  19.1 us (12%)
  local copies, waits for them, and re-layouts  6.28 us (4%)
    pallas_call x10, Pallas kernels, call_stage(): pl.pallas_call(kernel, out_shape=[jax.ShapeDtypeStruct((layers, HALF, NG,...  65.3 us
    pallas_call x3, Pallas kernels, run_scatter(): pl.pallas_call(functools.partial(kernel, peers), out_shape=out_shape, in_...  22.9 us
    ppermute x9, starting transfers between devices, swap(): return lax.ppermute(array, 'brick', [(i, i ^ j) for i in range(size)])  13.5 us
    pallas_call x4, Pallas kernels, make_gather(): pl.pallas_call(gather_kernel, out_shape=jax.ShapeDtypeStruct((CH, count),...  12.5 us
    ppermute x9, waiting for transfers between devices, swap(): return lax.ppermute(array, 'brick', [(i, i ^ j) for i in range(size)])  7.77 us
    ppermute x6, waiting for transfers between devices, exchange(): lax.ppermute(low, 'slab', down)  6.65 us
    ppermute x6, starting transfers between devices, exchange(): lax.ppermute(low, 'slab', down)  6.28 us
    unnamed x28, local copies, waits for them, and re-layouts  6.28 us
  transfers between devices with their start and end apart: 21, of which 8 were waited for; matrix products, arithmetic and copies ran while one was open for 0% of the time, Pallas kernels for 58%

profile of v3, /device:TPU:0, one launch (start us, length us, event | category | flops | bytes accessed | tf_op | source)
XLA Modules:
  0.0 158.5 jit_solution(7590850270326081101)
XLA Ops:
  5.9 3.0 %collective-permute-start = (s32[2048]{0:T(1024)S(1)}, s32[2048]{0:T(1024)S(1)}, u32[]{:S(2)}, u32[]{:S(2)}) collective-permute-start(s32[2048]{0:T(1024)S(1)} %get-tuple-element.60.refs_0_), channel_id=1, source_target_pairs={{0,1},{1,0},{2,3},{3,2},{4,5},{5,4},{6,7},{7,6},{8,9},{9,8},{10,11... | collective-permute-start | bytes 24584 | tf_op jit(solution)/shard_map/ppermute | solution.py:717
  8.9 1.5 collective-permute-start.4
  11.1 6.5 %own_sums.1.refs_6_ = f32[32768,128]{1,0:T(8,128)S(1)} custom-call(s32[2048]{0:T(1024)S(1)} %get-tuple-element.60.refs_0_, bf16[128,2048]{1,0:T(8,128)(2,1)S(1)} %get-tuple-element.67.refs_1_, s32[1,2048]{1,0:T(1,128)S(1)} %bitcast.16), custom_call_target="tpu_custom_call" | custom-call | flops 4000000000 | bytes 8000000 | tf_op jit(solution)/shard_map/own_sums/pallas_call | solution.py:200
  17.8 3.0 %collective-permute-start.1 = (s32[2048]{0:T(1024)S(1)}, s32[2048]{0:T(1024)S(1)}, u32[]{:S(2)}, u32[]{:S(2)}) collective-permute-start(s32[2048]{0:T(1024)S(1)} %get-tuple-element.60.refs_0_), channel_id=1, source_target_pairs={{0,3},{1,2},{2,1},{3,0},{4,7},{5,6},{6,5},{7,4},{8,11},{9,10},{10,... | collective-permute-start | bytes 24584 | tf_op jit(solution)/shard_map/ppermute | solution.py:717
  20.8 2.9 %collective-permute-done.1.refs_0_ = s32[2048]{0:T(1024)S(1)} collective-permute-done((s32[2048]{0:T(1024)S(1)}, s32[2048]{0:T(1024)S(1)}, u32[]{:S(2)}, u32[]{:S(2)}) %collective-permute-start.1) | collective-permute-done | bytes 8224 | tf_op jit(solution)/shard_map/ppermute | solution.py:717
  23.8 1.7 %collective-permute-start.3 = (bf16[128,2048]{1,0:T(8,128)(2,1)S(1)}, bf16[128,2048]{1,0:T(8,128)(2,1)S(1)}, u32[]{:S(2)}, u32[]{:S(2)}) collective-permute-start(bf16[128,2048]{1,0:T(8,128)(2,1)S(1)} %get-tuple-element.63), channel_id=1, source_target_pairs={{0,3},{1,2},{2,1},{3,0},{4,7},{5,6},{6,5},{7,4},{8,11},{9,10},{10,... | collective-permute-start | bytes 1572872 | tf_op jit(solution)/shard_map/ppermute | solution.py:717
  25.5 9.8 %more_sums.1.refs_3_ = f32[32768,128]{1,0:T(8,128)S(1)} custom-call(s32[2048]{0:T(1024)S(1)} %collective-permute-done.refs_0_, s32[2048]{0:T(1024)S(1)} %collective-permute-done.4.refs_1_, bf16[128,2048]{1,0:T(8,128)(2,1)S(1)} %collective-permute-done.2.refs_2_, ...), custom_call_target="tpu_custom_call", output_to_operand_aliasing={{}: (6, {})} | custom-call | flops 8000000000 | bytes 16000000 | tf_op jit(solution)/shard_map/more_sums/pallas_call | solution.py:200
  36.6 6.6 %charge.1 = (f32[32768,128]{1,0:T(8,128)S(1)}, bf16[1,64,64,128]{3,2,1,0:T(8,128)(2,1)S(1)}, bf16[6,64,64,128]{3,2,1,0:T(8,128)(2,1)S(1)}, bf16[1,64,64,128]{3,2,1,0:T(8,128)(2,1)S(1)}) custom-call(s32[2048]{0:T(1024)S(1)} %collective-permute-done.1.refs_0_, bf16[128,2048]{1,0:T(8,128)(2,1)S(1)} %collective-permute-done.3.refs_1_, ...), custom_call_target="tpu_custom_call", output_to_operand_aliasing={{0}: (3, {})} | custom-call | flops 4000000000 | bytes 8000000 | tf_op jit(solution)/shard_map/charge/pallas_call | solution.py:200
  43.8 14.6 %first_inner.1 = (bf16[6,32,64,128]{3,2,1,0:T(8,128)(2,1)S(1)}, bf16[6,32,64,128]{3,2,1,0:T(8,128)(2,1)S(1)}, f32[6,32,64,128]{3,2,1,0:T(8,128)S(1)}, f32[6,32,64,128]{3,2,1,0:T(8,128)S(1)}) custom-call(f32[24,128]{1,0:T(8,128)S(1)} %get-tuple-element.55.refs_0_.w_ref, bf16[256,256]{1,0:T(8,128)(2,1)S(1)} %get-tuple-element.59.refs_1_, ...), custom_call_target="tpu_custom_call" | custom-call | flops 24000000000 | bytes 36000000 | tf_op jit(solution)/shard_map/first_inner/pallas_call | solution.py:563
  58.4 2.7 %copy-done.11 = f32[6,32,64,128]{3,2,1,0:T(8,128)} copy-done((f32[6,32,64,128]{3,2,1,0:T(8,128)}, f32[6,32,64,128]{3,2,1,0:T(8,128)S(1)}, u32[]{:S(2)}) %copy-start.11) | copy-done | bytes 6291480
  61.0 5.3 %collective-permute-done.7.refs_4_ = bf16[1,64,64,128]{3,2,1,0:T(8,128)(2,1)S(1)} collective-permute-done((bf16[1,64,64,128]{3,2,1,0:T(8,128)(2,1)S(1)}, bf16[1,64,64,128]{3,2,1,0:T(8,128)(2,1)S(1)}, u32[]{:S(2)}, u32[]{:S(2)}) %collective-permute-start.7) | collective-permute-done | bytes 1048608 | tf_op jit(solution)/shard_map/ppermute | solution.py:602
  66.4 2.4 %first_high.1 = (bf16[1,32,64,128]{3,2,1,0:T(8,128)(2,1)S(1)}, bf16[1,32,64,128]{3,2,1,0:T(8,128)(2,1)S(1)}, f32[1,32,64,128]{3,2,1,0:T(8,128)S(1)}, f32[1,32,64,128]{3,2,1,0:T(8,128)S(1)}) custom-call(f32[24,128]{1,0:T(8,128)S(1)} %get-tuple-element.55.refs_0_.w_ref, bf16[256,256]{1,0:T(8,128)(2,1)S(1)} %get-tuple-element.59.refs_1_, ...), custom_call_target="tpu_custom_call" | custom-call | flops 4000000000 | bytes 6000000 | tf_op jit(solution)/shard_map/first_high/pallas_call | solution.py:563
  70.8 2.4 %first_low.1 = (bf16[1,32,64,128]{3,2,1,0:T(8,128)(2,1)S(1)}, bf16[1,32,64,128]{3,2,1,0:T(8,128)(2,1)S(1)}, f32[1,32,64,128]{3,2,1,0:T(8,128)S(1)}, f32[1,32,64,128]{3,2,1,0:T(8,128)S(1)}) custom-call(f32[24,128]{1,0:T(8,128)S(1)} %get-tuple-element.55.refs_0_.w_ref, bf16[256,256]{1,0:T(8,128)(2,1)S(1)} %get-tuple-element.59.refs_1_, ...), custom_call_target="tpu_custom_call" | custom-call | flops 4000000000 | bytes 6000000 | tf_op jit(solution)/shard_map/first_low/pallas_call | solution.py:563
  73.2 2.4 %collective-permute-start.8 = (bf16[1,32,64,128]{3,2,1,0:T(8,128)(2,1)S(1)}, bf16[1,32,64,128]{3,2,1,0:T(8,128)(2,1)S(1)}, u32[]{:S(2)}, u32[]{:S(2)}) collective-permute-start(bf16[1,32,64,128]{3,2,1,0:T(8,128)(2,1)S(1)} %get-tuple-element.71.refs_3_.refs_4_), channel_id=1, source_target_pairs={{4,0},{8,4},{12,8},{16,12},{20,16},{24,20},{28,24},{0,28},{5,1},{9... | collective-permute-start | bytes 1572872 | tf_op jit(solution)/shard_map/ppermute | solution.py:602
  75.6 17.5 %second_inner.1 = (bf16[6,32,64,128]{3,2,1,0:T(8,128)(2,1)S(1)}, bf16[6,32,64,128]{3,2,1,0:T(8,128)(2,1)S(1)}) custom-call(f32[24,128]{1,0:T(8,128)S(1)} %get-tuple-element.55.refs_0_.w_ref, bf16[256,256]{1,0:T(8,128)(2,1)S(1)} %get-tuple-element.57.refs_1_, bf16[256,256]{1,0:T(8,128)(2,1)S(1)} %get-tuple-element.58.refs_2_, ...), custom_call_target="tpu_custom_call" | custom-call | flops 24000000000 | bytes 36000000 | tf_op jit(solution)/shard_map/second_inner/pallas_call | solution.py:563
  93.1 2.9 %second_high.1 = (bf16[1,32,64,128]{3,2,1,0:T(8,128)(2,1)S(1)}, bf16[1,32,64,128]{3,2,1,0:T(8,128)(2,1)S(1)}) custom-call(f32[24,128]{1,0:T(8,128)S(1)} %get-tuple-element.55.refs_0_.w_ref, bf16[256,256]{1,0:T(8,128)(2,1)S(1)} %get-tuple-element.57.refs_1_, bf16[256,256]{1,0:T(8,128)(2,1)S(1)} %get-tuple-element.58.refs_2_, ...), custom_call_target="tpu_custom_call" | custom-call | flops 4000000000 | bytes 6000000 | tf_op jit(solution)/shard_map/second_high/pallas_call | solution.py:563
  96.0 3.0 %collective-permute-start.15 = (bf16[1,32,64,128]{3,2,1,0:T(8,128)(2,1)S(1)}, bf16[1,32,64,128]{3,2,1,0:T(8,128)(2,1)S(1)}, u32[]{:S(2)}, u32[]{:S(2)}) collective-permute-start(bf16[1,32,64,128]{3,2,1,0:T(8,128)(2,1)S(1)} %get-tuple-element.78.refs_3_.refs_4_), channel_id=1, source_target_pairs={{0,4},{4,8},{8,12},{12,16},{16,20},{20,24},{24,28},{28,0},{1,5},{5... | collective-permute-start | bytes 1572872 | tf_op jit(solution)/shard_map/ppermute | solution.py:602
  99.3 2.9 %second_low.1 = (bf16[1,32,64,128]{3,2,1,0:T(8,128)(2,1)S(1)}, bf16[1,32,64,128]{3,2,1,0:T(8,128)(2,1)S(1)}) custom-call(f32[24,128]{1,0:T(8,128)S(1)} %get-tuple-element.55.refs_0_.w_ref, bf16[256,256]{1,0:T(8,128)(2,1)S(1)} %get-tuple-element.57.refs_1_, bf16[256,256]{1,0:T(8,128)(2,1)S(1)} %get-tuple-element.58.refs_2_, ...), custom_call_target="tpu_custom_call" | custom-call | flops 4000000000 | bytes 6000000 | tf_op jit(solution)/shard_map/second_low/pallas_call | solution.py:563
  102.1 3.3 %collective-permute-start.12 = (bf16[1,32,64,128]{3,2,1,0:T(8,128)(2,1)S(1)}, bf16[1,32,64,128]{3,2,1,0:T(8,128)(2,1)S(1)}, u32[]{:S(2)}, u32[]{:S(2)}) collective-permute-start(bf16[1,32,64,128]{3,2,1,0:T(8,128)(2,1)S(1)} %get-tuple-element.79.refs_3_.refs_2_), channel_id=1, source_target_pairs={{4,0},{8,4},{12,8},{16,12},{20,16},{24,20},{28,24},{0,28},{5,1},{9... | collective-permute-start | bytes 1572872 | tf_op jit(solution)/shard_map/ppermute | solution.py:602
  105.5 12.8 %third_inner.1.refs_2_.mid_ref = bf16[6,32,64,128]{3,2,1,0:T(8,128)(2,1)S(1)} custom-call(f32[24,128]{1,0:T(8,128)S(1)} %get-tuple-element.55.refs_0_.w_ref, bf16[128,128]{1,0:T(8,128)(2,1)S(1)} %get-tuple-element.56.refs_1_, bf16[1,32,64,128]{3,2,1,0:T(8,128)(2,1)S(1)} %get-tuple-element.79.refs_3_.refs_2_, ...), custom_call_target="tpu_custom_call" | custom-call | flops 24000000000 | bytes 36000000 | tf_op jit(solution)/shard_map/third_inner/pallas_call | solution.py:563
  118.4 2.1 %third_low.1.refs_1_.low_ref = bf16[1,32,64,128]{3,2,1,0:T(8,128)(2,1)S(1)} custom-call(f32[24,128]{1,0:T(8,128)S(1)} %get-tuple-element.55.refs_0_.w_ref, bf16[128,128]{1,0:T(8,128)(2,1)S(1)} %get-tuple-element.56.refs_1_, bf16[1,32,64,128]{3,2,1,0:T(8,128)(2,1)S(1)} %collective-permute-done.15.refs_2_, ...), custom_call_target="tpu_custom_call" | custom-call | flops 4000000000 | bytes 6000000 | tf_op jit(solution)/shard_map/third_low/pallas_call | solution.py:563
  121.9 2.1 %third_high.1.refs_3_.high_ref = bf16[1,32,64,128]{3,2,1,0:T(8,128)(2,1)S(1)} custom-call(f32[24,128]{1,0:T(8,128)S(1)} %get-tuple-element.55.refs_0_.w_ref, bf16[128,128]{1,0:T(8,128)(2,1)S(1)} %get-tuple-element.56.refs_1_, bf16[6,32,64,128]{3,2,1,0:T(8,128)(2,1)S(1)} %get-tuple-element.77.refs_2_.refs_4_.refs_3_, ...), custom_call_target="tpu_custom_call" | custom-call | flops 4000000000 | bytes 6000000 | tf_op jit(solution)/shard_map/third_high/pallas_call | solution.py:563
  125.4 5.8 %fourth_inner.1 = f32[6,32,64,128]{3,2,1,0:T(8,128)S(1)} custom-call(f32[24,128]{1,0:T(8,128)S(1)} %get-tuple-element.55.refs_0_.w_ref, bf16[1,32,64,128]{3,2,1,0:T(8,128)(2,1)S(1)} %third_low.1.refs_1_.low_ref, bf16[6,32,64,128]{3,2,1,0:T(8,128)(2,1)S(1)} %third_inner.1.refs_2_.mid_ref, bf16[1,32,64,128]{3,2,1,0:T(8,128)(2,1)S(1)} %third_high.1.refs_3_.high_ref), custom_call_target="tpu_custom_call" | custom-call | flops 24000000000 | bytes 36000000 | tf_op jit(solution)/shard_map/fourth_inner/pallas_call | solution.py:563
  131.2 3.5 %collective-permute-done.14.below_ref = bf16[1,32,64,128]{3,2,1,0:T(8,128)(2,1)S(1)} collective-permute-done((bf16[1,32,64,128]{3,2,1,0:T(8,128)(2,1)S(1)}, bf16[1,32,64,128]{3,2,1,0:T(8,128)(2,1)S(1)}, u32[]{:S(2)}, u32[]{:S(2)}) %collective-permute-start.14) | collective-permute-done | bytes 524320 | tf_op jit(solution)/shard_map/ppermute | solution.py:602
  134.7 2.3 %ends.1.f_ref = f32[16384,128]{1,0:T(8,128)S(1)} custom-call(f32[24,128]{1,0:T(8,128)S(1)} %get-tuple-element.55.refs_0_.w_ref, bf16[1,32,64,128]{3,2,1,0:T(8,128)(2,1)S(1)} %collective-permute-done.14.below_ref, bf16[1,32,64,128]{3,2,1,0:T(8,128)(2,1)S(1)} %third_low.1.refs_1_.low_ref, bf16[6,32,64,128]{3,2,1,0:T(8,128)(2,1)S(1)} %third_inner.1.refs_2_.mid_ref, ...), custom_call_target="tpu_custom_call" | custom-call | tf_op jit(solution)/shard_map/ends/pallas_call | solution.py:636
  137.0 3.1 %gather.7 = bf16[64,2048]{1,0:T(8,128)(2,1)S(1)} custom-call(s32[2048]{0:T(1024)S(1)} %get-tuple-element.92.spots_ref, s32[1,2048]{1,0:T(1,128)S(1)} %bitcast.23, f32[16384,128]{1,0:T(8,128)S(1)} %ends.1.f_ref), custom_call_target="tpu_custom_call" | custom-call | flops 4000000000 | bytes 6000000 | tf_op jit(solution)/shard_map/gather/pallas_call | solution.py:682
  140.2 1.6 %collective-permute-start.20 = (bf16[64,2048]{1,0:T(8,128)(2,1)S(1)}, bf16[64,2048]{1,0:T(8,128)(2,1)S(1)}, u32[]{:S(2)}, u32[]{:S(2)}) collective-permute-start(bf16[64,2048]{1,0:T(8,128)(2,1)S(1)} %gather.7), channel_id=1, source_target_pairs={{0,3},{1,2},{2,1},{3,0},{4,7},{5,6},{6,5},{7,4},{8,11},{9,10},{10,... | collective-permute-start | bytes 786440 | tf_op jit(solution)/shard_map/ppermute | solution.py:717
  141.8 3.1 %gather.6 = bf16[64,2048]{1,0:T(8,128)(2,1)S(1)} custom-call(s32[2048]{0:T(1024)S(1)} %get-tuple-element.94.spots_ref, s32[1,2048]{1,0:T(1,128)S(1)} %bitcast.22, f32[16384,128]{1,0:T(8,128)S(1)} %ends.1.f_ref), custom_call_target="tpu_custom_call" | custom-call | flops 4000000000 | bytes 6000000 | tf_op jit(solution)/shard_map/gather/pallas_call | solution.py:682
  145.6 3.1 %gather.5 = bf16[64,2048]{1,0:T(8,128)(2,1)S(1)} custom-call(s32[2048]{0:T(1024)S(1)} %get-tuple-element.96.spots_ref, s32[1,2048]{1,0:T(1,128)S(1)} %bitcast.21, f32[16384,128]{1,0:T(8,128)S(1)} %ends.1.f_ref), custom_call_target="tpu_custom_call" | custom-call | flops 4000000000 | bytes 6000000 | tf_op jit(solution)/shard_map/gather/pallas_call | solution.py:682
  150.2 3.1 %gather.4.refs_0_ = bf16[64,2048]{1,0:T(8,128)(2,1)S(1)} custom-call(s32[2048]{0:T(1024)S(1)} %fusion.11.spots_ref, s32[1,2048]{1,0:T(1,128)S(1)} %bitcast.24, f32[16384,128]{1,0:T(8,128)S(1)} %ends.1.f_ref), custom_call_target="tpu_custom_call" | custom-call | flops 4000000000 | bytes 6000000 | tf_op jit(solution)/shard_map/gather/pallas_call | solution.py:682
  153.3 2.2 %collective-permute-done.19.refs_2_ = bf16[64,2048]{1,0:T(8,128)(2,1)S(1)} collective-permute-done((bf16[64,2048]{1,0:T(8,128)(2,1)S(1)}, bf16[64,2048]{1,0:T(8,128)(2,1)S(1)}, u32[]{:S(2)}, u32[]{:S(2)}) %collective-permute-start.19) | collective-permute-done | bytes 262176 | tf_op jit(solution)/shard_map/ppermute | solution.py:717
  156.9 1.6 finish.1
  (66 shorter events, 17.3 us)
Async XLA Ops:
  0.0 1.2 copy-start
  5.9 11.9 %collective-permute-start = (s32[2048]{0:T(1024)S(1)}, s32[2048]{0:T(1024)S(1)}, u32[]{:S(2)}, u32[]{:S(2)}) collective-permute-start(s32[2048]{0:T(1024)S(1)} %get-tuple-element.60.refs_0_), channel_id=1, source_target_pairs={{0,1},{1,0},{2,3},{3,2},{4,5},{5,4},{6,7},{7,6},{8,9},{9,8},{10,11... | collective-permute-start | bytes 24584 | tf_op jit(solution)/shard_map/ppermute | solution.py:717
  8.9 11.9 %collective-permute-start.4 = (s32[2048]{0:T(1024)S(1)}, s32[2048]{0:T(1024)S(1)}, u32[]{:S(2)}, u32[]{:S(2)}) collective-permute-start(s32[2048]{0:T(1024)S(1)} %get-tuple-element.60.refs_0_), channel_id=1, source_target_pairs={{0,2},{1,3},{2,0},{3,1},{4,6},{5,7},{6,4},{7,5},{8,10},{9,11},{10,... | collective-permute-start | bytes 24584 | tf_op jit(solution)/shard_map/ppermute | solution.py:717
  10.4 13.4 %collective-permute-start.2 = (bf16[128,2048]{1,0:T(8,128)(2,1)S(1)}, bf16[128,2048]{1,0:T(8,128)(2,1)S(1)}, u32[]{:S(2)}, u32[]{:S(2)}) collective-permute-start(bf16[128,2048]{1,0:T(8,128)(2,1)S(1)} %get-tuple-element.61), channel_id=1, source_target_pairs={{0,1},{1,0},{2,3},{3,2},{4,5},{5,4},{6,7},{7,6},{8,9},{9,8},{10,11... | collective-permute-start | bytes 1572872 | tf_op jit(solution)/shard_map/ppermute | solution.py:717
  11.0 14.6 %collective-permute-start.5 = (bf16[128,2048]{1,0:T(8,128)(2,1)S(1)}, bf16[128,2048]{1,0:T(8,128)(2,1)S(1)}, u32[]{:S(2)}, u32[]{:S(2)}) collective-permute-start(bf16[128,2048]{1,0:T(8,128)(2,1)S(1)} %get-tuple-element.66), channel_id=1, source_target_pairs={{0,2},{1,3},{2,0},{3,1},{4,6},{5,7},{6,4},{7,5},{8,10},{9,11},{10,... | collective-permute-start | bytes 1572872 | tf_op jit(solution)/shard_map/ppermute | solution.py:717
  11.0 6.5 %copy-start.2 = (bf16[64,64]{1,0:T(8,128)(2,1)S(1)}, bf16[64,64]{1,0:T(8,128)(2,1)}, u32[]{:S(2)}) copy-start(bf16[64,64]{1,0:T(8,128)(2,1)} %p1_ref) | copy-start | bytes 24580
  11.0 6.6 %copy-start.3 = (bf16[64,64]{1,0:T(8,128)(2,1)S(1)}, bf16[64,64]{1,0:T(8,128)(2,1)}, u32[]{:S(2)}) copy-start(bf16[64,64]{1,0:T(8,128)(2,1)} %p2_ref.1) | copy-start | bytes 24580
  11.0 6.6 %copy-start.5 = (f32[3,3,64]{2,1,0:T(4,128)S(1)}, f32[3,3,64]{2,1,0:T(4,128)}, u32[]{:S(2)}) copy-start(f32[3,3,64]{2,1,0:T(4,128)} %t1_ref.1) | copy-start | bytes 6916
  11.0 6.6 %copy-start.6 = (f32[3,3,64]{2,1,0:T(4,128)S(1)}, f32[3,3,64]{2,1,0:T(4,128)}, u32[]{:S(2)}) copy-start(f32[3,3,64]{2,1,0:T(4,128)} %t2_ref.1) | copy-start | bytes 6916
  11.0 6.6 %copy-start.8 = (f32[64]{0:T(128)S(1)}, f32[64]{0:T(128)}, u32[]{:S(2)}) copy-start(f32[64]{0:T(128)} %param.23) | copy-start | bytes 772
  11.0 6.6 %copy-start.9 = (f32[64]{0:T(128)S(1)}, f32[64]{0:T(128)}, u32[]{:S(2)}) copy-start(f32[64]{0:T(128)} %param.24) | copy-start | bytes 772
  11.0 6.6 %copy-start.10 = (f32[64]{0:T(128)S(1)}, f32[64]{0:T(128)}, u32[]{:S(2)}) copy-start(f32[64]{0:T(128)} %param.25) | copy-start | bytes 772
  17.8 5.9 %collective-permute-start.1 = (s32[2048]{0:T(1024)S(1)}, s32[2048]{0:T(1024)S(1)}, u32[]{:S(2)}, u32[]{:S(2)}) collective-permute-start(s32[2048]{0:T(1024)S(1)} %get-tuple-element.60.refs_0_), channel_id=1, source_target_pairs={{0,3},{1,2},{2,1},{3,0},{4,7},{5,6},{6,5},{7,4},{8,11},{9,10},{10,... | collective-permute-start | bytes 24584 | tf_op jit(solution)/shard_map/ppermute | solution.py:717
  23.8 12.8 %collective-permute-start.3 = (bf16[128,2048]{1,0:T(8,128)(2,1)S(1)}, bf16[128,2048]{1,0:T(8,128)(2,1)S(1)}, u32[]{:S(2)}, u32[]{:S(2)}) collective-permute-start(bf16[128,2048]{1,0:T(8,128)(2,1)S(1)} %get-tuple-element.63), channel_id=1, source_target_pairs={{0,3},{1,2},{2,1},{3,0},{4,7},{5,6},{6,5},{7,4},{8,11},{9,10},{10,... | collective-permute-start | bytes 1572872 | tf_op jit(solution)/shard_map/ppermute | solution.py:717
  43.2 23.2 %collective-permute-start.7 = (bf16[1,64,64,128]{3,2,1,0:T(8,128)(2,1)S(1)}, bf16[1,64,64,128]{3,2,1,0:T(8,128)(2,1)S(1)}, u32[]{:S(2)}, u32[]{:S(2)}) collective-permute-start(bf16[1,64,64,128]{3,2,1,0:T(8,128)(2,1)S(1)} %get-tuple-element.69.refs_3_.refs_2_), channel_id=1, source_target_pairs={{4,0},{8,4},{12,8},{16,12},{20,16},{24,20},{28,24},{0,28},{5,1},{9... | collective-permute-start | bytes 3145736 | tf_op jit(solution)/shard_map/ppermute | solution.py:602
  43.6 27.2 %collective-permute-start.6 = (bf16[1,64,64,128]{3,2,1,0:T(8,128)(2,1)S(1)}, bf16[1,64,64,128]{3,2,1,0:T(8,128)(2,1)S(1)}, u32[]{:S(2)}, u32[]{:S(2)}) collective-permute-start(bf16[1,64,64,128]{3,2,1,0:T(8,128)(2,1)S(1)} %get-tuple-element.68.refs_4_.refs_3_), channel_id=1, source_target_pairs={{0,4},{4,8},{8,12},{12,16},{16,20},{20,24},{24,28},{28,0},{1,5},{5... | collective-permute-start | bytes 3145736 | tf_op jit(solution)/shard_map/ppermute | solution.py:602
  58.3 2.7 %copy-start.11 = (f32[6,32,64,128]{3,2,1,0:T(8,128)}, f32[6,32,64,128]{3,2,1,0:T(8,128)S(1)}, u32[]{:S(2)}) copy-start(f32[6,32,64,128]{3,2,1,0:T(8,128)S(1)} %get-tuple-element.88.refs_9_) | copy-start | bytes 18874372
  68.8 30.5 %collective-permute-start.10 = (bf16[1,32,64,128]{3,2,1,0:T(8,128)(2,1)S(1)}, bf16[1,32,64,128]{3,2,1,0:T(8,128)(2,1)S(1)}, u32[]{:S(2)}, u32[]{:S(2)}) collective-permute-start(bf16[1,32,64,128]{3,2,1,0:T(8,128)(2,1)S(1)} %get-tuple-element.73.refs_5_.refs_4_), channel_id=1, source_target_pairs={{0,4},{4,8},{8,12},{12,16},{16,20},{20,24},{24,28},{28,0},{1,5},{5... | collective-permute-start | bytes 1572872 | tf_op jit(solution)/shard_map/ppermute | solution.py:602
  69.5 29.7 %collective-permute-start.11 = (bf16[1,32,64,128]{3,2,1,0:T(8,128)(2,1)S(1)}, bf16[1,32,64,128]{3,2,1,0:T(8,128)(2,1)S(1)}, u32[]{:S(2)}, u32[]{:S(2)}) collective-permute-start(bf16[1,32,64,128]{3,2,1,0:T(8,128)(2,1)S(1)} %get-tuple-element.76.refs_8_.refs_7_), channel_id=1, source_target_pairs={{0,4},{4,8},{8,12},{12,16},{16,20},{20,24},{24,28},{28,0},{1,5},{5... | collective-permute-start | bytes 1572872 | tf_op jit(solution)/shard_map/ppermute | solution.py:602
  73.2 20.0 %collective-permute-start.8 = (bf16[1,32,64,128]{3,2,1,0:T(8,128)(2,1)S(1)}, bf16[1,32,64,128]{3,2,1,0:T(8,128)(2,1)S(1)}, u32[]{:S(2)}, u32[]{:S(2)}) collective-permute-start(bf16[1,32,64,128]{3,2,1,0:T(8,128)(2,1)S(1)} %get-tuple-element.71.refs_3_.refs_4_), channel_id=1, source_target_pairs={{4,0},{8,4},{12,8},{16,12},{20,16},{24,20},{28,24},{0,28},{5,1},{9... | collective-permute-start | bytes 1572872 | tf_op jit(solution)/shard_map/ppermute | solution.py:602
  75.5 17.6 %collective-permute-start.9 = (bf16[1,32,64,128]{3,2,1,0:T(8,128)(2,1)S(1)}, bf16[1,32,64,128]{3,2,1,0:T(8,128)(2,1)S(1)}, u32[]{:S(2)}, u32[]{:S(2)}) collective-permute-start(bf16[1,32,64,128]{3,2,1,0:T(8,128)(2,1)S(1)} %get-tuple-element.74.refs_6_.refs_7_), channel_id=1, source_target_pairs={{4,0},{8,4},{12,8},{16,12},{20,16},{24,20},{28,24},{0,28},{5,1},{9... | collective-permute-start | bytes 1572872 | tf_op jit(solution)/shard_map/ppermute | solution.py:602
  96.0 22.3 %collective-permute-start.15 = (bf16[1,32,64,128]{3,2,1,0:T(8,128)(2,1)S(1)}, bf16[1,32,64,128]{3,2,1,0:T(8,128)(2,1)S(1)}, u32[]{:S(2)}, u32[]{:S(2)}) collective-permute-start(bf16[1,32,64,128]{3,2,1,0:T(8,128)(2,1)S(1)} %get-tuple-element.78.refs_3_.refs_4_), channel_id=1, source_target_pairs={{0,4},{4,8},{8,12},{12,16},{16,20},{20,24},{24,28},{28,0},{1,5},{5... | collective-permute-start | bytes 1572872 | tf_op jit(solution)/shard_map/ppermute | solution.py:602
  99.0 6.5 %slice-start = ((s8[6291456]{0:T(1024)(128)(4,1)}), s8[4194304]{0:T(1024)(128)(4,1)S(1)}, s32[]{:S(2)}) async-start(s8[6291456]{0:T(1024)(128)(4,1)} %bitcast.28), calls=%async_computation | async-start | bytes 8388608
  99.0 6.5 %slice-start.1 = ((s8[6291456]{0:T(1024)(128)(4,1)}), s8[2097152]{0:T(1024)(128)(4,1)S(1)}, s32[]{:S(2)}) async-start(s8[6291456]{0:T(1024)(128)(4,1)} %bitcast.28), calls=%async_computation.1 | async-start | bytes 4194304
  99.0 19.4 %collective-permute-start.16 = (bf16[1,32,64,128]{3,2,1,0:T(8,128)(2,1)S(1)}, bf16[1,32,64,128]{3,2,1,0:T(8,128)(2,1)S(1)}, u32[]{:S(2)}, u32[]{:S(2)}) collective-permute-start(bf16[1,32,64,128]{3,2,1,0:T(8,128)(2,1)S(1)} %get-tuple-element.81.refs_6_.refs_7_), channel_id=1, source_target_pairs={{0,4},{4,8},{8,12},{12,16},{16,20},{20,24},{24,28},{28,0},{1,5},{5... | collective-permute-start | bytes 1572872 | tf_op jit(solution)/shard_map/ppermute | solution.py:602
  102.1 18.4 %collective-permute-start.12 = (bf16[1,32,64,128]{3,2,1,0:T(8,128)(2,1)S(1)}, bf16[1,32,64,128]{3,2,1,0:T(8,128)(2,1)S(1)}, u32[]{:S(2)}, u32[]{:S(2)}) collective-permute-start(bf16[1,32,64,128]{3,2,1,0:T(8,128)(2,1)S(1)} %get-tuple-element.79.refs_3_.refs_2_), channel_id=1, source_target_pairs={{4,0},{8,4},{12,8},{16,12},{20,16},{24,20},{28,24},{0,28},{5,1},{9... | collective-permute-start | bytes 1572872 | tf_op jit(solution)/shard_map/ppermute | solution.py:602
  105.5 16.4 %collective-permute-start.13 = (bf16[1,32,64,128]{3,2,1,0:T(8,128)(2,1)S(1)}, bf16[1,32,64,128]{3,2,1,0:T(8,128)(2,1)S(1)}, u32[]{:S(2)}, u32[]{:S(2)}) collective-permute-start(bf16[1,32,64,128]{3,2,1,0:T(8,128)(2,1)S(1)} %get-tuple-element.82.refs_6_.refs_5_), channel_id=1, source_target_pairs={{4,0},{8,4},{12,8},{16,12},{20,16},{24,20},{28,24},{0,28},{5,1},{9... | collective-permute-start | bytes 1572872 | tf_op jit(solution)/shard_map/ppermute | solution.py:602
  120.5 10.7 %collective-permute-start.17 = (bf16[1,32,64,128]{3,2,1,0:T(8,128)(2,1)S(1)}, bf16[1,32,64,128]{3,2,1,0:T(8,128)(2,1)S(1)}, u32[]{:S(2)}, u32[]{:S(2)}) collective-permute-start(bf16[1,32,64,128]{3,2,1,0:T(8,128)(2,1)S(1)} %third_low.1.refs_1_.low_ref), channel_id=1, source_target_pairs={{4,0},{8,4},{12,8},{16,12},{20,16},{24,20},{28,24},{0,28},{5,1},{9... | collective-permute-start | bytes 1572872 | tf_op jit(solution)/shard_map/ppermute | solution.py:602
  124.0 10.7 %collective-permute-start.14 = (bf16[1,32,64,128]{3,2,1,0:T(8,128)(2,1)S(1)}, bf16[1,32,64,128]{3,2,1,0:T(8,128)(2,1)S(1)}, u32[]{:S(2)}, u32[]{:S(2)}) collective-permute-start(bf16[1,32,64,128]{3,2,1,0:T(8,128)(2,1)S(1)} %third_high.1.refs_3_.high_ref), channel_id=1, source_target_pairs={{0,4},{4,8},{8,12},{12,16},{16,20},{20,24},{24,28},{28,0},{1,5},{5... | collective-permute-start | bytes 1572872 | tf_op jit(solution)/shard_map/ppermute | solution.py:602
  140.2 13.1 %collective-permute-start.20 = (bf16[64,2048]{1,0:T(8,128)(2,1)S(1)}, bf16[64,2048]{1,0:T(8,128)(2,1)S(1)}, u32[]{:S(2)}, u32[]{:S(2)}) collective-permute-start(bf16[64,2048]{1,0:T(8,128)(2,1)S(1)} %gather.7), channel_id=1, source_target_pairs={{0,3},{1,2},{2,1},{3,0},{4,7},{5,6},{6,5},{7,4},{8,11},{9,10},{10,... | collective-permute-start | bytes 786440 | tf_op jit(solution)/shard_map/ppermute | solution.py:717
  144.9 10.5 %collective-permute-start.19 = (bf16[64,2048]{1,0:T(8,128)(2,1)S(1)}, bf16[64,2048]{1,0:T(8,128)(2,1)S(1)}, u32[]{:S(2)}, u32[]{:S(2)}) collective-permute-start(bf16[64,2048]{1,0:T(8,128)(2,1)S(1)} %gather.6), channel_id=1, source_target_pairs={{0,2},{1,3},{2,0},{3,1},{4,6},{5,7},{6,4},{7,5},{8,10},{9,11},{10,... | collective-permute-start | bytes 786440 | tf_op jit(solution)/shard_map/ppermute | solution.py:717
  148.7 8.2 %collective-permute-start.18 = (bf16[64,2048]{1,0:T(8,128)(2,1)S(1)}, bf16[64,2048]{1,0:T(8,128)(2,1)S(1)}, u32[]{:S(2)}, u32[]{:S(2)}) collective-permute-start(bf16[64,2048]{1,0:T(8,128)(2,1)S(1)} %gather.5), channel_id=1, source_target_pairs={{0,1},{1,0},{2,3},{3,2},{4,5},{5,4},{6,7},{7,6},{8,9},{9,8},{10,11... | collective-permute-start | bytes 786440 | tf_op jit(solution)/shard_map/ppermute | solution.py:717
  (3 other events, 2.3 us)

commit v4 on v3

--- a/solution.py
+++ b/solution.py
@@ -38,15 +38,20 @@
     return pl.BlockSpec(memory_space=pltpu.SMEM)
 
 
-def deposits_kernel(peers, me_ref, feat_ref, tan_ref, sten_ref, table_ref, tab_ref, *refs):
-    outs = refs[:peers]
-    feat, tan, sten, rows, sems, small = refs[peers:]
+def deposits_kernel(peers, width, me_ref, feat_ref, tan_ref, sten_ref, table_ref, route_ref, local_ref, *refs):
+    tab_ref, cell_ref = refs[:2]
+    outs = refs[2 : peers + 2]
+    feat, tan, sten, rows, route, local, sems, small = refs[peers + 2 :]
     me = me_ref[0]
     parts, _, step = feat.shape
-    kinds_copy = pltpu.make_async_copy(sten_ref, sten, small.at[0])
-    table_copy = pltpu.make_async_copy(table_ref, rows, small.at[1])
-    kinds_copy.start()
-    table_copy.start()
+    lists = [
+        pltpu.make_async_copy(far, near, small.at[n])
+        for n, (far, near) in enumerate(
+            ((sten_ref, sten), (table_ref, rows), (route_ref, route), (local_ref, local))
+        )
+    ]
+    for copy in lists:
+        copy.start()
     copies = []
     for p in range(parts):
         at = pl.ds(p * step, step)
@@ -57,8 +62,12 @@
         for copy in pair:
             copy.start()
         copies.append(pair)
-    kinds_copy.wait()
-    table_copy.wait()
+    for copy in lists:
+        copy.wait()
+    place = local[...]
+    z_part = lax.shift_right_logical(place, (width * NG).bit_length() - 1)
+    y_part = lax.shift_right_logical(place, NG.bit_length() - 1) & (width - 1)
+    cell_ref[...] = (z_part * NG + route[...] * width + y_part) * NG + (place & (NG - 1))
     table = rows[...].T
     for p in range(parts):
         at = pl.ds(p * step, step)
@@ -76,29 +85,33 @@
             outs[j][CH:, at] = (own.astype(F32) * tab).astype(BF16)
 
 
-def make_deposits(me, features, tangents, stencil, table, peers):
+def make_deposits(me, features, tangents, stencil, table, route, local, peers):
     count = features.shape[1]
     step = min(512, count)
     parts = count // step
     far = pl.BlockSpec(memory_space=pltpu.HBM)
-    out_shape = [jax.ShapeDtypeStruct((CH, count), F32)]
+    row = jax.ShapeDtypeStruct((1, count), jnp.int32)
+    out_shape = [jax.ShapeDtypeStruct((CH, count), F32), row]
     out_shape += [jax.ShapeDtypeStruct((LANES, count), BF16)] * peers
+    near_row = pltpu.VMEM((1, count), jnp.int32)
     return pl.pallas_call(
-        functools.partial(deposits_kernel, peers),
+        functools.partial(deposits_kernel, peers, NG // peers),
         out_shape=out_shape,
-        in_specs=[smem()] + [far] * 4,
-        out_specs=[vmem()] * (peers + 1),
+        in_specs=[smem()] + [far] * 6,
+        out_specs=[vmem()] * (peers + 2),
         scratch_shapes=[
             pltpu.VMEM((parts, CH, step), BF16),
             pltpu.VMEM((parts, NT, CH, step), BF16),
-            pltpu.VMEM((1, count), jnp.int32),
+            near_row,
             pltpu.VMEM(table.shape, F32),
+            near_row,
+            near_row,
             pltpu.SemaphoreType.DMA((parts, 2)),
-            pltpu.SemaphoreType.DMA((2,)),
+            pltpu.SemaphoreType.DMA((4,)),
         ],
-        compiler_params=params(8),
+        compiler_params=params(63),
         name="deposits",
-    )(me, features, tangents, stencil.reshape(1, count), table)
+    )(me, features, tangents, stencil.reshape(1, count), table, route.reshape(1, count), local.reshape(1, count))
 
 
 def clear(ref):
@@ -160,28 +173,41 @@
     scatter(cells, chunks, marks, sums_ref, rows_ref, early_ref)
 
 
+def round_layer(sums_ref, layer, out_ref, index):
+    def body(y, carry):
+        at = pl.ds(pl.multiple_of((layer * NG + y) * NG, NG), NG)
+        out_ref[index, y] = sums_ref[at, :].astype(BF16)
+        return carry
+
+    lax.fori_loop(0, NG, body, 0, unroll=4)
+
+
 def charge_kernel(peers, *refs):
     cells, chunks, marks, rest = split_scatter(peers, refs)
-    _, sums_ref, low_ref, mid_ref, high_ref, rows_ref, early_ref = rest
+    _, sums_ref, low_ref, high_ref, rows_ref, early_ref = rest
     scatter(cells, chunks, marks, sums_ref, rows_ref, early_ref)
-
-    def finish(base, out_ref, index):
-        def body(y, carry):
-            at = pl.ds(pl.multiple_of(base + y * NG, NG), NG)
-            out_ref[index, y] = sums_ref[at, :].astype(BF16)
-            return carry
-
-        lax.fori_loop(0, NG, body, 0, unroll=4)
-
-    inner = mid_ref.shape[0]
-    finish(0, low_ref, 0)
-    finish((inner + 1) * NG * NG, high_ref, 0)
-
-    def between(z, carry):
-        finish((z + 1) * NG * NG, mid_ref, z)
+    round_layer(sums_ref, 0, low_ref, 0)
+    round_layer(sums_ref, sums_ref.shape[0] // (NG * NG) - 1, high_ref, 0)
+
+
+def inner_charge_kernel(sums_ref, mid_ref):
+    def body(z, carry):
+        round_layer(sums_ref, z + 1, mid_ref, z)
         return carry
 
-    lax.fori_loop(0, inner, between, 0)
+    lax.fori_loop(0, mid_ref.shape[0], body, 0)
+
+
+def inner_charge(sums, depth):
+    return pl.pallas_call(
+        inner_charge_kernel,
+        out_shape=jax.ShapeDtypeStruct((depth - 2, NG, NG, LANES), BF16),
+        in_specs=[vmem()],
+        out_specs=vmem(),
+        compiler_params=params(4),
+        cost_estimate=cost(500_000_000, 600_000),
+        name="inner_charge",
+    )(sums)
 
 
 def run_scatter(kernel, name, cells, chunks, sums, depth):
@@ -196,7 +222,7 @@
         args.append(sums)
         specs.append(vmem())
     if kernel is charge_kernel:
-        out_shape += [jax.ShapeDtypeStruct((n, NG, NG, LANES), BF16) for n in (1, depth - 2, 1)]
+        out_shape += [jax.ShapeDtypeStruct((n, NG, NG, LANES), BF16) for n in (1, 1)]
     return pl.pallas_call(
         functools.partial(kernel, peers),
         out_shape=out_shape,
@@ -205,7 +231,7 @@
         scratch_shapes=[pltpu.VMEM((count, LANES), F32), pltpu.VMEM((width, width), F32)],
         input_output_aliases=aliases,
         compiler_params=params(6),
-        cost_estimate=cost(peers * 4_000_000_000, peers * 8_000_000),
+        cost_estimate=cost(peers * 500_000_000, peers * 800_000),
         name=name,
     )(*args)
 
@@ -360,7 +386,7 @@
 
     def turn(i, first, last):
         for n in reversed(range(first, last)):
-            steps[n](i - n)
+            steps[n](i - n, 0)
 
     for i in range(depth - 1):
         turn(i, 0, i + 1)
@@ -374,11 +400,29 @@
         turn(i, i - groups + 1, depth)
 
 
+def staggered_layer(steps, groups, layer, final):
+    depth = len(steps)
+
+    def turn(i, first):
+        for n in reversed(range(first, depth)):
+            group = jnp.maximum(i - n, 0)
+            steps[n](lax.rem(group, groups), lax.div(group, groups))
+
+    def body(i, carry):
+        turn(layer * groups + i, 0)
+        return carry
+
+    lax.fori_loop(0, groups, body, 0)
+    if final:
+        for n in range(1, depth):
+            turn(jnp.int32((layer + 1) * groups + n - 1), n)
+
+
 def part(t):
     return slice(t * NG, (t + 1) * NG)
 
 
-def first_stage(refs, u_refs, work, outs, at):
+def first_stage(refs, u_refs, work, outs):
     w_ref, mix_ref = refs
     (u_ref,) = u_refs
     v_ref, left_ref = work[:2]
@@ -386,7 +430,7 @@
     wy, wx = taps_of(w_ref, 3, False), taps_of(w_ref, 6, False)
     bias = w_ref[ROW_BIAS1 : ROW_BIAS1 + 1, :]
 
-    def taps(i):
+    def taps(i, at):
         for t in range(GROUP):
             y = i * GROUP + t
             z = y + HALF
@@ -395,7 +439,7 @@
             left_ref[part(t), :LANES] = along_x(wx, top, v_ref, 2 * t).astype(BF16)
             left_ref[part(t), LANES:] = along_x(wx, end, v_ref, 2 * t + 1).astype(BF16)
 
-    def mix(i):
+    def mix(i, at):
         mixed = jnp.dot(left_ref[...], mix_ref[...], preferred_element_type=F32)
         for t in range(GROUP):
             y = i * GROUP + t
@@ -406,10 +450,10 @@
             a_ref[at, y] = curve * tangent
             b_ref[at, y] = slope
 
-    staggered((taps, mix), HALF // GROUP)
-
-
-def second_stage(refs, u_refs, work, outs, at):
+    return taps, mix
+
+
+def second_stage(refs, u_refs, work, outs):
     w_ref, mix_ref, back_ref = refs
     uh_ref, um_ref = u_refs
     v_ref, left_ref, next_ref = work
@@ -418,7 +462,7 @@
     bias = w_ref[ROW_BIAS2 : ROW_BIAS2 + 1, :]
     scale = w_ref[ROW_SCALE : ROW_SCALE + 1, :]
 
-    def taps(i):
+    def taps(i, at):
         for t in range(GROUP):
             y = i * GROUP + t
             sh = along_x(wx, along_y(wy, uh_ref, y, y + 1, y + 2), v_ref, 2 * t)
@@ -426,22 +470,22 @@
             left_ref[part(t), :LANES] = sh.astype(BF16)
             left_ref[part(t), LANES:] = sm.astype(BF16)
 
-    def mix(i):
+    def mix(i, at):
         mixed = jnp.dot(left_ref[...], mix_ref[...], preferred_element_type=F32)
         _, slope, curve = silu_terms(mixed[:, :LANES] + bias)
         next_ref[:, :LANES] = (slope * (0.5 * scale)).astype(BF16)
         next_ref[:, LANES:] = (curve * scale * mixed[:, LANES:]).astype(BF16)
 
-    def back(i):
+    def back(i, at):
         mixed = jnp.dot(next_ref[...], back_ref[...], preferred_element_type=F32).astype(BF16)
         for t in range(GROUP):
             rh_ref[at, i * GROUP + t] = mixed[part(t), :LANES]
             rm_ref[at, i * GROUP + t] = mixed[part(t), LANES:]
 
-    staggered((taps, mix, back), HALF // GROUP)
-
-
-def third_stage(refs, u_refs, work, outs, at):
+    return taps, mix, back
+
+
+def third_stage(refs, u_refs, work, outs):
     w_ref, back_ref, a_ref, b_ref = refs
     uh_ref, um_ref = u_refs
     v_ref, left_ref = work[:2]
@@ -449,39 +493,35 @@
     wy, wx = taps_of(w_ref, 12, True), taps_of(w_ref, 15, True)
     wx_half = taps_of(w_ref, ROW_HALF, True)
 
-    def taps(i):
+    def taps(i, at):
         for t in range(GROUP):
             y = i * GROUP + t
             g = along_x(wx, along_y(wy, uh_ref, y, y + 1, y + 2), v_ref, 2 * t)
             dg = along_x(wx_half, along_y(wy, um_ref, y, y + 1, y + 2), v_ref, 2 * t + 1)
             left_ref[part(t), :LANES] = (a_ref[at, y] * g + b_ref[at, y] * dg).astype(BF16)
 
-    def back(i):
+    def back(i, at):
         mixed = jnp.dot(left_ref[:, :LANES], back_ref[...], preferred_element_type=F32)
         for t in range(GROUP):
             y_ref[at, i * GROUP + t] = mixed[part(t)].astype(BF16)
 
-    staggered((taps, back), HALF // GROUP)
-
-
-def fourth_rows(w_ref, u_ref, v_ref, put):
+    return taps, back
+
+
+def fourth_stage(refs, u_refs, work, outs):
+    (w_ref,) = refs
+    (u_ref,) = u_refs
+    v_ref = work[0]
+    (f_ref,) = outs
     wy, wx = taps_of(w_ref, 3, True), taps_of(w_ref, 6, True)
 
-    def body(i, carry):
+    def taps(i, at):
         for t in range(GROUP):
             y = i * GROUP + t
             out = along_x(wx, along_y(wy, u_ref, y, y + 1, y + 2), v_ref, t)
-            put(y, out.astype(BF16).astype(F32))
-        return carry
-
-    lax.fori_loop(0, HALF // GROUP, body, 0)
-
-
-def fourth_stage(refs, u_refs, work, outs, at):
-    def put(y, row):
-        outs[0][at, y] = row
-
-    fourth_rows(refs[0], u_refs[0], work[0], put)
+            f_ref[at, y] = out.astype(BF16).astype(F32)
+
+    return (taps,)
 
 
 STAGES = {
@@ -514,23 +554,26 @@
     offset = 0 if rows == NG else 1
     wz = taps_of(consts[0], start, flip)
     inner = fields[0][1].shape[0]
-
-    def layer(step, which, index):
+    if stage == "fourth":
+        outs = [outs[0].at[pl.ds(1, inner)]]
+    steps = body(consts + local, u_refs, work, outs)
+
+    def layer(step, which, index, final):
         for field, u_ref, ring_ref in zip(fields, u_refs, ring_refs):
             along_z_ring(wz, (field[which], index), step, ring_ref, u_ref, rows, offset)
             if offset:
                 wrap_halves(u_ref)
-        body(consts + local, u_refs, work, outs, step - 2)
+        staggered_layer(steps, HALF // GROUP, step - 2, final)
 
     def loop(step, carry):
-        layer(step, 1, step - 1)
+        layer(step, 1, step - 1, False)
         return carry
 
     for (low_ref, mid_ref, _), ring_ref in zip(fields, ring_refs):
         keep_layer((low_ref, 0), 0, ring_ref, rows)
         keep_layer((mid_ref, 0), 1, ring_ref, rows)
     lax.fori_loop(2, inner + 1, loop, 0)
-    layer(inner + 1, 2, 0)
+    layer(inner + 1, 2, 0, True)
 
 
 def edge_kernel(stage, n_const, n_field, n_local, places, *refs):
@@ -546,7 +589,7 @@
         along_z(wz, list(zip(field, places)), u_ref, rows, offset)
         if offset:
             wrap_halves(u_ref)
-    body(consts + local, u_refs, work, outs, 0)
+    staggered(body(consts + local, u_refs, work, outs), HALF // GROUP)
 
 
 def field_scratch(stage, n_field, ring):
@@ -577,12 +620,14 @@
     args = [*consts, *[ref for field in fields for ref in field], *[x[1] for x in local]]
     scratch = field_scratch(stage, len(fields), True)
     layers = fields[0][1].shape[0]
+    if stage == "fourth":
+        layers += 2
     return call_stage(kernel, stage + "_inner", layers, 16, STAGES[stage][2], args, scratch)
 
 
 def run_edge(stage, consts, fields, local, halos, side):
-    inner = fields[0][1].shape[0]
-    around, places = [], (0, 0, 0) if side == 0 else (inner - 1, 0, 0)
+    last = fields[0][1].shape[0] - 1
+    around, places = [], (0, 0, 0) if side == 0 else (last, 0, 0)
     for (low, mid, high), (below, above) in zip(fields, halos):
         around += [below, low, mid] if side == 0 else [mid, high, above]
     kernel = functools.partial(
@@ -604,47 +649,33 @@
     ]
 
 
-def ends_kernel(w_ref, below_ref, low_ref, mid_ref, high_ref, above_ref, inner_ref, f_ref, *work):
-    u_ref, v_ref = work
+def ends_kernel(w_ref, below_ref, low_ref, mid_ref, high_ref, above_ref, _, f_ref, *scratch):
+    u_ref, *work = scratch
     inner = mid_ref.shape[0]
-    layer = HALF * NG
-
-    def copy(i, carry):
-        at = pl.multiple_of(i * 256, 256)
-        f_ref[pl.ds(layer + at, 256), :] = inner_ref[pl.ds(at, 256), :]
-        return carry
-
-    lax.fori_loop(0, inner * layer // 256, copy, 0)
     wz = taps_of(w_ref, 0, True)
-    for base, around in (
+    for at, around in (
         (0, ((below_ref, 0), (low_ref, 0), (mid_ref, 0))),
-        ((inner + 1) * layer, ((mid_ref, inner - 1), (high_ref, 0), (above_ref, 0))),
+        (inner + 1, ((mid_ref, inner - 1), (high_ref, 0), (above_ref, 0))),
     ):
         along_z(wz, around, u_ref, HALF, 1)
         wrap_halves(u_ref)
-
-        def put(y, row, base=base):
-            f_ref[pl.ds(pl.multiple_of(base + y * NG, NG), NG), :] = row
-
-        fourth_rows(w_ref, u_ref, v_ref, put)
-
-
-def run_ends(lanes, y, halos, inner):
+        out = [f_ref.at[pl.ds(at, 1)]]
+        staggered(fourth_stage((w_ref,), (u_ref,), work, out), HALF // GROUP)
+
+
+def run_ends(lanes, y, halos, field):
     low, mid, high = y
     below, above = halos
-    rows = (mid.shape[0] + 2) * HALF * NG
     return pl.pallas_call(
         ends_kernel,
-        out_shape=jax.ShapeDtypeStruct((rows, LANES), F32),
+        out_shape=jax.ShapeDtypeStruct(field.shape, F32),
         in_specs=[vmem()] * 7,
         out_specs=vmem(),
-        scratch_shapes=[
-            pltpu.VMEM((HALF + 2, NG, LANES), F32),
-            pltpu.VMEM((2 * GROUP, NG + 16, LANES), F32),
-        ],
+        scratch_shapes=field_scratch("fourth", 1, False),
+        input_output_aliases={6: 0},
         compiler_params=params(8),
         name="ends",
-    )(lanes, below, low, mid, high, above, inner.reshape(-1, LANES))
+    )(lanes, below, low, mid, high, above, field)
 
 
 def gather_kernel(spots_ref, half_ref, f_ref, out_ref, rows_ref):
@@ -686,7 +717,7 @@
         out_specs=vmem(),
         scratch_shapes=[pltpu.VMEM((count, LANES), F32)],
         compiler_params=params(6),
-        cost_estimate=cost(4_000_000_000, 6_000_000),
+        cost_estimate=cost(500_000_000, 600_000),
         name="gather",
     )(spots, half.reshape(1, count), field)
 
@@ -734,33 +765,29 @@
 ):
     bricks = lax.axis_size("brick")
     depth = NG // lax.axis_size("slab")
-    width = NG // bricks
     me = lax.axis_index("brick").astype(jnp.int32)
     mine = me.reshape(1)
 
-    tab, *blocks = make_deposits(mine, features, tangents, stencil, stencil_table, bricks)
-    blocks, point1, route, cell_local = lax.optimization_barrier(
-        (blocks, point1, route, cell_local)
+    tab, cell, *blocks = make_deposits(
+        mine, features, tangents, stencil, stencil_table, route, cell_local, bricks
     )
+    cell = cell.reshape(-1)
+    chunks, cells = [blocks[0]], [cell]
+    for j in range(1, bricks):
+        block = blocks[j]
+        if j == 3:
+            (sums,) = run_scatter(first_sums_kernel, "own_sums", cells[:1], chunks[:1], None, depth)
+            sums, point1 = lax.optimization_barrier((sums, point1))
+        if j >= 3:
+            sums, cell, block = lax.optimization_barrier((sums, cell, block))
+        cells.append(swap(cell, j))
+        chunks.append(swap(block, j))
     mix1, mix2, back2, back1, lanes = make_weights(
         point1, point2, taps1, taps2, bias1, bias2, readout
     )
-    z_part = cell_local // (width * NG)
-    y_part = route[:, 0] * width + (cell_local // NG) % width
-    x_part = cell_local % NG
-    cell = (z_part * NG + y_part) * NG + x_part
-
-    chunks, cells = [blocks[0]], [cell]
-    (sums,) = run_scatter(first_sums_kernel, "own_sums", cells, chunks, None, depth)
-    for j in range(1, bricks):
-        block = blocks[j]
-        if j >= 3:
-            chunks[j - 2], block = lax.optimization_barrier((chunks[j - 2], block))
-            cells[j - 2], cell = lax.optimization_barrier((cells[j - 2], cell))
-        chunks.append(swap(block, j))
-        cells.append(swap(cell, j))
     (sums,) = run_scatter(more_sums_kernel, "more_sums", cells[1:-1], chunks[1:-1], sums, depth)
-    _, *charge = run_scatter(charge_kernel, "charge", cells[-1:], chunks[-1:], sums, depth)
+    sums, low, high = run_scatter(charge_kernel, "charge", cells[-1:], chunks[-1:], sums, depth)
+    charge = (low, inner_charge(sums, depth), high)
 
     def both(stage, consts, fields, local, halos):
         middle = run_inner(stage, consts, fields, local)
@@ -774,7 +801,7 @@
     ((below, above),) = exchange([y])
     (inner,) = run_inner("fourth", [lanes], [y], [])
 
-    field = run_ends(lanes, y, (below, above), inner)
+    field = run_ends(lanes, y, (below, above), inner).reshape(-1, LANES)
     returned = [None] * NT
     for j in (*range(NT - 1, 0, -1), 0):
         y_of = (cells[j] // NG) % NG

time: 159 us -> 156 us (0.981)
  local copies, waits for them, and re-layouts: 6.28 us -> 1.79 us
  waiting for transfers between devices: 19.1 us -> 20.9 us
    unnamed x28 -> x24, local copies, waits for them, and re-layouts: 6.28 us -> 1.79 us
    ppermute x6, waiting for transfers between devices: 6.65 us -> 10.3 us  [exchange(): lax.ppermute(low, 'slab', down)]
    ppermute x9, waiting for transfers between devices: 7.77 us -> 4.57 us  [swap(): return lax.ppermute(array, 'brick', [(i, i ^ j) for i in range(size)])]
    pallas_call x2 -> x3, Pallas kernels: 3.22 us -> 6.2 us  [the longest x1 3.33 us: make_deposits(): pl.pallas_call(functools.partial(deposits_kernel, peers, NG // peers), ou...]
    pallas_call x10, Pallas kernels: 65.3 us -> 63.4 us  [call_stage(): pl.pallas_call(kernel, out_shape=[jax.ShapeDtypeStruct((layers, HALF, NG,...]
  transfers between devices with their start and end apart: 21 -> 21, of which waited for: 8 -> 7; matrix products, arithmetic and copies ran while one was open for 0% -> 0% of each run, Pallas kernels for 58% -> 57%
where the time goes in v4:
time: 156 us
  Pallas kernels  106 us (68%)
  starting transfers between devices  26.7 us (17%)
  waiting for transfers between devices  20.9 us (13%)
  local copies, waits for them, and re-layouts  1.79 us (1%)
    pallas_call x10, Pallas kernels, call_stage(): pl.pallas_call(kernel, out_shape=[jax.ShapeDtypeStruct((layers, HALF, NG,...  63.4 us
    pallas_call x3, Pallas kernels, run_scatter(): pl.pallas_call(functools.partial(kernel, peers), out_shape=out_shape, in_...  21.8 us
    ppermute x9, starting transfers between devices, swap(): return lax.ppermute(array, 'brick', [(i, i ^ j) for i in range(size)])  14.5 us
    pallas_call x4, Pallas kernels, make_gather(): pl.pallas_call(gather_kernel, out_shape=jax.ShapeDtypeStruct((CH, count),...  12.5 us
    ppermute x6, waiting for transfers between devices, exchange(): lax.ppermute(low, 'slab', down)  10.3 us
    ppermute x6, starting transfers between devices, exchange(): lax.ppermute(low, 'slab', down)  7.41 us
    ppermute x6, waiting for transfers between devices, exchange(): lax.ppermute(high, 'slab', up)  6.04 us
    ppermute x6, starting transfers between devices, exchange(): lax.ppermute(high, 'slab', up)  4.77 us
  transfers between devices with their start and end apart: 21, of which 7 were waited for; matrix products, arithmetic and copies ran while one was open for 0% of the time, Pallas kernels for 57%

profile of v4, /device:TPU:0, one launch (start us, length us, event | category | flops | bytes accessed | tf_op | source)
XLA Modules:
  0.0 155.6 jit_solution(2472369593314591566)
XLA Ops:
  0.0 3.3 %deposits.1 = (f32[64,2048]{1,0:T(8,128)}, s32[1,2048]{1,0:T(1,128)}, bf16[128,2048]{1,0:T(8,128)(2,1)}, bf16[128,2048]{1,0:T(8,128)(2,1)}, bf16[128,2048]{1,0:T(8,128)(2,1)}, /*index=5*/bf16[128,2048]{1,0:T(8,128)(2,1)}) custom-call(s32[1]{0:T(128)} %bitcast.me_ref, bf16[64,2048]{1,0:T(8,128)(2,1)} %feat_ref.1, bf16[4,64,2048]{2,1,0:T(8,128)(2,1)} %tan_ref.1, ...), custom_call_target="tpu_custom_call" | custom-call | tf_op jit(solution)/shard_map/deposits/pallas_call | solution.py:97
  3.3 3.0 %collective-permute-start.3 = (s32[2048]{0:T(1024)}, s32[2048]{0:T(1024)S(1)}, u32[]{:S(2)}, u32[]{:S(2)}) collective-permute-start(s32[2048]{0:T(1024)} %bitcast.19), channel_id=1, source_target_pairs={{0,2},{1,3},{2,0},{3,1},{4,6},{5,7},{6,4},{7,5},{8,10},{9,11},{10,... | collective-permute-start | bytes 24584 | tf_op jit(solution)/shard_map/ppermute | solution.py:748
  6.4 1.5 collective-permute-start.2
  10.3 6.5 %own_sums.1.refs_6_ = f32[32768,128]{1,0:T(8,128)S(1)} custom-call(s32[2048]{0:T(1024)S(1)} %bitcast.21, bf16[128,2048]{1,0:T(8,128)(2,1)S(1)} %copy-done, s32[1,2048]{1,0:T(1,128)S(1)} %copy-done.2), custom_call_target="tpu_custom_call" | custom-call | flops 500000000 | bytes 800000 | tf_op jit(solution)/shard_map/own_sums/pallas_call | solution.py:226
  16.7 2.9 %collective-permute-start = (s32[2048]{0:T(1024)S(1)}, s32[2048]{0:T(1024)S(1)}, u32[]{:S(2)}, u32[]{:S(2)}) collective-permute-start(s32[2048]{0:T(1024)S(1)} %bitcast.22), channel_id=1, source_target_pairs={{0,3},{1,2},{2,1},{3,0},{4,7},{5,6},{6,5},{7,4},{8,11},{9,10},{10,... | collective-permute-start | bytes 24584 | tf_op jit(solution)/shard_map/ppermute | solution.py:748
  20.0 1.4 collective-permute-done.refs_0_
  21.5 2.8 %collective-permute-start.1 = (bf16[128,2048]{1,0:T(8,128)(2,1)S(1)}, bf16[128,2048]{1,0:T(8,128)(2,1)S(1)}, u32[]{:S(2)}, u32[]{:S(2)}) collective-permute-start(bf16[128,2048]{1,0:T(8,128)(2,1)S(1)} %copy-done.11), channel_id=1, source_target_pairs={{0,3},{1,2},{2,1},{3,0},{4,7},{5,6},{6,5},{7,4},{8,11},{9,10},{10,... | collective-permute-start | bytes 1572872 | tf_op jit(solution)/shard_map/ppermute | solution.py:748
  24.4 9.8 %more_sums.1.refs_3_ = f32[32768,128]{1,0:T(8,128)S(1)} custom-call(s32[2048]{0:T(1024)S(1)} %collective-permute-done.2.refs_0_, s32[2048]{0:T(1024)S(1)} %collective-permute-done.3.refs_1_, bf16[128,2048]{1,0:T(8,128)(2,1)S(1)} %collective-permute-done.4.refs_2_, ...), custom_call_target="tpu_custom_call", output_to_operand_aliasing={{}: (6, {})} | custom-call | flops 1000000000 | bytes 1600000 | tf_op jit(solution)/shard_map/more_sums/pallas_call | solution.py:226
  34.2 5.5 %charge.1 = (f32[32768,128]{1,0:T(8,128)S(1)}, bf16[1,64,64,128]{3,2,1,0:T(8,128)(2,1)S(1)}, bf16[1,64,64,128]{3,2,1,0:T(8,128)(2,1)S(1)}) custom-call(s32[2048]{0:T(1024)S(1)} %collective-permute-done.refs_0_, bf16[128,2048]{1,0:T(8,128)(2,1)S(1)} %collective-permute-done.1.refs_1_, s32[1,2048]{1,0:T(1,128)S(1)} %bitcast.24, ...), custom_call_target="tpu_custom_call", output_to_operand_aliasing={{0}: (3, {})} | custom-call | flops 500000000 | bytes 800000 | tf_op jit(solution)/shard_map/charge/pallas_call | solution.py:226
  41.5 14.2 %first_inner.1 = (bf16[6,32,64,128]{3,2,1,0:T(8,128)(2,1)S(1)}, bf16[6,32,64,128]{3,2,1,0:T(8,128)(2,1)S(1)}, f32[6,32,64,128]{3,2,1,0:T(8,128)S(1)}, f32[6,32,64,128]{3,2,1,0:T(8,128)S(1)}) custom-call(f32[24,128]{1,0:T(8,128)S(1)} %get-tuple-element.46.refs_0_.w_ref, bf16[256,256]{1,0:T(8,128)(2,1)S(1)} %get-tuple-element.50.refs_1_, ...), custom_call_target="tpu_custom_call" | custom-call | flops 24000000000 | bytes 36000000 | tf_op jit(solution)/shard_map/first_inner/pallas_call | solution.py:606
  55.6 8.9 %collective-permute-done.7.refs_4_ = bf16[1,64,64,128]{3,2,1,0:T(8,128)(2,1)S(1)} collective-permute-done((bf16[1,64,64,128]{3,2,1,0:T(8,128)(2,1)S(1)}, bf16[1,64,64,128]{3,2,1,0:T(8,128)(2,1)S(1)}, u32[]{:S(2)}, u32[]{:S(2)}) %collective-permute-start.7) | collective-permute-done | bytes 1048608 | tf_op jit(solution)/shard_map/ppermute | solution.py:647
  64.6 2.4 %first_high.1 = (bf16[1,32,64,128]{3,2,1,0:T(8,128)(2,1)S(1)}, bf16[1,32,64,128]{3,2,1,0:T(8,128)(2,1)S(1)}, f32[1,32,64,128]{3,2,1,0:T(8,128)S(1)}, f32[1,32,64,128]{3,2,1,0:T(8,128)S(1)}) custom-call(f32[24,128]{1,0:T(8,128)S(1)} %get-tuple-element.46.refs_0_.w_ref, bf16[256,256]{1,0:T(8,128)(2,1)S(1)} %get-tuple-element.50.refs_1_, ...), custom_call_target="tpu_custom_call" | custom-call | flops 4000000000 | bytes 6000000 | tf_op jit(solution)/shard_map/first_high/pallas_call | solution.py:606
  68.5 2.4 %first_low.1 = (bf16[1,32,64,128]{3,2,1,0:T(8,128)(2,1)S(1)}, bf16[1,32,64,128]{3,2,1,0:T(8,128)(2,1)S(1)}, f32[1,32,64,128]{3,2,1,0:T(8,128)S(1)}, f32[1,32,64,128]{3,2,1,0:T(8,128)S(1)}) custom-call(f32[24,128]{1,0:T(8,128)S(1)} %get-tuple-element.46.refs_0_.w_ref, bf16[256,256]{1,0:T(8,128)(2,1)S(1)} %get-tuple-element.50.refs_1_, ...), custom_call_target="tpu_custom_call" | custom-call | flops 4000000000 | bytes 6000000 | tf_op jit(solution)/shard_map/first_low/pallas_call | solution.py:606
  70.9 2.4 %collective-permute-start.8 = (bf16[1,32,64,128]{3,2,1,0:T(8,128)(2,1)S(1)}, bf16[1,32,64,128]{3,2,1,0:T(8,128)(2,1)S(1)}, u32[]{:S(2)}, u32[]{:S(2)}) collective-permute-start(bf16[1,32,64,128]{3,2,1,0:T(8,128)(2,1)S(1)} %get-tuple-element.61.refs_3_.refs_4_), channel_id=1, source_target_pairs={{4,0},{8,4},{12,8},{16,12},{20,16},{24,20},{28,24},{0,28},{5,1},{9... | collective-permute-start | bytes 1572872 | tf_op jit(solution)/shard_map/ppermute | solution.py:647
  73.7 16.4 %second_inner.1 = (bf16[6,32,64,128]{3,2,1,0:T(8,128)(2,1)S(1)}, bf16[6,32,64,128]{3,2,1,0:T(8,128)(2,1)S(1)}) custom-call(f32[24,128]{1,0:T(8,128)S(1)} %get-tuple-element.46.refs_0_.w_ref, bf16[256,256]{1,0:T(8,128)(2,1)S(1)} %get-tuple-element.48.refs_1_, bf16[256,256]{1,0:T(8,128)(2,1)S(1)} %get-tuple-element.49.refs_2_, ...), custom_call_target="tpu_custom_call" | custom-call | flops 24000000000 | bytes 36000000 | tf_op jit(solution)/shard_map/second_inner/pallas_call | solution.py:606
  90.1 2.8 %second_high.1 = (bf16[1,32,64,128]{3,2,1,0:T(8,128)(2,1)S(1)}, bf16[1,32,64,128]{3,2,1,0:T(8,128)(2,1)S(1)}) custom-call(f32[24,128]{1,0:T(8,128)S(1)} %get-tuple-element.46.refs_0_.w_ref, bf16[256,256]{1,0:T(8,128)(2,1)S(1)} %get-tuple-element.48.refs_1_, bf16[256,256]{1,0:T(8,128)(2,1)S(1)} %get-tuple-element.49.refs_2_, ...), custom_call_target="tpu_custom_call" | custom-call | flops 4000000000 | bytes 6000000 | tf_op jit(solution)/shard_map/second_high/pallas_call | solution.py:606
  93.0 4.2 %collective-permute-start.15 = (bf16[1,32,64,128]{3,2,1,0:T(8,128)(2,1)S(1)}, bf16[1,32,64,128]{3,2,1,0:T(8,128)(2,1)S(1)}, u32[]{:S(2)}, u32[]{:S(2)}) collective-permute-start(bf16[1,32,64,128]{3,2,1,0:T(8,128)(2,1)S(1)} %get-tuple-element.68.refs_3_.refs_4_), channel_id=1, source_target_pairs={{0,4},{4,8},{8,12},{12,16},{16,20},{20,24},{24,28},{28,0},{1,5},{5... | collective-permute-start | bytes 1572872 | tf_op jit(solution)/shard_map/ppermute | solution.py:647
  97.2 2.9 %second_low.1 = (bf16[1,32,64,128]{3,2,1,0:T(8,128)(2,1)S(1)}, bf16[1,32,64,128]{3,2,1,0:T(8,128)(2,1)S(1)}) custom-call(f32[24,128]{1,0:T(8,128)S(1)} %get-tuple-element.46.refs_0_.w_ref, bf16[256,256]{1,0:T(8,128)(2,1)S(1)} %get-tuple-element.48.refs_1_, bf16[256,256]{1,0:T(8,128)(2,1)S(1)} %get-tuple-element.49.refs_2_, ...), custom_call_target="tpu_custom_call" | custom-call | flops 4000000000 | bytes 6000000 | tf_op jit(solution)/shard_map/second_low/pallas_call | solution.py:606
  100.1 3.5 %collective-permute-start.12 = (bf16[1,32,64,128]{3,2,1,0:T(8,128)(2,1)S(1)}, bf16[1,32,64,128]{3,2,1,0:T(8,128)(2,1)S(1)}, u32[]{:S(2)}, u32[]{:S(2)}) collective-permute-start(bf16[1,32,64,128]{3,2,1,0:T(8,128)(2,1)S(1)} %get-tuple-element.69.refs_3_.refs_2_), channel_id=1, source_target_pairs={{4,0},{8,4},{12,8},{16,12},{20,16},{24,20},{28,24},{0,28},{5,1},{9... | collective-permute-start | bytes 1572872 | tf_op jit(solution)/shard_map/ppermute | solution.py:647
  103.9 12.6 %third_inner.1.refs_2_.mid_ref = bf16[6,32,64,128]{3,2,1,0:T(8,128)(2,1)S(1)} custom-call(f32[24,128]{1,0:T(8,128)S(1)} %get-tuple-element.46.refs_0_.w_ref, bf16[128,128]{1,0:T(8,128)(2,1)S(1)} %get-tuple-element.47.refs_1_, bf16[1,32,64,128]{3,2,1,0:T(8,128)(2,1)S(1)} %get-tuple-element.69.refs_3_.refs_2_, ...), custom_call_target="tpu_custom_call" | custom-call | flops 24000000000 | bytes 36000000 | tf_op jit(solution)/shard_map/third_inner/pallas_call | solution.py:606
  116.5 2.1 %third_low.1.refs_1_.low_ref = bf16[1,32,64,128]{3,2,1,0:T(8,128)(2,1)S(1)} custom-call(f32[24,128]{1,0:T(8,128)S(1)} %get-tuple-element.46.refs_0_.w_ref, bf16[128,128]{1,0:T(8,128)(2,1)S(1)} %get-tuple-element.47.refs_1_, bf16[1,32,64,128]{3,2,1,0:T(8,128)(2,1)S(1)} %collective-permute-done.15.refs_2_, ...), custom_call_target="tpu_custom_call" | custom-call | flops 4000000000 | bytes 6000000 | tf_op jit(solution)/shard_map/third_low/pallas_call | solution.py:606
  120.0 2.1 %third_high.1.refs_3_.high_ref = bf16[1,32,64,128]{3,2,1,0:T(8,128)(2,1)S(1)} custom-call(f32[24,128]{1,0:T(8,128)S(1)} %get-tuple-element.46.refs_0_.w_ref, bf16[128,128]{1,0:T(8,128)(2,1)S(1)} %get-tuple-element.47.refs_1_, bf16[6,32,64,128]{3,2,1,0:T(8,128)(2,1)S(1)} %get-tuple-element.67.refs_2_.refs_4_.refs_3_, ...), custom_call_target="tpu_custom_call" | custom-call | flops 4000000000 | bytes 6000000 | tf_op jit(solution)/shard_map/third_high/pallas_call | solution.py:606
  122.5 5.7 %fourth_inner.1._ = f32[8,32,64,128]{3,2,1,0:T(8,128)S(1)} custom-call(f32[24,128]{1,0:T(8,128)S(1)} %get-tuple-element.46.refs_0_.w_ref, bf16[1,32,64,128]{3,2,1,0:T(8,128)(2,1)S(1)} %third_low.1.refs_1_.low_ref, bf16[6,32,64,128]{3,2,1,0:T(8,128)(2,1)S(1)} %third_inner.1.refs_2_.mid_ref, bf16[1,32,64,128]{3,2,1,0:T(8,128)(2,1)S(1)} %third_high.1.refs_3_.high_ref), custom_call_target="tpu_custom_call" | custom-call | flops 32000000000 | bytes 48000000 | tf_op jit(solution)/shard_map/fourth_inner/pallas_call | solution.py:606
  128.2 4.6 %collective-permute-done.14.below_ref = bf16[1,32,64,128]{3,2,1,0:T(8,128)(2,1)S(1)} collective-permute-done((bf16[1,32,64,128]{3,2,1,0:T(8,128)(2,1)S(1)}, bf16[1,32,64,128]{3,2,1,0:T(8,128)(2,1)S(1)}, u32[]{:S(2)}, u32[]{:S(2)}) %collective-permute-start.14) | collective-permute-done | bytes 524320 | tf_op jit(solution)/shard_map/ppermute | solution.py:647
  132.9 1.8 %ends.1 = f32[8,32,64,128]{3,2,1,0:T(8,128)S(1)} custom-call(f32[24,128]{1,0:T(8,128)S(1)} %get-tuple-element.46.refs_0_.w_ref, bf16[1,32,64,128]{3,2,1,0:T(8,128)(2,1)S(1)} %collective-permute-done.14.below_ref, bf16[1,32,64,128]{3,2,1,0:T(8,128)(2,1)S(1)} %third_low.1.refs_1_.low_ref, ...), custom_call_target="tpu_custom_call", output_to_operand_aliasing={{}: (6, {})} | custom-call | tf_op jit(solution)/shard_map/ends/pallas_call | solution.py:669
  134.7 3.1 %gather.7 = bf16[64,2048]{1,0:T(8,128)(2,1)S(1)} custom-call(s32[2048]{0:T(1024)S(1)} %get-tuple-element.80.spots_ref, s32[1,2048]{1,0:T(1,128)S(1)} %bitcast.29, f32[16384,128]{1,0:T(8,128)S(1)} %bitcast.15), custom_call_target="tpu_custom_call" | custom-call | flops 500000000 | bytes 600000 | tf_op jit(solution)/shard_map/gather/pallas_call | solution.py:713
  137.8 1.7 %collective-permute-start.20 = (bf16[64,2048]{1,0:T(8,128)(2,1)S(1)}, bf16[64,2048]{1,0:T(8,128)(2,1)S(1)}, u32[]{:S(2)}, u32[]{:S(2)}) collective-permute-start(bf16[64,2048]{1,0:T(8,128)(2,1)S(1)} %gather.7), channel_id=1, source_target_pairs={{0,3},{1,2},{2,1},{3,0},{4,7},{5,6},{6,5},{7,4},{8,11},{9,10},{10,... | collective-permute-start | bytes 786440 | tf_op jit(solution)/shard_map/ppermute | solution.py:748
  139.5 3.1 %gather.6 = bf16[64,2048]{1,0:T(8,128)(2,1)S(1)} custom-call(s32[2048]{0:T(1024)S(1)} %get-tuple-element.82.spots_ref, s32[1,2048]{1,0:T(1,128)S(1)} %bitcast.28, f32[16384,128]{1,0:T(8,128)S(1)} %bitcast.16), custom_call_target="tpu_custom_call" | custom-call | flops 500000000 | bytes 600000 | tf_op jit(solution)/shard_map/gather/pallas_call | solution.py:713
  143.2 3.1 %gather.5 = bf16[64,2048]{1,0:T(8,128)(2,1)S(1)} custom-call(s32[2048]{0:T(1024)S(1)} %get-tuple-element.84.spots_ref, s32[1,2048]{1,0:T(1,128)S(1)} %bitcast.27, f32[16384,128]{1,0:T(8,128)S(1)} %bitcast.17), custom_call_target="tpu_custom_call" | custom-call | flops 500000000 | bytes 600000 | tf_op jit(solution)/shard_map/gather/pallas_call | solution.py:713
  147.9 3.1 %gather.4.refs_0_ = bf16[64,2048]{1,0:T(8,128)(2,1)S(1)} custom-call(s32[2048]{0:T(1024)S(1)} %fusion.4.spots_ref, s32[1,2048]{1,0:T(1,128)S(1)} %and_select_fusion.half_ref, f32[16384,128]{1,0:T(8,128)S(1)} %bitcast.18), custom_call_target="tpu_custom_call" | custom-call | flops 500000000 | bytes 600000 | tf_op jit(solution)/shard_map/gather/pallas_call | solution.py:713
  151.0 1.9 %collective-permute-done.19.refs_2_ = bf16[64,2048]{1,0:T(8,128)(2,1)S(1)} collective-permute-done((bf16[64,2048]{1,0:T(8,128)(2,1)S(1)}, bf16[64,2048]{1,0:T(8,128)(2,1)S(1)}, u32[]{:S(2)}, u32[]{:S(2)}) %collective-permute-start.19) | collective-permute-done | bytes 262176 | tf_op jit(solution)/shard_map/ppermute | solution.py:748
  154.1 1.5 finish.1
  (61 shorter events, 11.9 us)
Async XLA Ops:
  3.3 20.9 %collective-permute-start.3 = (s32[2048]{0:T(1024)}, s32[2048]{0:T(1024)S(1)}, u32[]{:S(2)}, u32[]{:S(2)}) collective-permute-start(s32[2048]{0:T(1024)} %bitcast.19), channel_id=1, source_target_pairs={{0,2},{1,3},{2,0},{3,1},{4,6},{5,7},{6,4},{7,5},{8,10},{9,11},{10,... | collective-permute-start | bytes 24584 | tf_op jit(solution)/shard_map/ppermute | solution.py:748
  6.4 17.9 %collective-permute-start.2 = (s32[2048]{0:T(1024)}, s32[2048]{0:T(1024)S(1)}, u32[]{:S(2)}, u32[]{:S(2)}) collective-permute-start(s32[2048]{0:T(1024)} %bitcast.20), channel_id=1, source_target_pairs={{0,1},{1,0},{2,3},{3,2},{4,5},{5,4},{6,7},{7,6},{8,9},{9,8},{10,11... | collective-permute-start | bytes 24584 | tf_op jit(solution)/shard_map/ppermute | solution.py:748
  7.9 16.5 %collective-permute-start.4 = (bf16[128,2048]{1,0:T(8,128)(2,1)}, bf16[128,2048]{1,0:T(8,128)(2,1)S(1)}, u32[]{:S(2)}, u32[]{:S(2)}) collective-permute-start(bf16[128,2048]{1,0:T(8,128)(2,1)} %get-tuple-element.55), channel_id=1, source_target_pairs={{0,1},{1,0},{2,3},{3,2},{4,5},{5,4},{6,7},{7,6},{8,9},{9,8},{10,11... | collective-permute-start | bytes 1572872 | tf_op jit(solution)/shard_map/ppermute | solution.py:748
  8.4 16.0 %collective-permute-start.5 = (bf16[128,2048]{1,0:T(8,128)(2,1)}, bf16[128,2048]{1,0:T(8,128)(2,1)S(1)}, u32[]{:S(2)}, u32[]{:S(2)}) collective-permute-start(bf16[128,2048]{1,0:T(8,128)(2,1)} %get-tuple-element.56), channel_id=1, source_target_pairs={{0,2},{1,3},{2,0},{3,1},{4,6},{5,7},{6,4},{7,5},{8,10},{9,11},{10,... | collective-permute-start | bytes 1572872 | tf_op jit(solution)/shard_map/ppermute | solution.py:748
  8.5 1.0 copy-start
  10.2 9.6 %copy-start.4 = (bf16[64,64]{1,0:T(8,128)(2,1)S(1)}, bf16[64,64]{1,0:T(8,128)(2,1)}, u32[]{:S(2)}) copy-start(bf16[64,64]{1,0:T(8,128)(2,1)} %p1_ref) | copy-start | bytes 24580
  10.2 9.6 %copy-start.5 = (bf16[64,64]{1,0:T(8,128)(2,1)S(1)}, bf16[64,64]{1,0:T(8,128)(2,1)}, u32[]{:S(2)}) copy-start(bf16[64,64]{1,0:T(8,128)(2,1)} %p2_ref.1) | copy-start | bytes 24580
  10.2 9.6 %copy-start.6 = (f32[3,3,64]{2,1,0:T(4,128)S(1)}, f32[3,3,64]{2,1,0:T(4,128)}, u32[]{:S(2)}) copy-start(f32[3,3,64]{2,1,0:T(4,128)} %t1_ref.1) | copy-start | bytes 6916
  10.2 9.6 %copy-start.7 = (f32[3,3,64]{2,1,0:T(4,128)S(1)}, f32[3,3,64]{2,1,0:T(4,128)}, u32[]{:S(2)}) copy-start(f32[3,3,64]{2,1,0:T(4,128)} %t2_ref.1) | copy-start | bytes 6916
  10.2 9.6 %copy-start.8 = (f32[64]{0:T(128)S(1)}, f32[64]{0:T(128)}, u32[]{:S(2)}) copy-start(f32[64]{0:T(128)} %param.23) | copy-start | bytes 772
  10.2 9.6 %copy-start.9 = (f32[64]{0:T(128)S(1)}, f32[64]{0:T(128)}, u32[]{:S(2)}) copy-start(f32[64]{0:T(128)} %param.24) | copy-start | bytes 772
  10.3 9.6 %copy-start.10 = (f32[64]{0:T(128)S(1)}, f32[64]{0:T(128)}, u32[]{:S(2)}) copy-start(f32[64]{0:T(128)} %param.25) | copy-start | bytes 772
  10.3 11.2 %copy-start.11 = (bf16[128,2048]{1,0:T(8,128)(2,1)S(1)}, bf16[128,2048]{1,0:T(8,128)(2,1)}, u32[]{:S(2)}) copy-start(bf16[128,2048]{1,0:T(8,128)(2,1)} %get-tuple-element.54) | copy-start | bytes 1572868
  16.7 4.7 %collective-permute-start = (s32[2048]{0:T(1024)S(1)}, s32[2048]{0:T(1024)S(1)}, u32[]{:S(2)}, u32[]{:S(2)}) collective-permute-start(s32[2048]{0:T(1024)S(1)} %bitcast.22), channel_id=1, source_target_pairs={{0,3},{1,2},{2,1},{3,0},{4,7},{5,6},{6,5},{7,4},{8,11},{9,10},{10,... | collective-permute-start | bytes 24584 | tf_op jit(solution)/shard_map/ppermute | solution.py:748
  21.5 12.7 %collective-permute-start.1 = (bf16[128,2048]{1,0:T(8,128)(2,1)S(1)}, bf16[128,2048]{1,0:T(8,128)(2,1)S(1)}, u32[]{:S(2)}, u32[]{:S(2)}) collective-permute-start(bf16[128,2048]{1,0:T(8,128)(2,1)S(1)} %copy-done.11), channel_id=1, source_target_pairs={{0,3},{1,2},{2,1},{3,0},{4,7},{5,6},{6,5},{7,4},{8,11},{9,10},{10,... | collective-permute-start | bytes 1572872 | tf_op jit(solution)/shard_map/ppermute | solution.py:748
  40.8 23.8 %collective-permute-start.7 = (bf16[1,64,64,128]{3,2,1,0:T(8,128)(2,1)S(1)}, bf16[1,64,64,128]{3,2,1,0:T(8,128)(2,1)S(1)}, u32[]{:S(2)}, u32[]{:S(2)}) collective-permute-start(bf16[1,64,64,128]{3,2,1,0:T(8,128)(2,1)S(1)} %get-tuple-element.59.refs_3_.refs_2_), channel_id=1, source_target_pairs={{4,0},{8,4},{12,8},{16,12},{20,16},{24,20},{28,24},{0,28},{5,1},{9... | collective-permute-start | bytes 3145736 | tf_op jit(solution)/shard_map/ppermute | solution.py:647
  41.5 27.0 %collective-permute-start.6 = (bf16[1,64,64,128]{3,2,1,0:T(8,128)(2,1)S(1)}, bf16[1,64,64,128]{3,2,1,0:T(8,128)(2,1)S(1)}, u32[]{:S(2)}, u32[]{:S(2)}) collective-permute-start(bf16[1,64,64,128]{3,2,1,0:T(8,128)(2,1)S(1)} %get-tuple-element.58.refs_4_.refs_3_), channel_id=1, source_target_pairs={{0,4},{4,8},{8,12},{12,16},{16,20},{20,24},{24,28},{28,0},{1,5},{5... | collective-permute-start | bytes 3145736 | tf_op jit(solution)/shard_map/ppermute | solution.py:647
  67.0 30.3 %collective-permute-start.10 = (bf16[1,32,64,128]{3,2,1,0:T(8,128)(2,1)S(1)}, bf16[1,32,64,128]{3,2,1,0:T(8,128)(2,1)S(1)}, u32[]{:S(2)}, u32[]{:S(2)}) collective-permute-start(bf16[1,32,64,128]{3,2,1,0:T(8,128)(2,1)S(1)} %get-tuple-element.63.refs_5_.refs_4_), channel_id=1, source_target_pairs={{0,4},{4,8},{8,12},{12,16},{16,20},{20,24},{24,28},{28,0},{1,5},{5... | collective-permute-start | bytes 1572872 | tf_op jit(solution)/shard_map/ppermute | solution.py:647
  67.0 30.2 %collective-permute-start.11 = (bf16[1,32,64,128]{3,2,1,0:T(8,128)(2,1)S(1)}, bf16[1,32,64,128]{3,2,1,0:T(8,128)(2,1)S(1)}, u32[]{:S(2)}, u32[]{:S(2)}) collective-permute-start(bf16[1,32,64,128]{3,2,1,0:T(8,128)(2,1)S(1)} %get-tuple-element.66.refs_8_.refs_7_), channel_id=1, source_target_pairs={{0,4},{4,8},{8,12},{12,16},{16,20},{20,24},{24,28},{28,0},{1,5},{5... | collective-permute-start | bytes 1572872 | tf_op jit(solution)/shard_map/ppermute | solution.py:647
  70.9 19.2 %collective-permute-start.8 = (bf16[1,32,64,128]{3,2,1,0:T(8,128)(2,1)S(1)}, bf16[1,32,64,128]{3,2,1,0:T(8,128)(2,1)S(1)}, u32[]{:S(2)}, u32[]{:S(2)}) collective-permute-start(bf16[1,32,64,128]{3,2,1,0:T(8,128)(2,1)S(1)} %get-tuple-element.61.refs_3_.refs_4_), channel_id=1, source_target_pairs={{4,0},{8,4},{12,8},{16,12},{20,16},{24,20},{28,24},{0,28},{5,1},{9... | collective-permute-start | bytes 1572872 | tf_op jit(solution)/shard_map/ppermute | solution.py:647
  73.3 16.9 %collective-permute-start.9 = (bf16[1,32,64,128]{3,2,1,0:T(8,128)(2,1)S(1)}, bf16[1,32,64,128]{3,2,1,0:T(8,128)(2,1)S(1)}, u32[]{:S(2)}, u32[]{:S(2)}) collective-permute-start(bf16[1,32,64,128]{3,2,1,0:T(8,128)(2,1)S(1)} %get-tuple-element.64.refs_6_.refs_7_), channel_id=1, source_target_pairs={{4,0},{8,4},{12,8},{16,12},{20,16},{24,20},{28,24},{0,28},{5,1},{9... | collective-permute-start | bytes 1572872 | tf_op jit(solution)/shard_map/ppermute | solution.py:647
  93.0 23.5 %collective-permute-start.15 = (bf16[1,32,64,128]{3,2,1,0:T(8,128)(2,1)S(1)}, bf16[1,32,64,128]{3,2,1,0:T(8,128)(2,1)S(1)}, u32[]{:S(2)}, u32[]{:S(2)}) collective-permute-start(bf16[1,32,64,128]{3,2,1,0:T(8,128)(2,1)S(1)} %get-tuple-element.68.refs_3_.refs_4_), channel_id=1, source_target_pairs={{0,4},{4,8},{8,12},{12,16},{16,20},{20,24},{24,28},{28,0},{1,5},{5... | collective-permute-start | bytes 1572872 | tf_op jit(solution)/shard_map/ppermute | solution.py:647
  97.2 19.3 %collective-permute-start.16 = (bf16[1,32,64,128]{3,2,1,0:T(8,128)(2,1)S(1)}, bf16[1,32,64,128]{3,2,1,0:T(8,128)(2,1)S(1)}, u32[]{:S(2)}, u32[]{:S(2)}) collective-permute-start(bf16[1,32,64,128]{3,2,1,0:T(8,128)(2,1)S(1)} %get-tuple-element.71.refs_6_.refs_7_), channel_id=1, source_target_pairs={{0,4},{4,8},{8,12},{12,16},{16,20},{20,24},{24,28},{28,0},{1,5},{5... | collective-permute-start | bytes 1572872 | tf_op jit(solution)/shard_map/ppermute | solution.py:647
  100.1 18.6 %collective-permute-start.12 = (bf16[1,32,64,128]{3,2,1,0:T(8,128)(2,1)S(1)}, bf16[1,32,64,128]{3,2,1,0:T(8,128)(2,1)S(1)}, u32[]{:S(2)}, u32[]{:S(2)}) collective-permute-start(bf16[1,32,64,128]{3,2,1,0:T(8,128)(2,1)S(1)} %get-tuple-element.69.refs_3_.refs_2_), channel_id=1, source_target_pairs={{4,0},{8,4},{12,8},{16,12},{20,16},{24,20},{28,24},{0,28},{5,1},{9... | collective-permute-start | bytes 1572872 | tf_op jit(solution)/shard_map/ppermute | solution.py:647
  103.6 16.4 %collective-permute-start.13 = (bf16[1,32,64,128]{3,2,1,0:T(8,128)(2,1)S(1)}, bf16[1,32,64,128]{3,2,1,0:T(8,128)(2,1)S(1)}, u32[]{:S(2)}, u32[]{:S(2)}) collective-permute-start(bf16[1,32,64,128]{3,2,1,0:T(8,128)(2,1)S(1)} %get-tuple-element.72.refs_6_.refs_5_), channel_id=1, source_target_pairs={{4,0},{8,4},{12,8},{16,12},{20,16},{24,20},{28,24},{0,28},{5,1},{9... | collective-permute-start | bytes 1572872 | tf_op jit(solution)/shard_map/ppermute | solution.py:647
  118.6 9.6 %collective-permute-start.17 = (bf16[1,32,64,128]{3,2,1,0:T(8,128)(2,1)S(1)}, bf16[1,32,64,128]{3,2,1,0:T(8,128)(2,1)S(1)}, u32[]{:S(2)}, u32[]{:S(2)}) collective-permute-start(bf16[1,32,64,128]{3,2,1,0:T(8,128)(2,1)S(1)} %third_low.1.refs_1_.low_ref), channel_id=1, source_target_pairs={{4,0},{8,4},{12,8},{16,12},{20,16},{24,20},{28,24},{0,28},{5,1},{9... | collective-permute-start | bytes 1572872 | tf_op jit(solution)/shard_map/ppermute | solution.py:647
  122.1 10.7 %collective-permute-start.14 = (bf16[1,32,64,128]{3,2,1,0:T(8,128)(2,1)S(1)}, bf16[1,32,64,128]{3,2,1,0:T(8,128)(2,1)S(1)}, u32[]{:S(2)}, u32[]{:S(2)}) collective-permute-start(bf16[1,32,64,128]{3,2,1,0:T(8,128)(2,1)S(1)} %third_high.1.refs_3_.high_ref), channel_id=1, source_target_pairs={{0,4},{4,8},{8,12},{12,16},{16,20},{20,24},{24,28},{28,0},{1,5},{5... | collective-permute-start | bytes 1572872 | tf_op jit(solution)/shard_map/ppermute | solution.py:647
  137.8 13.2 %collective-permute-start.20 = (bf16[64,2048]{1,0:T(8,128)(2,1)S(1)}, bf16[64,2048]{1,0:T(8,128)(2,1)S(1)}, u32[]{:S(2)}, u32[]{:S(2)}) collective-permute-start(bf16[64,2048]{1,0:T(8,128)(2,1)S(1)} %gather.7), channel_id=1, source_target_pairs={{0,3},{1,2},{2,1},{3,0},{4,7},{5,6},{6,5},{7,4},{8,11},{9,10},{10,... | collective-permute-start | bytes 786440 | tf_op jit(solution)/shard_map/ppermute | solution.py:748
  142.6 5.2 %copy-start.3 = (s32[1,2048]{1,0:T(1,128)S(1)}, s32[1,2048]{1,0:T(1,128)}, u32[]{:S(2)}) copy-start(s32[1,2048]{1,0:T(1,128)} %get-tuple-element.43.refs_2_) | copy-start | bytes 24580
  142.6 10.3 %collective-permute-start.19 = (bf16[64,2048]{1,0:T(8,128)(2,1)S(1)}, bf16[64,2048]{1,0:T(8,128)(2,1)S(1)}, u32[]{:S(2)}, u32[]{:S(2)}) collective-permute-start(bf16[64,2048]{1,0:T(8,128)(2,1)S(1)} %gather.6), channel_id=1, source_target_pairs={{0,2},{1,3},{2,0},{3,1},{4,6},{5,7},{6,4},{7,5},{8,10},{9,11},{10,... | collective-permute-start | bytes 786440 | tf_op jit(solution)/shard_map/ppermute | solution.py:748
  146.4 7.7 %copy-start.1 = (f32[64,2048]{1,0:T(8,128)S(1)}, f32[64,2048]{1,0:T(8,128)}, u32[]{:S(2)}) copy-start(f32[64,2048]{1,0:T(8,128)} %get-tuple-element.42.tab_ref) | copy-start | bytes 1572868
  146.4 7.7 %collective-permute-start.18 = (bf16[64,2048]{1,0:T(8,128)(2,1)S(1)}, bf16[64,2048]{1,0:T(8,128)(2,1)S(1)}, u32[]{:S(2)}, u32[]{:S(2)}) collective-permute-start(bf16[64,2048]{1,0:T(8,128)(2,1)S(1)} %gather.5), channel_id=1, source_target_pairs={{0,1},{1,0},{2,3},{3,2},{4,5},{5,4},{6,7},{7,6},{8,9},{9,8},{10,11... | collective-permute-start | bytes 786440 | tf_op jit(solution)/shard_map/ppermute | solution.py:748
  (1 other events, 0.7 us)

commit v5 on v4

--- a/solution.py
+++ b/solution.py
@@ -14,7 +14,7 @@
 LANES = 2 * CH
 HALF = NG // 2
 GROUP = 8
-ROWS = 4
+ROWS = 8
 RUN = 16
 BLOCK = 256
 MIB = 1024 * 1024
@@ -154,7 +154,7 @@
                 sums_ref[pl.ds(cell, 1), :] = value
             return carry
 
-        lax.fori_loop(0, blocks * width // RUN, add, 0)
+        lax.fori_loop(0, blocks * width // RUN, add, 0, unroll=4)
 
 
 def split_scatter(peers, refs):
@@ -680,7 +680,7 @@
 
 def gather_kernel(spots_ref, half_ref, f_ref, out_ref, rows_ref):
     count = rows_ref.shape[0]
-    unroll = 16
+    unroll = 128
     eye = jnp.where(
         lax.broadcasted_iota(jnp.int32, (LANES, LANES), 0)
         == lax.broadcasted_iota(jnp.int32, (LANES, LANES), 1),
@@ -723,19 +723,28 @@
 
 
 def finish_kernel(peers, me_ref, tab_ref, *refs):
-    out_ref = refs[peers]
-    me = me_ref[0]
-    for j in range(peers):
-        k = lax.rem(lax.bitwise_xor(me, j), NT)
-        out_ref[k] = refs[j][...].astype(F32) * tab_ref[...]
+    out_ref, rows_ref, sems = refs[-3:]
+    copies = []
+    for n in range(peers):
+        k = lax.rem(lax.bitwise_xor(me_ref[0], n), NT)
+        rows_ref[n] = refs[n][...].astype(F32) * tab_ref[...]
+        copies.append(pltpu.make_async_copy(rows_ref.at[n], out_ref.at[k], sems.at[n]))
+        copies[-1].start()
+    for copy in copies:
+        copy.wait()
 
 
 def make_output(me, tab, returned):
+    count = len(returned)
     return pl.pallas_call(
-        functools.partial(finish_kernel, len(returned)),
+        functools.partial(finish_kernel, count),
         out_shape=jax.ShapeDtypeStruct((NT,) + tab.shape, F32),
-        in_specs=[smem()] + [vmem()] * (len(returned) + 1),
-        out_specs=vmem(),
+        in_specs=[smem()] + [vmem()] * (count + 1),
+        out_specs=pl.BlockSpec(memory_space=pl.ANY),
+        scratch_shapes=[
+            pltpu.VMEM((count,) + tab.shape, F32),
+            pltpu.SemaphoreType.DMA((count,)),
+        ],
         compiler_params=params(8),
         name="finish",
     )(me, tab, *returned)

time: 156 us -> 152 us (0.974)
  Pallas kernels: 106 us -> 98.4 us
  waiting for transfers between devices: 20.9 us -> 24.3 us
    pallas_call x10, Pallas kernels: 63.4 us -> 60.7 us  [call_stage(): pl.pallas_call(kernel, out_shape=[jax.ShapeDtypeStruct((layers, HALF, NG,...]
    pallas_call x3, Pallas kernels: 21.8 us -> 19.4 us  [run_scatter(): pl.pallas_call(functools.partial(kernel, peers), out_shape=out_shape, in_...]
    ppermute x6, waiting for transfers between devices: 10.3 us -> 12.7 us  [exchange(): lax.ppermute(low, 'slab', down)]
    pallas_call x4, Pallas kernels: 12.5 us -> 10.6 us  [make_gather(): pl.pallas_call(gather_kernel, out_shape=jax.ShapeDtypeStruct((CH, count),...]
  transfers between devices with their start and end apart: 21 -> 21, of which waited for: 7 -> 9; matrix products, arithmetic and copies ran while one was open for 0% -> 0% of each run, Pallas kernels for 57% -> 55%
where the time goes in v5:
time: 152 us
  Pallas kernels  98.4 us (65%)
  starting transfers between devices  26.2 us (17%)
  waiting for transfers between devices  24.3 us (16%)
  local copies, waits for them, and re-layouts  1.79 us (1%)
    pallas_call x10, Pallas kernels, call_stage(): pl.pallas_call(kernel, out_shape=[jax.ShapeDtypeStruct((layers, HALF, NG,...  60.7 us
    pallas_call x3, Pallas kernels, run_scatter(): pl.pallas_call(functools.partial(kernel, peers), out_shape=out_shape, in_...  19.4 us
    ppermute x9, starting transfers between devices, swap(): return lax.ppermute(array, 'brick', [(i, i ^ j) for i in range(size)])  14 us
    ppermute x6, waiting for transfers between devices, exchange(): lax.ppermute(low, 'slab', down)  12.7 us
    pallas_call x4, Pallas kernels, make_gather(): pl.pallas_call(gather_kernel, out_shape=jax.ShapeDtypeStruct((CH, count),...  10.6 us
    ppermute x6, starting transfers between devices, exchange(): lax.ppermute(low, 'slab', down)  6.77 us
    ppermute x9, waiting for transfers between devices, swap(): return lax.ppermute(array, 'brick', [(i, i ^ j) for i in range(size)])  5.92 us
    ppermute x6, waiting for transfers between devices, exchange(): lax.ppermute(high, 'slab', up)  5.74 us
  transfers between devices with their start and end apart: 21, of which 9 were waited for; matrix products, arithmetic and copies ran while one was open for 0% of the time, Pallas kernels for 55%

profile of v5, /device:TPU:0, one launch (start us, length us, event | category | flops | bytes accessed | tf_op | source)
XLA Modules:
  0.0 151.5 jit_solution(14847250819056748340)
XLA Ops:
  0.0 3.3 %deposits.1 = (f32[64,2048]{1,0:T(8,128)}, s32[1,2048]{1,0:T(1,128)}, bf16[128,2048]{1,0:T(8,128)(2,1)}, bf16[128,2048]{1,0:T(8,128)(2,1)}, bf16[128,2048]{1,0:T(8,128)(2,1)}, /*index=5*/bf16[128,2048]{1,0:T(8,128)(2,1)}) custom-call(s32[1]{0:T(128)} %bitcast.me_ref, bf16[64,2048]{1,0:T(8,128)(2,1)} %feat_ref.1, bf16[4,64,2048]{2,1,0:T(8,128)(2,1)} %tan_ref.1, ...), custom_call_target="tpu_custom_call" | custom-call | tf_op jit(solution)/shard_map/deposits/pallas_call | solution.py:97
  3.3 3.0 %collective-permute-start.3 = (s32[2048]{0:T(1024)}, s32[2048]{0:T(1024)S(1)}, u32[]{:S(2)}, u32[]{:S(2)}) collective-permute-start(s32[2048]{0:T(1024)} %bitcast.19), channel_id=1, source_target_pairs={{0,2},{1,3},{2,0},{3,1},{4,6},{5,7},{6,4},{7,5},{8,10},{9,11},{10,... | collective-permute-start | bytes 24584 | tf_op jit(solution)/shard_map/ppermute | solution.py:757
  10.3 5.8 %own_sums.1.refs_6_ = f32[32768,128]{1,0:T(8,128)S(1)} custom-call(s32[2048]{0:T(1024)S(1)} %bitcast.21, bf16[128,2048]{1,0:T(8,128)(2,1)S(1)} %copy-done, s32[1,2048]{1,0:T(1,128)S(1)} %copy-done.2), custom_call_target="tpu_custom_call" | custom-call | flops 500000000 | bytes 800000 | tf_op jit(solution)/shard_map/own_sums/pallas_call | solution.py:226
  16.1 2.9 %collective-permute-start = (s32[2048]{0:T(1024)S(1)}, s32[2048]{0:T(1024)S(1)}, u32[]{:S(2)}, u32[]{:S(2)}) collective-permute-start(s32[2048]{0:T(1024)S(1)} %bitcast.22), channel_id=1, source_target_pairs={{0,3},{1,2},{2,1},{3,0},{4,7},{5,6},{6,5},{7,4},{8,11},{9,10},{10,... | collective-permute-start | bytes 24584 | tf_op jit(solution)/shard_map/ppermute | solution.py:757
  19.4 2.0 %collective-permute-done.refs_0_ = s32[2048]{0:T(1024)S(1)} collective-permute-done((s32[2048]{0:T(1024)S(1)}, s32[2048]{0:T(1024)S(1)}, u32[]{:S(2)}, u32[]{:S(2)}) %collective-permute-start) | collective-permute-done | bytes 8224 | tf_op jit(solution)/shard_map/ppermute | solution.py:757
  21.4 2.2 %collective-permute-start.1 = (bf16[128,2048]{1,0:T(8,128)(2,1)S(1)}, bf16[128,2048]{1,0:T(8,128)(2,1)S(1)}, u32[]{:S(2)}, u32[]{:S(2)}) collective-permute-start(bf16[128,2048]{1,0:T(8,128)(2,1)S(1)} %copy-done.11), channel_id=1, source_target_pairs={{0,3},{1,2},{2,1},{3,0},{4,7},{5,6},{6,5},{7,4},{8,11},{9,10},{10,... | collective-permute-start | bytes 1572872 | tf_op jit(solution)/shard_map/ppermute | solution.py:757
  23.8 8.6 %more_sums.1.refs_3_ = f32[32768,128]{1,0:T(8,128)S(1)} custom-call(s32[2048]{0:T(1024)S(1)} %collective-permute-done.2.refs_0_, s32[2048]{0:T(1024)S(1)} %collective-permute-done.3.refs_1_, bf16[128,2048]{1,0:T(8,128)(2,1)S(1)} %collective-permute-done.4.refs_2_, ...), custom_call_target="tpu_custom_call", output_to_operand_aliasing={{}: (6, {})} | custom-call | flops 1000000000 | bytes 1600000 | tf_op jit(solution)/shard_map/more_sums/pallas_call | solution.py:226
  32.4 1.7 %collective-permute-done.1.refs_1_ = bf16[128,2048]{1,0:T(8,128)(2,1)S(1)} collective-permute-done((bf16[128,2048]{1,0:T(8,128)(2,1)S(1)}, bf16[128,2048]{1,0:T(8,128)(2,1)S(1)}, u32[]{:S(2)}, u32[]{:S(2)}) %collective-permute-start.1) | collective-permute-done | bytes 524320 | tf_op jit(solution)/shard_map/ppermute | solution.py:757
  34.1 4.9 %charge.1 = (f32[32768,128]{1,0:T(8,128)S(1)}, bf16[1,64,64,128]{3,2,1,0:T(8,128)(2,1)S(1)}, bf16[1,64,64,128]{3,2,1,0:T(8,128)(2,1)S(1)}) custom-call(s32[2048]{0:T(1024)S(1)} %collective-permute-done.refs_0_, bf16[128,2048]{1,0:T(8,128)(2,1)S(1)} %collective-permute-done.1.refs_1_, s32[1,2048]{1,0:T(1,128)S(1)} %bitcast.24, ...), custom_call_target="tpu_custom_call", output_to_operand_aliasing={{0}: (3, {})} | custom-call | flops 500000000 | bytes 800000 | tf_op jit(solution)/shard_map/charge/pallas_call | solution.py:226
  40.6 13.4 %first_inner.1 = (bf16[6,32,64,128]{3,2,1,0:T(8,128)(2,1)S(1)}, bf16[6,32,64,128]{3,2,1,0:T(8,128)(2,1)S(1)}, f32[6,32,64,128]{3,2,1,0:T(8,128)S(1)}, f32[6,32,64,128]{3,2,1,0:T(8,128)S(1)}) custom-call(f32[24,128]{1,0:T(8,128)S(1)} %get-tuple-element.46.refs_0_.w_ref, bf16[256,256]{1,0:T(8,128)(2,1)S(1)} %get-tuple-element.50.refs_1_, ...), custom_call_target="tpu_custom_call" | custom-call | flops 24000000000 | bytes 36000000 | tf_op jit(solution)/shard_map/first_inner/pallas_call | solution.py:606
  54.0 9.5 %collective-permute-done.7.refs_4_ = bf16[1,64,64,128]{3,2,1,0:T(8,128)(2,1)S(1)} collective-permute-done((bf16[1,64,64,128]{3,2,1,0:T(8,128)(2,1)S(1)}, bf16[1,64,64,128]{3,2,1,0:T(8,128)(2,1)S(1)}, u32[]{:S(2)}, u32[]{:S(2)}) %collective-permute-start.7) | collective-permute-done | bytes 1048608 | tf_op jit(solution)/shard_map/ppermute | solution.py:647
  63.5 2.3 %first_high.1 = (bf16[1,32,64,128]{3,2,1,0:T(8,128)(2,1)S(1)}, bf16[1,32,64,128]{3,2,1,0:T(8,128)(2,1)S(1)}, f32[1,32,64,128]{3,2,1,0:T(8,128)S(1)}, f32[1,32,64,128]{3,2,1,0:T(8,128)S(1)}) custom-call(f32[24,128]{1,0:T(8,128)S(1)} %get-tuple-element.46.refs_0_.w_ref, bf16[256,256]{1,0:T(8,128)(2,1)S(1)} %get-tuple-element.50.refs_1_, ...), custom_call_target="tpu_custom_call" | custom-call | flops 4000000000 | bytes 6000000 | tf_op jit(solution)/shard_map/first_high/pallas_call | solution.py:606
  67.8 2.3 %first_low.1 = (bf16[1,32,64,128]{3,2,1,0:T(8,128)(2,1)S(1)}, bf16[1,32,64,128]{3,2,1,0:T(8,128)(2,1)S(1)}, f32[1,32,64,128]{3,2,1,0:T(8,128)S(1)}, f32[1,32,64,128]{3,2,1,0:T(8,128)S(1)}) custom-call(f32[24,128]{1,0:T(8,128)S(1)} %get-tuple-element.46.refs_0_.w_ref, bf16[256,256]{1,0:T(8,128)(2,1)S(1)} %get-tuple-element.50.refs_1_, ...), custom_call_target="tpu_custom_call" | custom-call | flops 4000000000 | bytes 6000000 | tf_op jit(solution)/shard_map/first_low/pallas_call | solution.py:606
  70.2 2.1 %collective-permute-start.8 = (bf16[1,32,64,128]{3,2,1,0:T(8,128)(2,1)S(1)}, bf16[1,32,64,128]{3,2,1,0:T(8,128)(2,1)S(1)}, u32[]{:S(2)}, u32[]{:S(2)}) collective-permute-start(bf16[1,32,64,128]{3,2,1,0:T(8,128)(2,1)S(1)} %get-tuple-element.61.refs_3_.refs_4_), channel_id=1, source_target_pairs={{4,0},{8,4},{12,8},{16,12},{20,16},{24,20},{28,24},{0,28},{5,1},{9... | collective-permute-start | bytes 1572872 | tf_op jit(solution)/shard_map/ppermute | solution.py:647
  72.6 15.7 %second_inner.1 = (bf16[6,32,64,128]{3,2,1,0:T(8,128)(2,1)S(1)}, bf16[6,32,64,128]{3,2,1,0:T(8,128)(2,1)S(1)}) custom-call(f32[24,128]{1,0:T(8,128)S(1)} %get-tuple-element.46.refs_0_.w_ref, bf16[256,256]{1,0:T(8,128)(2,1)S(1)} %get-tuple-element.48.refs_1_, bf16[256,256]{1,0:T(8,128)(2,1)S(1)} %get-tuple-element.49.refs_2_, ...), custom_call_target="tpu_custom_call" | custom-call | flops 24000000000 | bytes 36000000 | tf_op jit(solution)/shard_map/second_inner/pallas_call | solution.py:606
  89.3 2.8 %second_high.1 = (bf16[1,32,64,128]{3,2,1,0:T(8,128)(2,1)S(1)}, bf16[1,32,64,128]{3,2,1,0:T(8,128)(2,1)S(1)}) custom-call(f32[24,128]{1,0:T(8,128)S(1)} %get-tuple-element.46.refs_0_.w_ref, bf16[256,256]{1,0:T(8,128)(2,1)S(1)} %get-tuple-element.48.refs_1_, bf16[256,256]{1,0:T(8,128)(2,1)S(1)} %get-tuple-element.49.refs_2_, ...), custom_call_target="tpu_custom_call" | custom-call | flops 4000000000 | bytes 6000000 | tf_op jit(solution)/shard_map/second_high/pallas_call | solution.py:606
  92.1 3.9 %collective-permute-start.15 = (bf16[1,32,64,128]{3,2,1,0:T(8,128)(2,1)S(1)}, bf16[1,32,64,128]{3,2,1,0:T(8,128)(2,1)S(1)}, u32[]{:S(2)}, u32[]{:S(2)}) collective-permute-start(bf16[1,32,64,128]{3,2,1,0:T(8,128)(2,1)S(1)} %get-tuple-element.68.refs_3_.refs_4_), channel_id=1, source_target_pairs={{0,4},{4,8},{8,12},{12,16},{16,20},{20,24},{24,28},{28,0},{1,5},{5... | collective-permute-start | bytes 1572872 | tf_op jit(solution)/shard_map/ppermute | solution.py:647
  96.1 2.8 %second_low.1 = (bf16[1,32,64,128]{3,2,1,0:T(8,128)(2,1)S(1)}, bf16[1,32,64,128]{3,2,1,0:T(8,128)(2,1)S(1)}) custom-call(f32[24,128]{1,0:T(8,128)S(1)} %get-tuple-element.46.refs_0_.w_ref, bf16[256,256]{1,0:T(8,128)(2,1)S(1)} %get-tuple-element.48.refs_1_, bf16[256,256]{1,0:T(8,128)(2,1)S(1)} %get-tuple-element.49.refs_2_, ...), custom_call_target="tpu_custom_call" | custom-call | flops 4000000000 | bytes 6000000 | tf_op jit(solution)/shard_map/second_low/pallas_call | solution.py:606
  98.9 3.5 %collective-permute-start.12 = (bf16[1,32,64,128]{3,2,1,0:T(8,128)(2,1)S(1)}, bf16[1,32,64,128]{3,2,1,0:T(8,128)(2,1)S(1)}, u32[]{:S(2)}, u32[]{:S(2)}) collective-permute-start(bf16[1,32,64,128]{3,2,1,0:T(8,128)(2,1)S(1)} %get-tuple-element.69.refs_3_.refs_2_), channel_id=1, source_target_pairs={{4,0},{8,4},{12,8},{16,12},{20,16},{24,20},{28,24},{0,28},{5,1},{9... | collective-permute-start | bytes 1572872 | tf_op jit(solution)/shard_map/ppermute | solution.py:647
  102.7 11.8 %third_inner.1.refs_2_.mid_ref = bf16[6,32,64,128]{3,2,1,0:T(8,128)(2,1)S(1)} custom-call(f32[24,128]{1,0:T(8,128)S(1)} %get-tuple-element.46.refs_0_.w_ref, bf16[128,128]{1,0:T(8,128)(2,1)S(1)} %get-tuple-element.47.refs_1_, bf16[1,32,64,128]{3,2,1,0:T(8,128)(2,1)S(1)} %get-tuple-element.69.refs_3_.refs_2_, ...), custom_call_target="tpu_custom_call" | custom-call | flops 24000000000 | bytes 36000000 | tf_op jit(solution)/shard_map/third_inner/pallas_call | solution.py:606
  114.5 2.1 %third_low.1.refs_1_.low_ref = bf16[1,32,64,128]{3,2,1,0:T(8,128)(2,1)S(1)} custom-call(f32[24,128]{1,0:T(8,128)S(1)} %get-tuple-element.46.refs_0_.w_ref, bf16[128,128]{1,0:T(8,128)(2,1)S(1)} %get-tuple-element.47.refs_1_, bf16[1,32,64,128]{3,2,1,0:T(8,128)(2,1)S(1)} %collective-permute-done.15.refs_2_, ...), custom_call_target="tpu_custom_call" | custom-call | flops 4000000000 | bytes 6000000 | tf_op jit(solution)/shard_map/third_low/pallas_call | solution.py:606
  116.7 2.2 %collective-permute-done.13.refs_7_ = bf16[1,32,64,128]{3,2,1,0:T(8,128)(2,1)S(1)} collective-permute-done((bf16[1,32,64,128]{3,2,1,0:T(8,128)(2,1)S(1)}, bf16[1,32,64,128]{3,2,1,0:T(8,128)(2,1)S(1)}, u32[]{:S(2)}, u32[]{:S(2)}) %collective-permute-start.13) | collective-permute-done | bytes 524320 | tf_op jit(solution)/shard_map/ppermute | solution.py:647
  118.8 2.0 %third_high.1.refs_3_.high_ref = bf16[1,32,64,128]{3,2,1,0:T(8,128)(2,1)S(1)} custom-call(f32[24,128]{1,0:T(8,128)S(1)} %get-tuple-element.46.refs_0_.w_ref, bf16[128,128]{1,0:T(8,128)(2,1)S(1)} %get-tuple-element.47.refs_1_, bf16[6,32,64,128]{3,2,1,0:T(8,128)(2,1)S(1)} %get-tuple-element.67.refs_2_.refs_4_.refs_3_, ...), custom_call_target="tpu_custom_call" | custom-call | flops 4000000000 | bytes 6000000 | tf_op jit(solution)/shard_map/third_high/pallas_call | solution.py:606
  121.8 5.3 %fourth_inner.1._ = f32[8,32,64,128]{3,2,1,0:T(8,128)S(1)} custom-call(f32[24,128]{1,0:T(8,128)S(1)} %get-tuple-element.46.refs_0_.w_ref, bf16[1,32,64,128]{3,2,1,0:T(8,128)(2,1)S(1)} %third_low.1.refs_1_.low_ref, bf16[6,32,64,128]{3,2,1,0:T(8,128)(2,1)S(1)} %third_inner.1.refs_2_.mid_ref, bf16[1,32,64,128]{3,2,1,0:T(8,128)(2,1)S(1)} %third_high.1.refs_3_.high_ref), custom_call_target="tpu_custom_call" | custom-call | flops 32000000000 | bytes 48000000 | tf_op jit(solution)/shard_map/fourth_inner/pallas_call | solution.py:606
  127.2 4.3 %collective-permute-done.14.below_ref = bf16[1,32,64,128]{3,2,1,0:T(8,128)(2,1)S(1)} collective-permute-done((bf16[1,32,64,128]{3,2,1,0:T(8,128)(2,1)S(1)}, bf16[1,32,64,128]{3,2,1,0:T(8,128)(2,1)S(1)}, u32[]{:S(2)}, u32[]{:S(2)}) %collective-permute-start.14) | collective-permute-done | bytes 524320 | tf_op jit(solution)/shard_map/ppermute | solution.py:647
  131.5 1.8 %ends.1 = f32[8,32,64,128]{3,2,1,0:T(8,128)S(1)} custom-call(f32[24,128]{1,0:T(8,128)S(1)} %get-tuple-element.46.refs_0_.w_ref, bf16[1,32,64,128]{3,2,1,0:T(8,128)(2,1)S(1)} %collective-permute-done.14.below_ref, bf16[1,32,64,128]{3,2,1,0:T(8,128)(2,1)S(1)} %third_low.1.refs_1_.low_ref, ...), custom_call_target="tpu_custom_call", output_to_operand_aliasing={{}: (6, {})} | custom-call | tf_op jit(solution)/shard_map/ends/pallas_call | solution.py:669
  133.3 2.7 %gather.7 = bf16[64,2048]{1,0:T(8,128)(2,1)S(1)} custom-call(s32[2048]{0:T(1024)S(1)} %get-tuple-element.80.spots_ref, s32[1,2048]{1,0:T(1,128)S(1)} %bitcast.29, f32[16384,128]{1,0:T(8,128)S(1)} %bitcast.15), custom_call_target="tpu_custom_call" | custom-call | flops 500000000 | bytes 600000 | tf_op jit(solution)/shard_map/gather/pallas_call | solution.py:713
  136.0 1.6 %collective-permute-start.20 = (bf16[64,2048]{1,0:T(8,128)(2,1)S(1)}, bf16[64,2048]{1,0:T(8,128)(2,1)S(1)}, u32[]{:S(2)}, u32[]{:S(2)}) collective-permute-start(bf16[64,2048]{1,0:T(8,128)(2,1)S(1)} %gather.7), channel_id=1, source_target_pairs={{0,3},{1,2},{2,1},{3,0},{4,7},{5,6},{6,5},{7,4},{8,11},{9,10},{10,... | collective-permute-start | bytes 786440 | tf_op jit(solution)/shard_map/ppermute | solution.py:757
  137.6 2.7 %gather.6 = bf16[64,2048]{1,0:T(8,128)(2,1)S(1)} custom-call(s32[2048]{0:T(1024)S(1)} %get-tuple-element.82.spots_ref, s32[1,2048]{1,0:T(1,128)S(1)} %bitcast.28, f32[16384,128]{1,0:T(8,128)S(1)} %bitcast.16), custom_call_target="tpu_custom_call" | custom-call | flops 500000000 | bytes 600000 | tf_op jit(solution)/shard_map/gather/pallas_call | solution.py:713
  140.9 2.7 %gather.5 = bf16[64,2048]{1,0:T(8,128)(2,1)S(1)} custom-call(s32[2048]{0:T(1024)S(1)} %get-tuple-element.84.spots_ref, s32[1,2048]{1,0:T(1,128)S(1)} %bitcast.27, f32[16384,128]{1,0:T(8,128)S(1)} %bitcast.17), custom_call_target="tpu_custom_call" | custom-call | flops 500000000 | bytes 600000 | tf_op jit(solution)/shard_map/gather/pallas_call | solution.py:713
  145.1 2.7 %gather.4.refs_0_ = bf16[64,2048]{1,0:T(8,128)(2,1)S(1)} custom-call(s32[2048]{0:T(1024)S(1)} %fusion.4.spots_ref, s32[1,2048]{1,0:T(1,128)S(1)} %and_select_fusion.half_ref, f32[16384,128]{1,0:T(8,128)S(1)} %bitcast.18), custom_call_target="tpu_custom_call" | custom-call | flops 500000000 | bytes 600000 | tf_op jit(solution)/shard_map/gather/pallas_call | solution.py:713
  147.8 1.7 %collective-permute-done.19.refs_2_ = bf16[64,2048]{1,0:T(8,128)(2,1)S(1)} collective-permute-done((bf16[64,2048]{1,0:T(8,128)(2,1)S(1)}, bf16[64,2048]{1,0:T(8,128)(2,1)S(1)}, u32[]{:S(2)}, u32[]{:S(2)}) %collective-permute-start.19) | collective-permute-done | bytes 262176 | tf_op jit(solution)/shard_map/ppermute | solution.py:757
  (61 shorter events, 14.4 us)
Async XLA Ops:
  3.3 20.3 %collective-permute-start.3 = (s32[2048]{0:T(1024)}, s32[2048]{0:T(1024)S(1)}, u32[]{:S(2)}, u32[]{:S(2)}) collective-permute-start(s32[2048]{0:T(1024)} %bitcast.19), channel_id=1, source_target_pairs={{0,2},{1,3},{2,0},{3,1},{4,6},{5,7},{6,4},{7,5},{8,10},{9,11},{10,... | collective-permute-start | bytes 24584 | tf_op jit(solution)/shard_map/ppermute | solution.py:757
  6.4 17.3 %collective-permute-start.2 = (s32[2048]{0:T(1024)}, s32[2048]{0:T(1024)S(1)}, u32[]{:S(2)}, u32[]{:S(2)}) collective-permute-start(s32[2048]{0:T(1024)} %bitcast.20), channel_id=1, source_target_pairs={{0,1},{1,0},{2,3},{3,2},{4,5},{5,4},{6,7},{7,6},{8,9},{9,8},{10,11... | collective-permute-start | bytes 24584 | tf_op jit(solution)/shard_map/ppermute | solution.py:757
  7.9 15.9 %collective-permute-start.4 = (bf16[128,2048]{1,0:T(8,128)(2,1)}, bf16[128,2048]{1,0:T(8,128)(2,1)S(1)}, u32[]{:S(2)}, u32[]{:S(2)}) collective-permute-start(bf16[128,2048]{1,0:T(8,128)(2,1)} %get-tuple-element.55), channel_id=1, source_target_pairs={{0,1},{1,0},{2,3},{3,2},{4,5},{5,4},{6,7},{7,6},{8,9},{9,8},{10,11... | collective-permute-start | bytes 1572872 | tf_op jit(solution)/shard_map/ppermute | solution.py:757
  8.4 15.4 %collective-permute-start.5 = (bf16[128,2048]{1,0:T(8,128)(2,1)}, bf16[128,2048]{1,0:T(8,128)(2,1)S(1)}, u32[]{:S(2)}, u32[]{:S(2)}) collective-permute-start(bf16[128,2048]{1,0:T(8,128)(2,1)} %get-tuple-element.56), channel_id=1, source_target_pairs={{0,2},{1,3},{2,0},{3,1},{4,6},{5,7},{6,4},{7,5},{8,10},{9,11},{10,... | collective-permute-start | bytes 1572872 | tf_op jit(solution)/shard_map/ppermute | solution.py:757
  8.5 1.0 copy-start
  10.2 9.0 %copy-start.4 = (bf16[64,64]{1,0:T(8,128)(2,1)S(1)}, bf16[64,64]{1,0:T(8,128)(2,1)}, u32[]{:S(2)}) copy-start(bf16[64,64]{1,0:T(8,128)(2,1)} %p1_ref) | copy-start | bytes 24580
  10.2 9.0 %copy-start.5 = (bf16[64,64]{1,0:T(8,128)(2,1)S(1)}, bf16[64,64]{1,0:T(8,128)(2,1)}, u32[]{:S(2)}) copy-start(bf16[64,64]{1,0:T(8,128)(2,1)} %p2_ref.1) | copy-start | bytes 24580
  10.2 9.0 %copy-start.6 = (f32[3,3,64]{2,1,0:T(4,128)S(1)}, f32[3,3,64]{2,1,0:T(4,128)}, u32[]{:S(2)}) copy-start(f32[3,3,64]{2,1,0:T(4,128)} %t1_ref.1) | copy-start | bytes 6916
  10.2 9.0 %copy-start.7 = (f32[3,3,64]{2,1,0:T(4,128)S(1)}, f32[3,3,64]{2,1,0:T(4,128)}, u32[]{:S(2)}) copy-start(f32[3,3,64]{2,1,0:T(4,128)} %t2_ref.1) | copy-start | bytes 6916
  10.2 9.0 %copy-start.8 = (f32[64]{0:T(128)S(1)}, f32[64]{0:T(128)}, u32[]{:S(2)}) copy-start(f32[64]{0:T(128)} %param.23) | copy-start | bytes 772
  10.2 9.0 %copy-start.9 = (f32[64]{0:T(128)S(1)}, f32[64]{0:T(128)}, u32[]{:S(2)}) copy-start(f32[64]{0:T(128)} %param.24) | copy-start | bytes 772
  10.3 9.0 %copy-start.10 = (f32[64]{0:T(128)S(1)}, f32[64]{0:T(128)}, u32[]{:S(2)}) copy-start(f32[64]{0:T(128)} %param.25) | copy-start | bytes 772
  10.3 11.1 %copy-start.11 = (bf16[128,2048]{1,0:T(8,128)(2,1)S(1)}, bf16[128,2048]{1,0:T(8,128)(2,1)}, u32[]{:S(2)}) copy-start(bf16[128,2048]{1,0:T(8,128)(2,1)} %get-tuple-element.54) | copy-start | bytes 1572868
  16.1 5.3 %collective-permute-start = (s32[2048]{0:T(1024)S(1)}, s32[2048]{0:T(1024)S(1)}, u32[]{:S(2)}, u32[]{:S(2)}) collective-permute-start(s32[2048]{0:T(1024)S(1)} %bitcast.22), channel_id=1, source_target_pairs={{0,3},{1,2},{2,1},{3,0},{4,7},{5,6},{6,5},{7,4},{8,11},{9,10},{10,... | collective-permute-start | bytes 24584 | tf_op jit(solution)/shard_map/ppermute | solution.py:757
  21.4 12.7 %collective-permute-start.1 = (bf16[128,2048]{1,0:T(8,128)(2,1)S(1)}, bf16[128,2048]{1,0:T(8,128)(2,1)S(1)}, u32[]{:S(2)}, u32[]{:S(2)}) collective-permute-start(bf16[128,2048]{1,0:T(8,128)(2,1)S(1)} %copy-done.11), channel_id=1, source_target_pairs={{0,3},{1,2},{2,1},{3,0},{4,7},{5,6},{6,5},{7,4},{8,11},{9,10},{10,... | collective-permute-start | bytes 1572872 | tf_op jit(solution)/shard_map/ppermute | solution.py:757
  40.1 23.4 %collective-permute-start.7 = (bf16[1,64,64,128]{3,2,1,0:T(8,128)(2,1)S(1)}, bf16[1,64,64,128]{3,2,1,0:T(8,128)(2,1)S(1)}, u32[]{:S(2)}, u32[]{:S(2)}) collective-permute-start(bf16[1,64,64,128]{3,2,1,0:T(8,128)(2,1)S(1)} %get-tuple-element.59.refs_3_.refs_2_), channel_id=1, source_target_pairs={{4,0},{8,4},{12,8},{16,12},{20,16},{24,20},{28,24},{0,28},{5,1},{9... | collective-permute-start | bytes 3145736 | tf_op jit(solution)/shard_map/ppermute | solution.py:647
  40.6 27.2 %collective-permute-start.6 = (bf16[1,64,64,128]{3,2,1,0:T(8,128)(2,1)S(1)}, bf16[1,64,64,128]{3,2,1,0:T(8,128)(2,1)S(1)}, u32[]{:S(2)}, u32[]{:S(2)}) collective-permute-start(bf16[1,64,64,128]{3,2,1,0:T(8,128)(2,1)S(1)} %get-tuple-element.58.refs_4_.refs_3_), channel_id=1, source_target_pairs={{0,4},{4,8},{8,12},{12,16},{16,20},{20,24},{24,28},{28,0},{1,5},{5... | collective-permute-start | bytes 3145736 | tf_op jit(solution)/shard_map/ppermute | solution.py:647
  65.8 30.2 %collective-permute-start.10 = (bf16[1,32,64,128]{3,2,1,0:T(8,128)(2,1)S(1)}, bf16[1,32,64,128]{3,2,1,0:T(8,128)(2,1)S(1)}, u32[]{:S(2)}, u32[]{:S(2)}) collective-permute-start(bf16[1,32,64,128]{3,2,1,0:T(8,128)(2,1)S(1)} %get-tuple-element.63.refs_5_.refs_4_), channel_id=1, source_target_pairs={{0,4},{4,8},{8,12},{12,16},{16,20},{20,24},{24,28},{28,0},{1,5},{5... | collective-permute-start | bytes 1572872 | tf_op jit(solution)/shard_map/ppermute | solution.py:647
  66.4 29.7 %collective-permute-start.11 = (bf16[1,32,64,128]{3,2,1,0:T(8,128)(2,1)S(1)}, bf16[1,32,64,128]{3,2,1,0:T(8,128)(2,1)S(1)}, u32[]{:S(2)}, u32[]{:S(2)}) collective-permute-start(bf16[1,32,64,128]{3,2,1,0:T(8,128)(2,1)S(1)} %get-tuple-element.66.refs_8_.refs_7_), channel_id=1, source_target_pairs={{0,4},{4,8},{8,12},{12,16},{16,20},{20,24},{24,28},{28,0},{1,5},{5... | collective-permute-start | bytes 1572872 | tf_op jit(solution)/shard_map/ppermute | solution.py:647
  70.2 18.1 %collective-permute-start.8 = (bf16[1,32,64,128]{3,2,1,0:T(8,128)(2,1)S(1)}, bf16[1,32,64,128]{3,2,1,0:T(8,128)(2,1)S(1)}, u32[]{:S(2)}, u32[]{:S(2)}) collective-permute-start(bf16[1,32,64,128]{3,2,1,0:T(8,128)(2,1)S(1)} %get-tuple-element.61.refs_3_.refs_4_), channel_id=1, source_target_pairs={{4,0},{8,4},{12,8},{16,12},{20,16},{24,20},{28,24},{0,28},{5,1},{9... | collective-permute-start | bytes 1572872 | tf_op jit(solution)/shard_map/ppermute | solution.py:647
  72.3 17.0 %collective-permute-start.9 = (bf16[1,32,64,128]{3,2,1,0:T(8,128)(2,1)S(1)}, bf16[1,32,64,128]{3,2,1,0:T(8,128)(2,1)S(1)}, u32[]{:S(2)}, u32[]{:S(2)}) collective-permute-start(bf16[1,32,64,128]{3,2,1,0:T(8,128)(2,1)S(1)} %get-tuple-element.64.refs_6_.refs_7_), channel_id=1, source_target_pairs={{4,0},{8,4},{12,8},{16,12},{20,16},{24,20},{28,24},{0,28},{5,1},{9... | collective-permute-start | bytes 1572872 | tf_op jit(solution)/shard_map/ppermute | solution.py:647
  92.1 22.4 %collective-permute-start.15 = (bf16[1,32,64,128]{3,2,1,0:T(8,128)(2,1)S(1)}, bf16[1,32,64,128]{3,2,1,0:T(8,128)(2,1)S(1)}, u32[]{:S(2)}, u32[]{:S(2)}) collective-permute-start(bf16[1,32,64,128]{3,2,1,0:T(8,128)(2,1)S(1)} %get-tuple-element.68.refs_3_.refs_4_), channel_id=1, source_target_pairs={{0,4},{4,8},{8,12},{12,16},{16,20},{20,24},{24,28},{28,0},{1,5},{5... | collective-permute-start | bytes 1572872 | tf_op jit(solution)/shard_map/ppermute | solution.py:647
  96.0 18.5 %collective-permute-start.16 = (bf16[1,32,64,128]{3,2,1,0:T(8,128)(2,1)S(1)}, bf16[1,32,64,128]{3,2,1,0:T(8,128)(2,1)S(1)}, u32[]{:S(2)}, u32[]{:S(2)}) collective-permute-start(bf16[1,32,64,128]{3,2,1,0:T(8,128)(2,1)S(1)} %get-tuple-element.71.refs_6_.refs_7_), channel_id=1, source_target_pairs={{0,4},{4,8},{8,12},{12,16},{16,20},{20,24},{24,28},{28,0},{1,5},{5... | collective-permute-start | bytes 1572872 | tf_op jit(solution)/shard_map/ppermute | solution.py:647
  98.9 17.8 %collective-permute-start.12 = (bf16[1,32,64,128]{3,2,1,0:T(8,128)(2,1)S(1)}, bf16[1,32,64,128]{3,2,1,0:T(8,128)(2,1)S(1)}, u32[]{:S(2)}, u32[]{:S(2)}) collective-permute-start(bf16[1,32,64,128]{3,2,1,0:T(8,128)(2,1)S(1)} %get-tuple-element.69.refs_3_.refs_2_), channel_id=1, source_target_pairs={{4,0},{8,4},{12,8},{16,12},{20,16},{24,20},{28,24},{0,28},{5,1},{9... | collective-permute-start | bytes 1572872 | tf_op jit(solution)/shard_map/ppermute | solution.py:647
  102.4 16.4 %collective-permute-start.13 = (bf16[1,32,64,128]{3,2,1,0:T(8,128)(2,1)S(1)}, bf16[1,32,64,128]{3,2,1,0:T(8,128)(2,1)S(1)}, u32[]{:S(2)}, u32[]{:S(2)}) collective-permute-start(bf16[1,32,64,128]{3,2,1,0:T(8,128)(2,1)S(1)} %get-tuple-element.72.refs_6_.refs_5_), channel_id=1, source_target_pairs={{4,0},{8,4},{12,8},{16,12},{20,16},{24,20},{28,24},{0,28},{5,1},{9... | collective-permute-start | bytes 1572872 | tf_op jit(solution)/shard_map/ppermute | solution.py:647
  116.6 10.6 %collective-permute-start.17 = (bf16[1,32,64,128]{3,2,1,0:T(8,128)(2,1)S(1)}, bf16[1,32,64,128]{3,2,1,0:T(8,128)(2,1)S(1)}, u32[]{:S(2)}, u32[]{:S(2)}) collective-permute-start(bf16[1,32,64,128]{3,2,1,0:T(8,128)(2,1)S(1)} %third_low.1.refs_1_.low_ref), channel_id=1, source_target_pairs={{4,0},{8,4},{12,8},{16,12},{20,16},{24,20},{28,24},{0,28},{5,1},{9... | collective-permute-start | bytes 1572872 | tf_op jit(solution)/shard_map/ppermute | solution.py:647
  120.9 10.6 %collective-permute-start.14 = (bf16[1,32,64,128]{3,2,1,0:T(8,128)(2,1)S(1)}, bf16[1,32,64,128]{3,2,1,0:T(8,128)(2,1)S(1)}, u32[]{:S(2)}, u32[]{:S(2)}) collective-permute-start(bf16[1,32,64,128]{3,2,1,0:T(8,128)(2,1)S(1)} %third_high.1.refs_3_.high_ref), channel_id=1, source_target_pairs={{0,4},{4,8},{8,12},{12,16},{16,20},{20,24},{24,28},{28,0},{1,5},{5... | collective-permute-start | bytes 1572872 | tf_op jit(solution)/shard_map/ppermute | solution.py:647
  136.0 11.8 %collective-permute-start.20 = (bf16[64,2048]{1,0:T(8,128)(2,1)S(1)}, bf16[64,2048]{1,0:T(8,128)(2,1)S(1)}, u32[]{:S(2)}, u32[]{:S(2)}) collective-permute-start(bf16[64,2048]{1,0:T(8,128)(2,1)S(1)} %gather.7), channel_id=1, source_target_pairs={{0,3},{1,2},{2,1},{3,0},{4,7},{5,6},{6,5},{7,4},{8,11},{9,10},{10,... | collective-permute-start | bytes 786440 | tf_op jit(solution)/shard_map/ppermute | solution.py:757
  140.3 4.7 %copy-start.3 = (s32[1,2048]{1,0:T(1,128)S(1)}, s32[1,2048]{1,0:T(1,128)}, u32[]{:S(2)}) copy-start(s32[1,2048]{1,0:T(1,128)} %get-tuple-element.43.refs_2_) | copy-start | bytes 24580
  140.3 9.2 %collective-permute-start.19 = (bf16[64,2048]{1,0:T(8,128)(2,1)S(1)}, bf16[64,2048]{1,0:T(8,128)(2,1)S(1)}, u32[]{:S(2)}, u32[]{:S(2)}) collective-permute-start(bf16[64,2048]{1,0:T(8,128)(2,1)S(1)} %gather.6), channel_id=1, source_target_pairs={{0,2},{1,3},{2,0},{3,1},{4,6},{5,7},{6,4},{7,5},{8,10},{9,11},{10,... | collective-permute-start | bytes 786440 | tf_op jit(solution)/shard_map/ppermute | solution.py:757
  143.5 6.5 %copy-start.1 = (f32[64,2048]{1,0:T(8,128)S(1)}, f32[64,2048]{1,0:T(8,128)}, u32[]{:S(2)}) copy-start(f32[64,2048]{1,0:T(8,128)} %get-tuple-element.42.tab_ref) | copy-start | bytes 1572868
  143.5 6.4 %collective-permute-start.18 = (bf16[64,2048]{1,0:T(8,128)(2,1)S(1)}, bf16[64,2048]{1,0:T(8,128)(2,1)S(1)}, u32[]{:S(2)}, u32[]{:S(2)}) collective-permute-start(bf16[64,2048]{1,0:T(8,128)(2,1)S(1)} %gather.5), channel_id=1, source_target_pairs={{0,1},{1,0},{2,3},{3,2},{4,5},{5,4},{6,7},{7,6},{8,9},{9,8},{10,11... | collective-permute-start | bytes 786440 | tf_op jit(solution)/shard_map/ppermute | solution.py:757
  (1 other events, 0.7 us)

commit v6 on v5

--- a/solution.py
+++ b/solution.py
@@ -41,7 +41,7 @@
 def deposits_kernel(peers, width, me_ref, feat_ref, tan_ref, sten_ref, table_ref, route_ref, local_ref, *refs):
     tab_ref, cell_ref = refs[:2]
     outs = refs[2 : peers + 2]
-    feat, tan, sten, rows, route, local, sems, small = refs[peers + 2 :]
+    feat, tan, sten, rows, route, local, tabs, blocks, sems, small, out_sems = refs[peers + 2 :]
     me = me_ref[0]
     parts, _, step = feat.shape
     lists = [
@@ -69,20 +69,29 @@
     y_part = lax.shift_right_logical(place, NG.bit_length() - 1) & (width - 1)
     cell_ref[...] = (z_part * NG + route[...] * width + y_part) * NG + (place & (NG - 1))
     table = rows[...].T
+    sent = []
     for p in range(parts):
         at = pl.ds(p * step, step)
         kinds = jnp.broadcast_to(sten[:, at], (CH, step))
         tab = jnp.zeros((CH, step), F32)
         for s in range(KSETS):
             tab = jnp.where(kinds == s, table[:, s : s + 1], tab)
-        tab_ref[:, at] = tab
+        tabs[p] = tab
+        sent.append(pltpu.make_async_copy(tabs.at[p], tab_ref.at[:, at], out_sems.at[p, peers]))
+        sent[-1].start()
         for copy in copies[p]:
             copy.wait()
         first = (feat[p].astype(F32) * tab).astype(BF16)
         for j in range(peers):
-            outs[j][:CH, at] = first
+            blocks[p, j, :CH, :] = first
             own = tan[p, lax.rem(lax.bitwise_xor(me, j), NT)]
-            outs[j][CH:, at] = (own.astype(F32) * tab).astype(BF16)
+            blocks[p, j, CH:, :] = (own.astype(F32) * tab).astype(BF16)
+            sent.append(
+                pltpu.make_async_copy(blocks.at[p, j], outs[j].at[:, at], out_sems.at[p, j])
+            )
+            sent[-1].start()
+    for copy in sent:
+        copy.wait()
 
 
 def make_deposits(me, features, tangents, stencil, table, route, local, peers):
@@ -98,7 +107,7 @@
         functools.partial(deposits_kernel, peers, NG // peers),
         out_shape=out_shape,
         in_specs=[smem()] + [far] * 6,
-        out_specs=[vmem()] * (peers + 2),
+        out_specs=[far, vmem()] + [far] * peers,
         scratch_shapes=[
             pltpu.VMEM((parts, CH, step), BF16),
             pltpu.VMEM((parts, NT, CH, step), BF16),
@@ -106,8 +115,11 @@
             pltpu.VMEM(table.shape, F32),
             near_row,
             near_row,
+            pltpu.VMEM((parts, CH, step), F32),
+            pltpu.VMEM((parts, peers, LANES, step), BF16),
             pltpu.SemaphoreType.DMA((parts, 2)),
             pltpu.SemaphoreType.DMA((4,)),
+            pltpu.SemaphoreType.DMA((parts, peers + 1)),
         ],
         compiler_params=params(63),
         name="deposits",

time: 152 us -> 152 us (level)
  no operation moved by 1% of the time
where the time goes in v6:
time: 152 us
  Pallas kernels  98.8 us (65%)
  starting transfers between devices  26.3 us (17%)
  waiting for transfers between devices  24.3 us (16%)
  local copies, waits for them, and re-layouts  1.79 us (1%)
    pallas_call x10, Pallas kernels, call_stage(): pl.pallas_call(kernel, out_shape=[jax.ShapeDtypeStruct((layers, HALF, NG,...  60.7 us
    pallas_call x3, Pallas kernels, run_scatter(): pl.pallas_call(functools.partial(kernel, peers), out_shape=out_shape, in_...  19.4 us
    ppermute x9, starting transfers between devices, swap(): return lax.ppermute(array, 'brick', [(i, i ^ j) for i in range(size)])  14 us
    ppermute x6, waiting for transfers between devices, exchange(): lax.ppermute(low, 'slab', down)  12.7 us
    pallas_call x4, Pallas kernels, make_gather(): pl.pallas_call(gather_kernel, out_shape=jax.ShapeDtypeStruct((CH, count),...  10.6 us
    ppermute x6, starting transfers between devices, exchange(): lax.ppermute(low, 'slab', down)  6.76 us
    ppermute x9, waiting for transfers between devices, swap(): return lax.ppermute(array, 'brick', [(i, i ^ j) for i in range(size)])  5.99 us
    ppermute x6, waiting for transfers between devices, exchange(): lax.ppermute(high, 'slab', up)  5.59 us
  transfers between devices with their start and end apart: 21, of which 9 were waited for; matrix products, arithmetic and copies ran while one was open for 0% of the time, Pallas kernels for 55%

profile of v6, /device:TPU:0, one launch (start us, length us, event | category | flops | bytes accessed | tf_op | source)
XLA Modules:
  0.0 151.9 jit_solution(670431855888182609)
XLA Ops:
  0.0 3.7 %deposits.1 = (f32[64,2048]{1,0:T(8,128)}, s32[1,2048]{1,0:T(1,128)}, bf16[128,2048]{1,0:T(8,128)(2,1)}, bf16[128,2048]{1,0:T(8,128)(2,1)}, bf16[128,2048]{1,0:T(8,128)(2,1)}, /*index=5*/bf16[128,2048]{1,0:T(8,128)(2,1)}) custom-call(s32[1]{0:T(128)} %bitcast.me_ref, bf16[64,2048]{1,0:T(8,128)(2,1)} %feat_ref.1, bf16[4,64,2048]{2,1,0:T(8,128)(2,1)} %tan_ref.1, ...), custom_call_target="tpu_custom_call" | custom-call | tf_op jit(solution)/shard_map/deposits/pallas_call | solution.py:106
  3.7 3.0 %collective-permute-start.3 = (s32[2048]{0:T(1024)}, s32[2048]{0:T(1024)S(1)}, u32[]{:S(2)}, u32[]{:S(2)}) collective-permute-start(s32[2048]{0:T(1024)} %bitcast.19), channel_id=1, source_target_pairs={{0,2},{1,3},{2,0},{3,1},{4,6},{5,7},{6,4},{7,5},{8,10},{9,11},{10,... | collective-permute-start | bytes 24584 | tf_op jit(solution)/shard_map/ppermute | solution.py:769
  10.6 5.9 %own_sums.1.refs_6_ = f32[32768,128]{1,0:T(8,128)S(1)} custom-call(s32[2048]{0:T(1024)S(1)} %bitcast.21, bf16[128,2048]{1,0:T(8,128)(2,1)S(1)} %copy-done, s32[1,2048]{1,0:T(1,128)S(1)} %copy-done.2), custom_call_target="tpu_custom_call" | custom-call | flops 500000000 | bytes 800000 | tf_op jit(solution)/shard_map/own_sums/pallas_call | solution.py:238
  16.5 2.9 %collective-permute-start = (s32[2048]{0:T(1024)S(1)}, s32[2048]{0:T(1024)S(1)}, u32[]{:S(2)}, u32[]{:S(2)}) collective-permute-start(s32[2048]{0:T(1024)S(1)} %bitcast.22), channel_id=1, source_target_pairs={{0,3},{1,2},{2,1},{3,0},{4,7},{5,6},{6,5},{7,4},{8,11},{9,10},{10,... | collective-permute-start | bytes 24584 | tf_op jit(solution)/shard_map/ppermute | solution.py:769
  19.8 2.0 %collective-permute-done.refs_0_ = s32[2048]{0:T(1024)S(1)} collective-permute-done((s32[2048]{0:T(1024)S(1)}, s32[2048]{0:T(1024)S(1)}, u32[]{:S(2)}, u32[]{:S(2)}) %collective-permute-start) | collective-permute-done | bytes 8224 | tf_op jit(solution)/shard_map/ppermute | solution.py:769
  21.8 2.2 %collective-permute-start.1 = (bf16[128,2048]{1,0:T(8,128)(2,1)S(1)}, bf16[128,2048]{1,0:T(8,128)(2,1)S(1)}, u32[]{:S(2)}, u32[]{:S(2)}) collective-permute-start(bf16[128,2048]{1,0:T(8,128)(2,1)S(1)} %copy-done.11), channel_id=1, source_target_pairs={{0,3},{1,2},{2,1},{3,0},{4,7},{5,6},{6,5},{7,4},{8,11},{9,10},{10,... | collective-permute-start | bytes 1572872 | tf_op jit(solution)/shard_map/ppermute | solution.py:769
  24.1 8.6 %more_sums.1.refs_3_ = f32[32768,128]{1,0:T(8,128)S(1)} custom-call(s32[2048]{0:T(1024)S(1)} %collective-permute-done.2.refs_0_, s32[2048]{0:T(1024)S(1)} %collective-permute-done.3.refs_1_, bf16[128,2048]{1,0:T(8,128)(2,1)S(1)} %collective-permute-done.4.refs_2_, ...), custom_call_target="tpu_custom_call", output_to_operand_aliasing={{}: (6, {})} | custom-call | flops 1000000000 | bytes 1600000 | tf_op jit(solution)/shard_map/more_sums/pallas_call | solution.py:238
  32.7 1.7 %collective-permute-done.1.refs_1_ = bf16[128,2048]{1,0:T(8,128)(2,1)S(1)} collective-permute-done((bf16[128,2048]{1,0:T(8,128)(2,1)S(1)}, bf16[128,2048]{1,0:T(8,128)(2,1)S(1)}, u32[]{:S(2)}, u32[]{:S(2)}) %collective-permute-start.1) | collective-permute-done | bytes 524320 | tf_op jit(solution)/shard_map/ppermute | solution.py:769
  34.5 4.9 %charge.1 = (f32[32768,128]{1,0:T(8,128)S(1)}, bf16[1,64,64,128]{3,2,1,0:T(8,128)(2,1)S(1)}, bf16[1,64,64,128]{3,2,1,0:T(8,128)(2,1)S(1)}) custom-call(s32[2048]{0:T(1024)S(1)} %collective-permute-done.refs_0_, bf16[128,2048]{1,0:T(8,128)(2,1)S(1)} %collective-permute-done.1.refs_1_, s32[1,2048]{1,0:T(1,128)S(1)} %bitcast.24, ...), custom_call_target="tpu_custom_call", output_to_operand_aliasing={{0}: (3, {})} | custom-call | flops 500000000 | bytes 800000 | tf_op jit(solution)/shard_map/charge/pallas_call | solution.py:238
  41.0 13.4 %first_inner.1 = (bf16[6,32,64,128]{3,2,1,0:T(8,128)(2,1)S(1)}, bf16[6,32,64,128]{3,2,1,0:T(8,128)(2,1)S(1)}, f32[6,32,64,128]{3,2,1,0:T(8,128)S(1)}, f32[6,32,64,128]{3,2,1,0:T(8,128)S(1)}) custom-call(f32[24,128]{1,0:T(8,128)S(1)} %get-tuple-element.46.refs_0_.w_ref, bf16[256,256]{1,0:T(8,128)(2,1)S(1)} %get-tuple-element.50.refs_1_, ...), custom_call_target="tpu_custom_call" | custom-call | flops 24000000000 | bytes 36000000 | tf_op jit(solution)/shard_map/first_inner/pallas_call | solution.py:618
  54.4 9.4 %collective-permute-done.7.refs_4_ = bf16[1,64,64,128]{3,2,1,0:T(8,128)(2,1)S(1)} collective-permute-done((bf16[1,64,64,128]{3,2,1,0:T(8,128)(2,1)S(1)}, bf16[1,64,64,128]{3,2,1,0:T(8,128)(2,1)S(1)}, u32[]{:S(2)}, u32[]{:S(2)}) %collective-permute-start.7) | collective-permute-done | bytes 1048608 | tf_op jit(solution)/shard_map/ppermute | solution.py:659
  63.8 2.3 %first_high.1 = (bf16[1,32,64,128]{3,2,1,0:T(8,128)(2,1)S(1)}, bf16[1,32,64,128]{3,2,1,0:T(8,128)(2,1)S(1)}, f32[1,32,64,128]{3,2,1,0:T(8,128)S(1)}, f32[1,32,64,128]{3,2,1,0:T(8,128)S(1)}) custom-call(f32[24,128]{1,0:T(8,128)S(1)} %get-tuple-element.46.refs_0_.w_ref, bf16[256,256]{1,0:T(8,128)(2,1)S(1)} %get-tuple-element.50.refs_1_, ...), custom_call_target="tpu_custom_call" | custom-call | flops 4000000000 | bytes 6000000 | tf_op jit(solution)/shard_map/first_high/pallas_call | solution.py:618
  68.2 2.3 %first_low.1 = (bf16[1,32,64,128]{3,2,1,0:T(8,128)(2,1)S(1)}, bf16[1,32,64,128]{3,2,1,0:T(8,128)(2,1)S(1)}, f32[1,32,64,128]{3,2,1,0:T(8,128)S(1)}, f32[1,32,64,128]{3,2,1,0:T(8,128)S(1)}) custom-call(f32[24,128]{1,0:T(8,128)S(1)} %get-tuple-element.46.refs_0_.w_ref, bf16[256,256]{1,0:T(8,128)(2,1)S(1)} %get-tuple-element.50.refs_1_, ...), custom_call_target="tpu_custom_call" | custom-call | flops 4000000000 | bytes 6000000 | tf_op jit(solution)/shard_map/first_low/pallas_call | solution.py:618
  70.5 2.2 %collective-permute-start.8 = (bf16[1,32,64,128]{3,2,1,0:T(8,128)(2,1)S(1)}, bf16[1,32,64,128]{3,2,1,0:T(8,128)(2,1)S(1)}, u32[]{:S(2)}, u32[]{:S(2)}) collective-permute-start(bf16[1,32,64,128]{3,2,1,0:T(8,128)(2,1)S(1)} %get-tuple-element.61.refs_3_.refs_4_), channel_id=1, source_target_pairs={{4,0},{8,4},{12,8},{16,12},{20,16},{24,20},{28,24},{0,28},{5,1},{9... | collective-permute-start | bytes 1572872 | tf_op jit(solution)/shard_map/ppermute | solution.py:659
  72.9 15.7 %second_inner.1 = (bf16[6,32,64,128]{3,2,1,0:T(8,128)(2,1)S(1)}, bf16[6,32,64,128]{3,2,1,0:T(8,128)(2,1)S(1)}) custom-call(f32[24,128]{1,0:T(8,128)S(1)} %get-tuple-element.46.refs_0_.w_ref, bf16[256,256]{1,0:T(8,128)(2,1)S(1)} %get-tuple-element.48.refs_1_, bf16[256,256]{1,0:T(8,128)(2,1)S(1)} %get-tuple-element.49.refs_2_, ...), custom_call_target="tpu_custom_call" | custom-call | flops 24000000000 | bytes 36000000 | tf_op jit(solution)/shard_map/second_inner/pallas_call | solution.py:618
  89.7 2.8 %second_high.1 = (bf16[1,32,64,128]{3,2,1,0:T(8,128)(2,1)S(1)}, bf16[1,32,64,128]{3,2,1,0:T(8,128)(2,1)S(1)}) custom-call(f32[24,128]{1,0:T(8,128)S(1)} %get-tuple-element.46.refs_0_.w_ref, bf16[256,256]{1,0:T(8,128)(2,1)S(1)} %get-tuple-element.48.refs_1_, bf16[256,256]{1,0:T(8,128)(2,1)S(1)} %get-tuple-element.49.refs_2_, ...), custom_call_target="tpu_custom_call" | custom-call | flops 4000000000 | bytes 6000000 | tf_op jit(solution)/shard_map/second_high/pallas_call | solution.py:618
  92.5 3.8 %collective-permute-start.15 = (bf16[1,32,64,128]{3,2,1,0:T(8,128)(2,1)S(1)}, bf16[1,32,64,128]{3,2,1,0:T(8,128)(2,1)S(1)}, u32[]{:S(2)}, u32[]{:S(2)}) collective-permute-start(bf16[1,32,64,128]{3,2,1,0:T(8,128)(2,1)S(1)} %get-tuple-element.68.refs_3_.refs_4_), channel_id=1, source_target_pairs={{0,4},{4,8},{8,12},{12,16},{16,20},{20,24},{24,28},{28,0},{1,5},{5... | collective-permute-start | bytes 1572872 | tf_op jit(solution)/shard_map/ppermute | solution.py:659
  96.4 2.8 %second_low.1 = (bf16[1,32,64,128]{3,2,1,0:T(8,128)(2,1)S(1)}, bf16[1,32,64,128]{3,2,1,0:T(8,128)(2,1)S(1)}) custom-call(f32[24,128]{1,0:T(8,128)S(1)} %get-tuple-element.46.refs_0_.w_ref, bf16[256,256]{1,0:T(8,128)(2,1)S(1)} %get-tuple-element.48.refs_1_, bf16[256,256]{1,0:T(8,128)(2,1)S(1)} %get-tuple-element.49.refs_2_, ...), custom_call_target="tpu_custom_call" | custom-call | flops 4000000000 | bytes 6000000 | tf_op jit(solution)/shard_map/second_low/pallas_call | solution.py:618
  99.2 3.5 %collective-permute-start.12 = (bf16[1,32,64,128]{3,2,1,0:T(8,128)(2,1)S(1)}, bf16[1,32,64,128]{3,2,1,0:T(8,128)(2,1)S(1)}, u32[]{:S(2)}, u32[]{:S(2)}) collective-permute-start(bf16[1,32,64,128]{3,2,1,0:T(8,128)(2,1)S(1)} %get-tuple-element.69.refs_3_.refs_2_), channel_id=1, source_target_pairs={{4,0},{8,4},{12,8},{16,12},{20,16},{24,20},{28,24},{0,28},{5,1},{9... | collective-permute-start | bytes 1572872 | tf_op jit(solution)/shard_map/ppermute | solution.py:659
  103.0 11.8 %third_inner.1.refs_2_.mid_ref = bf16[6,32,64,128]{3,2,1,0:T(8,128)(2,1)S(1)} custom-call(f32[24,128]{1,0:T(8,128)S(1)} %get-tuple-element.46.refs_0_.w_ref, bf16[128,128]{1,0:T(8,128)(2,1)S(1)} %get-tuple-element.47.refs_1_, bf16[1,32,64,128]{3,2,1,0:T(8,128)(2,1)S(1)} %get-tuple-element.69.refs_3_.refs_2_, ...), custom_call_target="tpu_custom_call" | custom-call | flops 24000000000 | bytes 36000000 | tf_op jit(solution)/shard_map/third_inner/pallas_call | solution.py:618
  114.9 2.1 %third_low.1.refs_1_.low_ref = bf16[1,32,64,128]{3,2,1,0:T(8,128)(2,1)S(1)} custom-call(f32[24,128]{1,0:T(8,128)S(1)} %get-tuple-element.46.refs_0_.w_ref, bf16[128,128]{1,0:T(8,128)(2,1)S(1)} %get-tuple-element.47.refs_1_, bf16[1,32,64,128]{3,2,1,0:T(8,128)(2,1)S(1)} %collective-permute-done.15.refs_2_, ...), custom_call_target="tpu_custom_call" | custom-call | flops 4000000000 | bytes 6000000 | tf_op jit(solution)/shard_map/third_low/pallas_call | solution.py:618
  117.0 2.2 %collective-permute-done.13.refs_7_ = bf16[1,32,64,128]{3,2,1,0:T(8,128)(2,1)S(1)} collective-permute-done((bf16[1,32,64,128]{3,2,1,0:T(8,128)(2,1)S(1)}, bf16[1,32,64,128]{3,2,1,0:T(8,128)(2,1)S(1)}, u32[]{:S(2)}, u32[]{:S(2)}) %collective-permute-start.13) | collective-permute-done | bytes 524320 | tf_op jit(solution)/shard_map/ppermute | solution.py:659
  119.2 2.0 %third_high.1.refs_3_.high_ref = bf16[1,32,64,128]{3,2,1,0:T(8,128)(2,1)S(1)} custom-call(f32[24,128]{1,0:T(8,128)S(1)} %get-tuple-element.46.refs_0_.w_ref, bf16[128,128]{1,0:T(8,128)(2,1)S(1)} %get-tuple-element.47.refs_1_, bf16[6,32,64,128]{3,2,1,0:T(8,128)(2,1)S(1)} %get-tuple-element.67.refs_2_.refs_4_.refs_3_, ...), custom_call_target="tpu_custom_call" | custom-call | flops 4000000000 | bytes 6000000 | tf_op jit(solution)/shard_map/third_high/pallas_call | solution.py:618
  122.2 5.3 %fourth_inner.1._ = f32[8,32,64,128]{3,2,1,0:T(8,128)S(1)} custom-call(f32[24,128]{1,0:T(8,128)S(1)} %get-tuple-element.46.refs_0_.w_ref, bf16[1,32,64,128]{3,2,1,0:T(8,128)(2,1)S(1)} %third_low.1.refs_1_.low_ref, bf16[6,32,64,128]{3,2,1,0:T(8,128)(2,1)S(1)} %third_inner.1.refs_2_.mid_ref, bf16[1,32,64,128]{3,2,1,0:T(8,128)(2,1)S(1)} %third_high.1.refs_3_.high_ref), custom_call_target="tpu_custom_call" | custom-call | flops 32000000000 | bytes 48000000 | tf_op jit(solution)/shard_map/fourth_inner/pallas_call | solution.py:618
  127.6 4.3 %collective-permute-done.14.below_ref = bf16[1,32,64,128]{3,2,1,0:T(8,128)(2,1)S(1)} collective-permute-done((bf16[1,32,64,128]{3,2,1,0:T(8,128)(2,1)S(1)}, bf16[1,32,64,128]{3,2,1,0:T(8,128)(2,1)S(1)}, u32[]{:S(2)}, u32[]{:S(2)}) %collective-permute-start.14) | collective-permute-done | bytes 524320 | tf_op jit(solution)/shard_map/ppermute | solution.py:659
  131.9 1.8 %ends.1 = f32[8,32,64,128]{3,2,1,0:T(8,128)S(1)} custom-call(f32[24,128]{1,0:T(8,128)S(1)} %get-tuple-element.46.refs_0_.w_ref, bf16[1,32,64,128]{3,2,1,0:T(8,128)(2,1)S(1)} %collective-permute-done.14.below_ref, bf16[1,32,64,128]{3,2,1,0:T(8,128)(2,1)S(1)} %third_low.1.refs_1_.low_ref, ...), custom_call_target="tpu_custom_call", output_to_operand_aliasing={{}: (6, {})} | custom-call | tf_op jit(solution)/shard_map/ends/pallas_call | solution.py:681
  133.7 2.7 %gather.7 = bf16[64,2048]{1,0:T(8,128)(2,1)S(1)} custom-call(s32[2048]{0:T(1024)S(1)} %get-tuple-element.80.spots_ref, s32[1,2048]{1,0:T(1,128)S(1)} %bitcast.29, f32[16384,128]{1,0:T(8,128)S(1)} %bitcast.15), custom_call_target="tpu_custom_call" | custom-call | flops 500000000 | bytes 600000 | tf_op jit(solution)/shard_map/gather/pallas_call | solution.py:725
  136.3 1.7 %collective-permute-start.20 = (bf16[64,2048]{1,0:T(8,128)(2,1)S(1)}, bf16[64,2048]{1,0:T(8,128)(2,1)S(1)}, u32[]{:S(2)}, u32[]{:S(2)}) collective-permute-start(bf16[64,2048]{1,0:T(8,128)(2,1)S(1)} %gather.7), channel_id=1, source_target_pairs={{0,3},{1,2},{2,1},{3,0},{4,7},{5,6},{6,5},{7,4},{8,11},{9,10},{10,... | collective-permute-start | bytes 786440 | tf_op jit(solution)/shard_map/ppermute | solution.py:769
  138.0 2.7 %gather.6 = bf16[64,2048]{1,0:T(8,128)(2,1)S(1)} custom-call(s32[2048]{0:T(1024)S(1)} %get-tuple-element.82.spots_ref, s32[1,2048]{1,0:T(1,128)S(1)} %bitcast.28, f32[16384,128]{1,0:T(8,128)S(1)} %bitcast.16), custom_call_target="tpu_custom_call" | custom-call | flops 500000000 | bytes 600000 | tf_op jit(solution)/shard_map/gather/pallas_call | solution.py:725
  141.3 2.7 %gather.5 = bf16[64,2048]{1,0:T(8,128)(2,1)S(1)} custom-call(s32[2048]{0:T(1024)S(1)} %get-tuple-element.84.spots_ref, s32[1,2048]{1,0:T(1,128)S(1)} %bitcast.27, f32[16384,128]{1,0:T(8,128)S(1)} %bitcast.17), custom_call_target="tpu_custom_call" | custom-call | flops 500000000 | bytes 600000 | tf_op jit(solution)/shard_map/gather/pallas_call | solution.py:725
  145.4 2.7 %gather.4.refs_0_ = bf16[64,2048]{1,0:T(8,128)(2,1)S(1)} custom-call(s32[2048]{0:T(1024)S(1)} %fusion.4.spots_ref, s32[1,2048]{1,0:T(1,128)S(1)} %and_select_fusion.half_ref, f32[16384,128]{1,0:T(8,128)S(1)} %bitcast.18), custom_call_target="tpu_custom_call" | custom-call | flops 500000000 | bytes 600000 | tf_op jit(solution)/shard_map/gather/pallas_call | solution.py:725
  148.1 1.7 %collective-permute-done.19.refs_2_ = bf16[64,2048]{1,0:T(8,128)(2,1)S(1)} collective-permute-done((bf16[64,2048]{1,0:T(8,128)(2,1)S(1)}, bf16[64,2048]{1,0:T(8,128)(2,1)S(1)}, u32[]{:S(2)}, u32[]{:S(2)}) %collective-permute-start.19) | collective-permute-done | bytes 262176 | tf_op jit(solution)/shard_map/ppermute | solution.py:769
  (61 shorter events, 14.5 us)
Async XLA Ops:
  3.7 20.3 %collective-permute-start.3 = (s32[2048]{0:T(1024)}, s32[2048]{0:T(1024)S(1)}, u32[]{:S(2)}, u32[]{:S(2)}) collective-permute-start(s32[2048]{0:T(1024)} %bitcast.19), channel_id=1, source_target_pairs={{0,2},{1,3},{2,0},{3,1},{4,6},{5,7},{6,4},{7,5},{8,10},{9,11},{10,... | collective-permute-start | bytes 24584 | tf_op jit(solution)/shard_map/ppermute | solution.py:769
  6.7 17.3 %collective-permute-start.2 = (s32[2048]{0:T(1024)}, s32[2048]{0:T(1024)S(1)}, u32[]{:S(2)}, u32[]{:S(2)}) collective-permute-start(s32[2048]{0:T(1024)} %bitcast.20), channel_id=1, source_target_pairs={{0,1},{1,0},{2,3},{3,2},{4,5},{5,4},{6,7},{7,6},{8,9},{9,8},{10,11... | collective-permute-start | bytes 24584 | tf_op jit(solution)/shard_map/ppermute | solution.py:769
  8.2 15.9 %collective-permute-start.4 = (bf16[128,2048]{1,0:T(8,128)(2,1)}, bf16[128,2048]{1,0:T(8,128)(2,1)S(1)}, u32[]{:S(2)}, u32[]{:S(2)}) collective-permute-start(bf16[128,2048]{1,0:T(8,128)(2,1)} %get-tuple-element.55), channel_id=1, source_target_pairs={{0,1},{1,0},{2,3},{3,2},{4,5},{5,4},{6,7},{7,6},{8,9},{9,8},{10,11... | collective-permute-start | bytes 1572872 | tf_op jit(solution)/shard_map/ppermute | solution.py:769
  8.8 15.4 %collective-permute-start.5 = (bf16[128,2048]{1,0:T(8,128)(2,1)}, bf16[128,2048]{1,0:T(8,128)(2,1)S(1)}, u32[]{:S(2)}, u32[]{:S(2)}) collective-permute-start(bf16[128,2048]{1,0:T(8,128)(2,1)} %get-tuple-element.56), channel_id=1, source_target_pairs={{0,2},{1,3},{2,0},{3,1},{4,6},{5,7},{6,4},{7,5},{8,10},{9,11},{10,... | collective-permute-start | bytes 1572872 | tf_op jit(solution)/shard_map/ppermute | solution.py:769
  8.8 1.0 copy-start
  10.6 9.0 %copy-start.4 = (bf16[64,64]{1,0:T(8,128)(2,1)S(1)}, bf16[64,64]{1,0:T(8,128)(2,1)}, u32[]{:S(2)}) copy-start(bf16[64,64]{1,0:T(8,128)(2,1)} %p1_ref) | copy-start | bytes 24580
  10.6 9.0 %copy-start.5 = (bf16[64,64]{1,0:T(8,128)(2,1)S(1)}, bf16[64,64]{1,0:T(8,128)(2,1)}, u32[]{:S(2)}) copy-start(bf16[64,64]{1,0:T(8,128)(2,1)} %p2_ref.1) | copy-start | bytes 24580
  10.6 9.0 %copy-start.6 = (f32[3,3,64]{2,1,0:T(4,128)S(1)}, f32[3,3,64]{2,1,0:T(4,128)}, u32[]{:S(2)}) copy-start(f32[3,3,64]{2,1,0:T(4,128)} %t1_ref.1) | copy-start | bytes 6916
  10.6 9.0 %copy-start.7 = (f32[3,3,64]{2,1,0:T(4,128)S(1)}, f32[3,3,64]{2,1,0:T(4,128)}, u32[]{:S(2)}) copy-start(f32[3,3,64]{2,1,0:T(4,128)} %t2_ref.1) | copy-start | bytes 6916
  10.6 9.0 %copy-start.8 = (f32[64]{0:T(128)S(1)}, f32[64]{0:T(128)}, u32[]{:S(2)}) copy-start(f32[64]{0:T(128)} %param.23) | copy-start | bytes 772
  10.6 9.0 %copy-start.9 = (f32[64]{0:T(128)S(1)}, f32[64]{0:T(128)}, u32[]{:S(2)}) copy-start(f32[64]{0:T(128)} %param.24) | copy-start | bytes 772
  10.6 9.0 %copy-start.10 = (f32[64]{0:T(128)S(1)}, f32[64]{0:T(128)}, u32[]{:S(2)}) copy-start(f32[64]{0:T(128)} %param.25) | copy-start | bytes 772
  10.6 11.1 %copy-start.11 = (bf16[128,2048]{1,0:T(8,128)(2,1)S(1)}, bf16[128,2048]{1,0:T(8,128)(2,1)}, u32[]{:S(2)}) copy-start(bf16[128,2048]{1,0:T(8,128)(2,1)} %get-tuple-element.54) | copy-start | bytes 1572868
  16.5 5.3 %collective-permute-start = (s32[2048]{0:T(1024)S(1)}, s32[2048]{0:T(1024)S(1)}, u32[]{:S(2)}, u32[]{:S(2)}) collective-permute-start(s32[2048]{0:T(1024)S(1)} %bitcast.22), channel_id=1, source_target_pairs={{0,3},{1,2},{2,1},{3,0},{4,7},{5,6},{6,5},{7,4},{8,11},{9,10},{10,... | collective-permute-start | bytes 24584 | tf_op jit(solution)/shard_map/ppermute | solution.py:769
  21.8 12.7 %collective-permute-start.1 = (bf16[128,2048]{1,0:T(8,128)(2,1)S(1)}, bf16[128,2048]{1,0:T(8,128)(2,1)S(1)}, u32[]{:S(2)}, u32[]{:S(2)}) collective-permute-start(bf16[128,2048]{1,0:T(8,128)(2,1)S(1)} %copy-done.11), channel_id=1, source_target_pairs={{0,3},{1,2},{2,1},{3,0},{4,7},{5,6},{6,5},{7,4},{8,11},{9,10},{10,... | collective-permute-start | bytes 1572872 | tf_op jit(solution)/shard_map/ppermute | solution.py:769
  40.4 23.4 %collective-permute-start.7 = (bf16[1,64,64,128]{3,2,1,0:T(8,128)(2,1)S(1)}, bf16[1,64,64,128]{3,2,1,0:T(8,128)(2,1)S(1)}, u32[]{:S(2)}, u32[]{:S(2)}) collective-permute-start(bf16[1,64,64,128]{3,2,1,0:T(8,128)(2,1)S(1)} %get-tuple-element.59.refs_3_.refs_2_), channel_id=1, source_target_pairs={{4,0},{8,4},{12,8},{16,12},{20,16},{24,20},{28,24},{0,28},{5,1},{9... | collective-permute-start | bytes 3145736 | tf_op jit(solution)/shard_map/ppermute | solution.py:659
  41.0 27.2 %collective-permute-start.6 = (bf16[1,64,64,128]{3,2,1,0:T(8,128)(2,1)S(1)}, bf16[1,64,64,128]{3,2,1,0:T(8,128)(2,1)S(1)}, u32[]{:S(2)}, u32[]{:S(2)}) collective-permute-start(bf16[1,64,64,128]{3,2,1,0:T(8,128)(2,1)S(1)} %get-tuple-element.58.refs_4_.refs_3_), channel_id=1, source_target_pairs={{0,4},{4,8},{8,12},{12,16},{16,20},{20,24},{24,28},{28,0},{1,5},{5... | collective-permute-start | bytes 3145736 | tf_op jit(solution)/shard_map/ppermute | solution.py:659
  66.1 30.2 %collective-permute-start.10 = (bf16[1,32,64,128]{3,2,1,0:T(8,128)(2,1)S(1)}, bf16[1,32,64,128]{3,2,1,0:T(8,128)(2,1)S(1)}, u32[]{:S(2)}, u32[]{:S(2)}) collective-permute-start(bf16[1,32,64,128]{3,2,1,0:T(8,128)(2,1)S(1)} %get-tuple-element.63.refs_5_.refs_4_), channel_id=1, source_target_pairs={{0,4},{4,8},{8,12},{12,16},{16,20},{20,24},{24,28},{28,0},{1,5},{5... | collective-permute-start | bytes 1572872 | tf_op jit(solution)/shard_map/ppermute | solution.py:659
  66.8 29.6 %collective-permute-start.11 = (bf16[1,32,64,128]{3,2,1,0:T(8,128)(2,1)S(1)}, bf16[1,32,64,128]{3,2,1,0:T(8,128)(2,1)S(1)}, u32[]{:S(2)}, u32[]{:S(2)}) collective-permute-start(bf16[1,32,64,128]{3,2,1,0:T(8,128)(2,1)S(1)} %get-tuple-element.66.refs_8_.refs_7_), channel_id=1, source_target_pairs={{0,4},{4,8},{8,12},{12,16},{16,20},{20,24},{24,28},{28,0},{1,5},{5... | collective-permute-start | bytes 1572872 | tf_op jit(solution)/shard_map/ppermute | solution.py:659
  70.5 18.1 %collective-permute-start.8 = (bf16[1,32,64,128]{3,2,1,0:T(8,128)(2,1)S(1)}, bf16[1,32,64,128]{3,2,1,0:T(8,128)(2,1)S(1)}, u32[]{:S(2)}, u32[]{:S(2)}) collective-permute-start(bf16[1,32,64,128]{3,2,1,0:T(8,128)(2,1)S(1)} %get-tuple-element.61.refs_3_.refs_4_), channel_id=1, source_target_pairs={{4,0},{8,4},{12,8},{16,12},{20,16},{24,20},{28,24},{0,28},{5,1},{9... | collective-permute-start | bytes 1572872 | tf_op jit(solution)/shard_map/ppermute | solution.py:659
  72.8 17.0 %collective-permute-start.9 = (bf16[1,32,64,128]{3,2,1,0:T(8,128)(2,1)S(1)}, bf16[1,32,64,128]{3,2,1,0:T(8,128)(2,1)S(1)}, u32[]{:S(2)}, u32[]{:S(2)}) collective-permute-start(bf16[1,32,64,128]{3,2,1,0:T(8,128)(2,1)S(1)} %get-tuple-element.64.refs_6_.refs_7_), channel_id=1, source_target_pairs={{4,0},{8,4},{12,8},{16,12},{20,16},{24,20},{28,24},{0,28},{5,1},{9... | collective-permute-start | bytes 1572872 | tf_op jit(solution)/shard_map/ppermute | solution.py:659
  92.5 22.3 %collective-permute-start.15 = (bf16[1,32,64,128]{3,2,1,0:T(8,128)(2,1)S(1)}, bf16[1,32,64,128]{3,2,1,0:T(8,128)(2,1)S(1)}, u32[]{:S(2)}, u32[]{:S(2)}) collective-permute-start(bf16[1,32,64,128]{3,2,1,0:T(8,128)(2,1)S(1)} %get-tuple-element.68.refs_3_.refs_4_), channel_id=1, source_target_pairs={{0,4},{4,8},{8,12},{12,16},{16,20},{20,24},{24,28},{28,0},{1,5},{5... | collective-permute-start | bytes 1572872 | tf_op jit(solution)/shard_map/ppermute | solution.py:659
  96.3 18.5 %collective-permute-start.16 = (bf16[1,32,64,128]{3,2,1,0:T(8,128)(2,1)S(1)}, bf16[1,32,64,128]{3,2,1,0:T(8,128)(2,1)S(1)}, u32[]{:S(2)}, u32[]{:S(2)}) collective-permute-start(bf16[1,32,64,128]{3,2,1,0:T(8,128)(2,1)S(1)} %get-tuple-element.71.refs_6_.refs_7_), channel_id=1, source_target_pairs={{0,4},{4,8},{8,12},{12,16},{16,20},{20,24},{24,28},{28,0},{1,5},{5... | collective-permute-start | bytes 1572872 | tf_op jit(solution)/shard_map/ppermute | solution.py:659
  99.2 17.8 %collective-permute-start.12 = (bf16[1,32,64,128]{3,2,1,0:T(8,128)(2,1)S(1)}, bf16[1,32,64,128]{3,2,1,0:T(8,128)(2,1)S(1)}, u32[]{:S(2)}, u32[]{:S(2)}) collective-permute-start(bf16[1,32,64,128]{3,2,1,0:T(8,128)(2,1)S(1)} %get-tuple-element.69.refs_3_.refs_2_), channel_id=1, source_target_pairs={{4,0},{8,4},{12,8},{16,12},{20,16},{24,20},{28,24},{0,28},{5,1},{9... | collective-permute-start | bytes 1572872 | tf_op jit(solution)/shard_map/ppermute | solution.py:659
  102.7 16.4 %collective-permute-start.13 = (bf16[1,32,64,128]{3,2,1,0:T(8,128)(2,1)S(1)}, bf16[1,32,64,128]{3,2,1,0:T(8,128)(2,1)S(1)}, u32[]{:S(2)}, u32[]{:S(2)}) collective-permute-start(bf16[1,32,64,128]{3,2,1,0:T(8,128)(2,1)S(1)} %get-tuple-element.72.refs_6_.refs_5_), channel_id=1, source_target_pairs={{4,0},{8,4},{12,8},{16,12},{20,16},{24,20},{28,24},{0,28},{5,1},{9... | collective-permute-start | bytes 1572872 | tf_op jit(solution)/shard_map/ppermute | solution.py:659
  116.9 10.6 %collective-permute-start.17 = (bf16[1,32,64,128]{3,2,1,0:T(8,128)(2,1)S(1)}, bf16[1,32,64,128]{3,2,1,0:T(8,128)(2,1)S(1)}, u32[]{:S(2)}, u32[]{:S(2)}) collective-permute-start(bf16[1,32,64,128]{3,2,1,0:T(8,128)(2,1)S(1)} %third_low.1.refs_1_.low_ref), channel_id=1, source_target_pairs={{4,0},{8,4},{12,8},{16,12},{20,16},{24,20},{28,24},{0,28},{5,1},{9... | collective-permute-start | bytes 1572872 | tf_op jit(solution)/shard_map/ppermute | solution.py:659
  121.2 10.6 %collective-permute-start.14 = (bf16[1,32,64,128]{3,2,1,0:T(8,128)(2,1)S(1)}, bf16[1,32,64,128]{3,2,1,0:T(8,128)(2,1)S(1)}, u32[]{:S(2)}, u32[]{:S(2)}) collective-permute-start(bf16[1,32,64,128]{3,2,1,0:T(8,128)(2,1)S(1)} %third_high.1.refs_3_.high_ref), channel_id=1, source_target_pairs={{0,4},{4,8},{8,12},{12,16},{16,20},{20,24},{24,28},{28,0},{1,5},{5... | collective-permute-start | bytes 1572872 | tf_op jit(solution)/shard_map/ppermute | solution.py:659
  136.3 11.8 %collective-permute-start.20 = (bf16[64,2048]{1,0:T(8,128)(2,1)S(1)}, bf16[64,2048]{1,0:T(8,128)(2,1)S(1)}, u32[]{:S(2)}, u32[]{:S(2)}) collective-permute-start(bf16[64,2048]{1,0:T(8,128)(2,1)S(1)} %gather.7), channel_id=1, source_target_pairs={{0,3},{1,2},{2,1},{3,0},{4,7},{5,6},{6,5},{7,4},{8,11},{9,10},{10,... | collective-permute-start | bytes 786440 | tf_op jit(solution)/shard_map/ppermute | solution.py:769
  140.7 4.7 %copy-start.3 = (s32[1,2048]{1,0:T(1,128)S(1)}, s32[1,2048]{1,0:T(1,128)}, u32[]{:S(2)}) copy-start(s32[1,2048]{1,0:T(1,128)} %get-tuple-element.43.refs_2_) | copy-start | bytes 24580
  140.7 9.1 %collective-permute-start.19 = (bf16[64,2048]{1,0:T(8,128)(2,1)S(1)}, bf16[64,2048]{1,0:T(8,128)(2,1)S(1)}, u32[]{:S(2)}, u32[]{:S(2)}) collective-permute-start(bf16[64,2048]{1,0:T(8,128)(2,1)S(1)} %gather.6), channel_id=1, source_target_pairs={{0,2},{1,3},{2,0},{3,1},{4,6},{5,7},{6,4},{7,5},{8,10},{9,11},{10,... | collective-permute-start | bytes 786440 | tf_op jit(solution)/shard_map/ppermute | solution.py:769
  143.9 6.5 %copy-start.1 = (f32[64,2048]{1,0:T(8,128)S(1)}, f32[64,2048]{1,0:T(8,128)}, u32[]{:S(2)}) copy-start(f32[64,2048]{1,0:T(8,128)} %get-tuple-element.42.tab_ref) | copy-start | bytes 1572868
  143.9 6.4 %collective-permute-start.18 = (bf16[64,2048]{1,0:T(8,128)(2,1)S(1)}, bf16[64,2048]{1,0:T(8,128)(2,1)S(1)}, u32[]{:S(2)}, u32[]{:S(2)}) collective-permute-start(bf16[64,2048]{1,0:T(8,128)(2,1)S(1)} %gather.5), channel_id=1, source_target_pairs={{0,1},{1,0},{2,3},{3,2},{4,5},{5,4},{6,7},{7,6},{8,9},{9,8},{10,11... | collective-permute-start | bytes 786440 | tf_op jit(solution)/shard_map/ppermute | solution.py:769
  (1 other events, 0.7 us)
